TPU v7x, 512 devices: a whole 4x8x8 slice. The times are simulated.
512 devices in a mesh: lat: 16 (over z_lo, y), lon: 32 (over x, z_hi, core).
Axes of the slice: x: 4, y: 8, z: 8 (z_hi: 4, z_lo: 2; z = z_hi * 2 + z_lo), core: 2. Of those that a mesh axis runs over, the one named last changes fastest.
Arguments:
- fine_tokens: bfloat16 [288, 768, 512], P('lat', 'lon'), may hold values from -6 to 6
- cotangent: bfloat16 [288, 768, 512], P('lat', 'lon'), may hold values from -6 to 6
- norm_gain: float32 [512], replicated, may hold values from 0.1 to 1.9
- qkv_weight: bfloat16 [512, 1536], replicated
- qkv_down: bfloat16 [512, 8], replicated, may hold values from -0.25 to 0.25
- qkv_up: bfloat16 [8, 1536], replicated, may hold values from -2 to 2
- out_weight: bfloat16 [512, 512], replicated, may hold values from -0.25 to 0.25
- out_down: bfloat16 [512, 8], replicated, may hold values from -0.25 to 0.25
- out_up: bfloat16 [8, 512], replicated, may hold values from -2 to 2
Outputs:
- mixed: bfloat16 [288, 768, 512], P('lat', 'lon')
- grad_in: bfloat16 [288, 768, 512], P('lat', 'lon')
- grad_qkv_down: float32 [512, 8], replicated
- grad_qkv_up: float32 [8, 1536], replicated
- grad_out_down: float32 [512, 8], replicated
- grad_out_up: float32 [8, 512], replicated
All inputs are finite; a program needn't handle non-finite values.
Results may differ from a plain program's by a relative error of at most 0.017.
The roundings to bfloat16 on the way count: a program that leaves them out, or rounds other values in their place, can miss the bound.
Values may be sent and summed in bfloat16 or wider, within the bound.
No kernel may reach another device: no remote copies, remote signals or barrier semaphores. Data moves between devices by JAX's collectives and lax.ppermute only.
A program may use at most 64 MiB of HBM per device.

v0:
```python
import math

import jax
import jax.numpy as jnp
from jax import lax
from jax.sharding import PartitionSpec as P

HEADS = 16
WIN_LAT = 6
WIN_LON = 12


def shifted_2(block, axis, distance):
    devices = range(lax.axis_size(axis))
    route = [((i - distance) % len(devices), i) for i in devices]
    return lax.ppermute(block, axis, route)


def layer_norm(widened, norm_gain):
    center = widened - jnp.mean(widened, axis=-1, keepdims=True)
    spread = jnp.mean(center * center, axis=-1, keepdims=True)
    return center * lax.rsqrt(spread + 1e-05) * norm_gain


def inner_product(left, right):
    return lax.dot_general(
        left, right, (((0,), (0,)), ((), ())), preferred_element_type=jnp.float32
    )


def times_transpose(left, right):
    return lax.dot_general(
        left, right, (((1,), (1,)), ((), ())), preferred_element_type=jnp.float32
    )


def window_attention(packed, pole_side):
    lat_cells, lon_cells, triple = packed.shape
    features = triple // 3
    head_width = features // HEADS
    lat_windows = lat_cells // WIN_LAT
    lon_windows = lon_cells // WIN_LON
    window_cells = WIN_LAT * WIN_LON
    window_tiles = packed.reshape(lat_windows, WIN_LAT, lon_windows, WIN_LON, 3, HEADS, head_width)
    window_tiles = window_tiles.transpose(0, 2, 4, 5, 1, 3, 6).reshape(
        lat_windows, lon_windows, 3, HEADS, window_cells, head_width
    )
    queries = window_tiles[:, :, 0]
    key_rows = window_tiles[:, :, 1]
    value_rows = window_tiles[:, :, 2]
    scores = jnp.einsum(
        "abhqd,abhkd->abhqk", queries, key_rows, preferred_element_type=jnp.float32
    ) / math.sqrt(head_width)
    pole_rows = jnp.broadcast_to(
        pole_side.reshape(lat_windows, WIN_LAT, 1), (lat_windows, WIN_LAT, WIN_LON)
    ).reshape(lat_windows, 1, window_cells)
    allowed = pole_rows[:, :, :, None] == pole_rows[:, :, None, :]
    scores = jnp.where(allowed[:, :, None], scores, -1e30)
    row_top = jnp.max(scores, axis=-1, keepdims=True)
    exponent = jnp.exp(scores - row_top)
    weights = (exponent / jnp.sum(exponent, axis=-1, keepdims=True)).astype(jnp.bfloat16)
    blended = jnp.einsum(
        "abhqk,abhkd->abhqd", weights, value_rows, preferred_element_type=jnp.float32
    ).astype(jnp.bfloat16)
    blended = blended.reshape(
        lat_windows, lon_windows, HEADS, WIN_LAT, WIN_LON, head_width
    ).transpose(0, 3, 1, 4, 2, 5)
    return blended.reshape(lat_cells * lon_cells, features)


def forward(shifted, pole_side, norm_gain, weight_set):
    qkv_weight, qkv_down, qkv_up, out_weight, out_down, out_up = weight_set
    lat_cells, lon_cells, features = shifted.shape
    widened = shifted.astype(jnp.float32).reshape(lat_cells * lon_cells, features)
    normed, norm_back = jax.vjp(lambda argument: layer_norm(argument, norm_gain), widened)
    hidden_in = normed.astype(jnp.bfloat16)
    low_query = jnp.dot(hidden_in, qkv_down, preferred_element_type=jnp.float32).astype(
        jnp.bfloat16
    )
    packed = (
        jnp.dot(hidden_in, qkv_weight, preferred_element_type=jnp.float32)
        + jnp.dot(low_query, qkv_up, preferred_element_type=jnp.float32)
    ).astype(jnp.bfloat16)
    blended, attend_back = jax.vjp(
        lambda argument: window_attention(
            argument.reshape(lat_cells, lon_cells, 3 * features), pole_side
        ),
        packed,
    )
    low_out = jnp.dot(blended, out_down, preferred_element_type=jnp.float32).astype(jnp.bfloat16)
    update = (
        jnp.dot(blended, out_weight, preferred_element_type=jnp.float32)
        + jnp.dot(low_out, out_up, preferred_element_type=jnp.float32)
    ).astype(jnp.bfloat16)
    return (
        update.reshape(lat_cells, lon_cells, features),
        (hidden_in, low_query, blended, low_out, norm_back, attend_back),
    )


def backward(saved, shifted_cot, weight_set):
    qkv_weight, qkv_down, qkv_up, out_weight, out_down, out_up = weight_set
    hidden_in, low_query, blended, low_out, norm_back, attend_back = saved
    lat_cells, lon_cells, features = shifted_cot.shape
    upstream = shifted_cot.reshape(lat_cells * lon_cells, features)
    grad_up_out = inner_product(low_out, upstream)
    back_low_out = times_transpose(upstream, out_up).astype(jnp.bfloat16)
    grad_down_out = inner_product(blended, back_low_out)
    back_blended = (
        times_transpose(upstream, out_weight) + times_transpose(back_low_out, out_down)
    ).astype(jnp.bfloat16)
    back_packed = attend_back(back_blended)[0]
    grad_up_qkv = inner_product(low_query, back_packed)
    back_low_query = times_transpose(back_packed, qkv_up).astype(jnp.bfloat16)
    grad_down_qkv = inner_product(hidden_in, back_low_query)
    back_hidden = times_transpose(back_packed, qkv_weight) + times_transpose(
        back_low_query, qkv_down
    )
    back_tokens = norm_back(back_hidden)[0].astype(jnp.bfloat16)
    return (
        back_tokens.reshape(lat_cells, lon_cells, features),
        (grad_down_qkv, grad_up_qkv, grad_down_out, grad_up_out),
    )


def roll_rows(field, step_dir):
    half = WIN_LAT // 2
    piece = field[..., :half, :, :] if step_dir < 0 else field[..., -half:, :, :]
    kept = field[..., half:, :, :] if step_dir < 0 else field[..., :-half, :, :]
    moved = shifted_2(piece, "lat", step_dir)
    return jnp.concatenate((kept, moved) if step_dir < 0 else (moved, kept), axis=-3)


def roll_columns(field, step_dir):
    half = WIN_LON // 2
    piece = field[..., :half, :] if step_dir < 0 else field[..., -half:, :]
    kept = field[..., half:, :] if step_dir < 0 else field[..., :-half, :]
    moved = shifted_2(piece, "lon", step_dir)
    return jnp.concatenate((kept, moved) if step_dir < 0 else (moved, kept), axis=-2)


def into_windows(field):
    return roll_rows(roll_columns(field, -1), -1)


def out_of_windows(field):
    return roll_columns(roll_rows(field, 1), 1)


def add_round(first, second):
    return (first.astype(jnp.float32) + second.astype(jnp.float32)).astype(jnp.bfloat16)


def shards(
    fine_tokens, cotangent, norm_gain, qkv_weight, qkv_down, qkv_up, out_weight, out_down, out_up
):
    weight_set = (qkv_weight, qkv_down, qkv_up, out_weight, out_down, out_up)
    lat_cells, lon_cells, features = fine_tokens.shape
    total_rows = lat_cells * lax.axis_size("lat")
    first_row = lax.axis_index("lat") * lat_cells
    pole_side = (
        first_row + jnp.arange(lat_cells, dtype=jnp.int32) + WIN_LAT // 2 >= total_rows
    ).astype(jnp.int32)
    shifted = into_windows(fine_tokens)
    update, saved = forward(shifted, pole_side, norm_gain, weight_set)
    mixed = add_round(fine_tokens, out_of_windows(update))
    shifted_cot = into_windows(cotangent)
    back_tokens, grads = backward(saved, shifted_cot, weight_set)
    grad_in = add_round(cotangent, out_of_windows(back_tokens))
    summed = lax.psum((grads[0], grads[1], grads[2], grads[3]), ("lat", "lon"))
    scale = 1.0 / math.sqrt(total_rows * lon_cells * lax.axis_size("lon"))
    return (
        mixed,
        grad_in,
        summed[0] * scale,
        summed[1] * scale,
        summed[2] * scale,
        summed[3] * scale,
    )


def solution(mesh):
    in_specs = (P("lat", "lon", None), P("lat", "lon", None), P(), P(), P(), P(), P(), P(), P())
    out_specs = (P("lat", "lon", None), P("lat", "lon", None), P(), P(), P(), P())
    return jax.shard_map(shards, mesh=mesh, in_specs=in_specs, out_specs=out_specs, check_vma=False)
```

profile of v0, /device:TPU:1, one launch (start us, length us, event | category | flops | bytes accessed | tf_op | source)
XLA Modules:
  0.0 422.3 jit_solution(13186085284483071096)
XLA Ops:
  8.3 8.8 %collective-permute-start.4 = (bf16[18,6,512]{2,1,0:T(8,128)(2,1)S(1)}, bf16[18,6,512]{2,1,0:T(8,128)(2,1)S(1)}, u32[]{:S(2)}, u32[]{:S(2)}) collective-permute-start(bf16[18,6,512]{2,1,0:T(8,128)(2,1)S(1)} %slice.83), channel_id=1, source_target_pairs={{1,0},{2,1},{3,2},{4,3},{5,4},{6,5},{7,6},{8,7},{9,8},{10,9},{11,1... | collective-permute-start | bytes 331784 | tf_op jit(solution)/shard_map/ppermute | solution.py:16
  18.0 7.2 %collective-permute-start = (bf16[18,6,512]{2,1,0:T(8,128)(2,1)S(1)}, bf16[18,6,512]{2,1,0:T(8,128)(2,1)S(1)}, u32[]{:S(2)}, u32[]{:S(2)}) collective-permute-start(bf16[18,6,512]{2,1,0:T(8,128)(2,1)S(1)} %slice.70), channel_id=1, source_target_pairs={{1,0},{2,1},{3,2},{4,3},{5,4},{6,5},{7,6},{8,7},{9,8},{10,9},{11,1... | collective-permute-start | bytes 331784 | tf_op jit(solution)/shard_map/ppermute | solution.py:16
  25.5 1.1 slice.69
  26.6 1.2 slice.82
  27.9 6.0 %collective-permute-start.1 = (bf16[3,24,512]{2,1,0:T(8,128)(2,1)S(1)}, bf16[3,24,512]{2,1,0:T(8,128)(2,1)S(1)}, u32[]{:S(2)}, u32[]{:S(2)}) collective-permute-start(bf16[3,24,512]{2,1,0:T(8,128)(2,1)S(1)} %pad_maximum_fusion.6), channel_id=1, source_target_pairs={{32,0},{64,32},{96,64},{128,96},{160,128},{192,160},{224,192},{256... | collective-permute-start | bytes 221192 | tf_op jit(solution)/shard_map/ppermute | solution.py:16
  33.9 3.0 collective-permute-start.5
  40.3 2.0 reshape.136
  42.3 1.9 copy.28
  44.1 2.2 copy.30
  46.3 1.0 maximum_convert_fusion
  48.7 1.7 fusion.4
  50.4 6.8 %reshape.131 = bf16[3,6,2,12,3,16,32]{6,5,4,3,2,1,0:T(8,128)(2,1)} reshape(bf16[432,1536]{1,0:T(8,128)(2,1)} %fusion.4) | data formatting | bytes 2654208 | tf_op jit(solution)/shard_map/jvp()/reshape;jvp()/reshape | solution.py:44
  57.2 4.0 copy.21
  61.2 2.9 fusion.47
  64.0 3.2 copy.42
  67.3 3.2 copy.41
  70.5 3.2 copy.40
  73.7 2.6 fusion.6
  76.3 1.1 fusion.25
  77.5 2.6 convert_reduce_fusion
  80.1 2.1 fusion.44
  82.3 1.8 fusion.20
  84.2 1.9 fusion.21
  86.1 2.0 fusion.22
  88.1 1.5 convolution_convert_fusion.2
  89.5 3.2 copy.26
  92.7 3.1 copy.27
  95.8 3.0 reshape.134
  99.8 2.4 fusion.49
  102.2 3.7 pad_add_fusion
  105.9 7.1 %copy.34 = bf16[3,2,3,16,72,32]{5,3,4,2,1,0:T(8,128)(2,1)} copy(bf16[3,2,3,16,72,32]{4,5,3,1,0,2:T(8,128)(2,1)} %pad_add_fusion) | data formatting | bytes 2654208 | tf_op jit(solution)/shard_map/transpose(jvp())/add_any | solution.py:48
  112.9 5.9 %copy.35 = bf16[3,6,2,12,3,16,32]{6,5,4,3,2,1,0:T(8,128)(2,1)} copy(bf16[3,6,2,12,3,16,32]{6,5,3,1,4,2,0:T(8,128)(2,1)} %bitcast.88) | data formatting | bytes 2654208 | tf_op jit(solution)/shard_map/transpose(jvp())/transpose | solution.py:45
  118.9 7.7 %reshape.139 = bf16[432,1536]{1,0:T(8,128)(2,1)} reshape(bf16[3,6,2,12,3,16,32]{6,5,4,3,2,1,0:T(8,128)(2,1)} %copy.35) | data formatting | bytes 2654208 | tf_op jit(solution)/shard_map/transpose(jvp())/reshape;transpose(jvp())/reshape | solution.py:86
  126.6 1.8 convolution_convert_fusion.3
  128.4 2.3 fusion.53
  130.6 3.2 fusion.51
  135.3 1.7 multiply_reduce_fusion
  140.7 1.9 collective-permute-start.2
  142.6 1.9 collective-permute-start.6
  144.6 255.0 %all-reduce.6.cloned.1.call-done = (f32[512,8]{0,1:T(8,128)}, f32[8,1536]{1,0:T(8,128)}, f32[512,8]{0,1:T(8,128)}, f32[8,512]{1,0:T(8,128)}) async-done(((f32[512,8]{0,1:T(8,128)}, f32[8,1536]{1,0:T(8,128)}, f32[512,8]{0,1:T(8,128)}, f32[8,512]{1,0:T(8,128)}), (f32[512,8]{0,1:T(8,128)}, f32[8,1536]{1,0:T(8,128)}, f32[512,8]{0,1:T(8,128)}, f32[8,512]{1,0:T(8,128)})) %all-reduce.6.cloned.1.call-update) | async-done | bytes 98320 | tf_op jit(solution)/shard_map/psum | solution.py:170
  399.6 1.4 broadcast_multiply_fusion
  401.0 1.3 broadcast_multiply_fusion.2
  402.4 1.3 broadcast_multiply_fusion.1
  403.7 3.5 collective-permute-start.3
  407.3 2.4 collective-permute-start.7
  409.7 2.0 add_convert_fusion.2
  411.7 1.9 collective-permute-done.7
  413.5 2.0 add_convert_fusion
  (81 shorter events, 13.2 us)
Async XLA Ops:
  7.2 40.7 %copy-start = (bf16[512,1536]{1,0:T(8,128)(2,1)S(1)}, bf16[512,1536]{1,0:T(8,128)(2,1)}, u32[]{:S(2)}) copy-start(bf16[512,1536]{1,0:T(8,128)(2,1)} %param.12) | copy-start | bytes 4718596
  7.2 392.4 %all-reduce.6.cloned.1.call-start = ((), (), s32[]{:S(2)}) async-start(), calls=%async_computation | async-start | bytes 196608 | tf_op jit(solution)/shard_map/psum | solution.py:170
  8.3 25.6 %collective-permute-start.4 = (bf16[18,6,512]{2,1,0:T(8,128)(2,1)S(1)}, bf16[18,6,512]{2,1,0:T(8,128)(2,1)S(1)}, u32[]{:S(2)}, u32[]{:S(2)}) collective-permute-start(bf16[18,6,512]{2,1,0:T(8,128)(2,1)S(1)} %slice.83), channel_id=1, source_target_pairs={{1,0},{2,1},{3,2},{4,3},{5,4},{6,5},{7,6},{8,7},{9,8},{10,9},{11,1... | collective-permute-start | bytes 331784 | tf_op jit(solution)/shard_map/ppermute | solution.py:16
  18.0 21.1 %copy-start.13 = (bf16[8,512]{1,0:T(8,128)(2,1)S(1)}, bf16[8,512]{1,0:T(8,128)(2,1)}, u32[]{:S(2)}) copy-start(bf16[8,512]{1,0:T(8,128)(2,1)} %param.17) | copy-start | bytes 24580
  18.0 9.9 %collective-permute-start = (bf16[18,6,512]{2,1,0:T(8,128)(2,1)S(1)}, bf16[18,6,512]{2,1,0:T(8,128)(2,1)S(1)}, u32[]{:S(2)}, u32[]{:S(2)}) collective-permute-start(bf16[18,6,512]{2,1,0:T(8,128)(2,1)S(1)} %slice.70), channel_id=1, source_target_pairs={{1,0},{2,1},{3,2},{4,3},{5,4},{6,5},{7,6},{8,7},{9,8},{10,9},{11,1... | collective-permute-start | bytes 331784 | tf_op jit(solution)/shard_map/ppermute | solution.py:16
  25.5 13.8 %copy-start.11 = (bf16[512,8]{0,1:T(8,128)(2,1)S(1)}, bf16[512,8]{0,1:T(8,128)(2,1)}, u32[]{:S(2)}) copy-start(bf16[512,8]{0,1:T(8,128)(2,1)} %param.16) | copy-start | bytes 24580
  26.6 13.2 %copy-start.9 = (bf16[512,512]{1,0:T(8,128)(2,1)S(1)}, bf16[512,512]{1,0:T(8,128)(2,1)}, u32[]{:S(2)}) copy-start(bf16[512,512]{1,0:T(8,128)(2,1)} %param.15) | copy-start | bytes 1572868
  27.9 9.2 %collective-permute-start.1 = (bf16[3,24,512]{2,1,0:T(8,128)(2,1)S(1)}, bf16[3,24,512]{2,1,0:T(8,128)(2,1)S(1)}, u32[]{:S(2)}, u32[]{:S(2)}) collective-permute-start(bf16[3,24,512]{2,1,0:T(8,128)(2,1)S(1)} %pad_maximum_fusion.6), channel_id=1, source_target_pairs={{32,0},{64,32},{96,64},{128,96},{160,128},{192,160},{224,192},{256... | collective-permute-start | bytes 221192 | tf_op jit(solution)/shard_map/ppermute | solution.py:16
  33.9 5.1 %collective-permute-start.5 = (bf16[3,24,512]{2,1,0:T(8,128)(2,1)S(1)}, bf16[3,24,512]{2,1,0:T(8,128)(2,1)S(1)}, u32[]{:S(2)}, u32[]{:S(2)}) collective-permute-start(bf16[3,24,512]{2,1,0:T(8,128)(2,1)S(1)} %pad_maximum_fusion.5), channel_id=1, source_target_pairs={{32,0},{64,32},{96,64},{128,96},{160,128},{192,160},{224,192},{256... | collective-permute-start | bytes 221192 | tf_op jit(solution)/shard_map/ppermute | solution.py:16
  37.0 0.7 copy-start.3
  39.1 0.8 copy-start.1
  42.3 5.1 %copy-start.14 = (f32[512]{0:T(512)S(1)}, f32[512]{0:T(512)}, u32[]{:S(2)}) copy-start(f32[512]{0:T(512)} %param.11) | copy-start | bytes 6148
  44.1 3.5 copy-start.12
  47.4 1.3 copy-start.10
  73.7 3.8 copy-start.5
  73.7 3.8 copy-start.6
  80.1 2.2 copy-start.7
  82.3 1.8 copy-start.8
  130.6 3.2 copy-start.2
  135.3 3.1 copy-start.4
  140.7 263.0 %collective-permute-start.2 = (bf16[3,24,512]{2,1,0:T(8,128)(2,1)S(1)}, bf16[3,24,512]{2,1,0:T(8,128)(2,1)S(1)}, u32[]{:S(2)}, u32[]{:S(2)}) collective-permute-start(bf16[3,24,512]{2,1,0:T(8,128)(2,1)S(1)} %bitcast.99), channel_id=1, source_target_pairs={{480,0},{0,32},{32,64},{64,96},{96,128},{128,160},{160,192},{192,2... | collective-permute-start | bytes 221192 | tf_op jit(solution)/shard_map/ppermute | solution.py:16
  142.6 264.6 %collective-permute-start.6 = (bf16[3,24,512]{2,1,0:T(8,128)(2,1)S(1)}, bf16[3,24,512]{2,1,0:T(8,128)(2,1)S(1)}, u32[]{:S(2)}, u32[]{:S(2)}) collective-permute-start(bf16[3,24,512]{2,1,0:T(8,128)(2,1)S(1)} %bitcast.98), channel_id=1, source_target_pairs={{480,0},{0,32},{32,64},{64,96},{96,128},{128,160},{160,192},{192,2... | collective-permute-start | bytes 221192 | tf_op jit(solution)/shard_map/ppermute | solution.py:16
  403.7 5.9 %collective-permute-start.3 = (bf16[18,6,512]{2,1,0:T(8,128)(2,1)S(1)}, bf16[18,6,512]{2,1,0:T(8,128)(2,1)S(1)}, u32[]{:S(2)}, u32[]{:S(2)}) collective-permute-start(bf16[18,6,512]{2,1,0:T(8,128)(2,1)S(1)} %pad_maximum_fusion.4), channel_id=1, source_target_pairs={{31,0},{0,1},{1,2},{2,3},{3,4},{4,5},{5,6},{6,7},{7,8},{8,9},{9,10... | collective-permute-start | bytes 331784 | tf_op jit(solution)/shard_map/ppermute | solution.py:16
  407.3 6.3 %collective-permute-start.7 = (bf16[18,6,512]{2,1,0:T(8,128)(2,1)S(1)}, bf16[18,6,512]{2,1,0:T(8,128)(2,1)S(1)}, u32[]{:S(2)}, u32[]{:S(2)}) collective-permute-start(bf16[18,6,512]{2,1,0:T(8,128)(2,1)S(1)} %pad_maximum_fusion.3), channel_id=1, source_target_pairs={{31,0},{0,1},{1,2},{2,3},{3,4},{4,5},{5,6},{6,7},{7,8},{8,9},{9,10... | collective-permute-start | bytes 331784 | tf_op jit(solution)/shard_map/ppermute | solution.py:16
Sparse Core Ops, SparseCore 0:
  138.5 261.0 all-reduce.5
where the time goes:
time: 427 us; the launch traced here: 422 us
  waiting for transfers between devices  258 us (60%)
  local copies, waits for them, and re-layouts  66.6 us (16%)
  starting transfers between devices  34.7 us (8%)
  matrix products  30.3 us (7%)
  other arithmetic  18.4 us (4%)
  between operations  14.5 us (3%)
    psum x1, waiting for transfers between devices, shards(): summed = lax.psum((grads[0], grads[1], grads[2], grads[3]), ('lat', 'lon'))  255 us
    ppermute x8, starting transfers between devices, shifted_2(): return lax.ppermute(block, axis, route)  34.7 us
    reshape x2, local copies, waits for them, and re-layouts, window_attention(): packed.reshape(lat_windows, WIN_LAT, lon_windows, WIN_LON, 3, HEADS, head...  10.8 us
    unnamed x33, local copies, waits for them, and re-layouts  10.4 us
  transfers between devices with their start and end apart: 9, of which 3 were waited for; matrix products, arithmetic and copies ran while one was open for 3% of the time, Pallas kernels for 0%

commit v1 on v0

--- a/solution.py
+++ b/solution.py
@@ -151,6 +151,26 @@
     return (first.astype(jnp.float32) + second.astype(jnp.float32)).astype(jnp.bfloat16)
 
 
+def exchange(tiles, axis):
+    return lax.all_to_all(tiles, axis, 0, 0, tiled=True)
+
+
+def gather_tiles(tile, axis):
+    spread = jnp.broadcast_to(tile[None], (lax.axis_size(axis),) + tile.shape)
+    return exchange(spread, axis)
+
+
+def total_over_mesh(packed):
+    rows, width = packed.shape
+    owners = lax.axis_size("lon")
+    tiles = jnp.pad(packed, ((0, 0), (0, owners * 128 - width)))
+    tiles = tiles.reshape(rows, owners, 128).transpose(1, 0, 2)
+    own = jnp.sum(exchange(tiles, "lon"), axis=0)
+    own = jnp.sum(gather_tiles(own, "lat"), axis=0)
+    tiles = gather_tiles(own, "lon")
+    return tiles.transpose(1, 0, 2).reshape(rows, owners * 128)[:, :width]
+
+
 def shards(
     fine_tokens, cotangent, norm_gain, qkv_weight, qkv_down, qkv_up, out_weight, out_down, out_up
 ):
@@ -167,15 +187,17 @@
     shifted_cot = into_windows(cotangent)
     back_tokens, grads = backward(saved, shifted_cot, weight_set)
     grad_in = add_round(cotangent, out_of_windows(back_tokens))
-    summed = lax.psum((grads[0], grads[1], grads[2], grads[3]), ("lat", "lon"))
     scale = 1.0 / math.sqrt(total_rows * lon_cells * lax.axis_size("lon"))
+    out_packed = lax.psum(jnp.concatenate((grads[2].T, grads[3]), axis=1), ("lat", "lon"))
+    qkv_packed = total_over_mesh(jnp.concatenate((grads[0].T, grads[1]), axis=1)) * scale
+    out_packed = out_packed * scale
     return (
         mixed,
         grad_in,
-        summed[0] * scale,
-        summed[1] * scale,
-        summed[2] * scale,
-        summed[3] * scale,
+        qkv_packed[:, :features].T,
+        qkv_packed[:, features:],
+        out_packed[:, :features].T,
+        out_packed[:, features:],
     )
 
 

time: 427 us -> 285 us (0.67)
  waiting for transfers between devices: 258 us -> 13.6 us
  blocking collectives: 0 us -> 99.9 us
  starting transfers between devices: 34.7 us -> 51.3 us
  between operations: 14.5 us -> 1.21 us
  local copies, waits for them, and re-layouts: 66.6 us -> 72 us
    psum x1 -> x0, waiting for transfers between devices: 255 us -> none  [shards(): summed = lax.psum((grads[0], grads[1], grads[2], grads[3]), ('lat', 'lon'))]
    psum x0 -> x1, blocking collectives: none -> 99.9 us  [shards(): lax.psum(jnp.concatenate((grads[2].T, grads[3]), axis=1), ('lat', 'lon'))]
    all_to_all x0 -> x3, starting transfers between devices: none -> 17.3 us  [exchange(): return lax.all_to_all(tiles, axis, 0, 0, tiled=True)]
    all_to_all x0 -> x3, waiting for transfers between devices: none -> 12.8 us  [exchange(): return lax.all_to_all(tiles, axis, 0, 0, tiled=True)]
    unnamed x33 -> x37, local copies, waits for them, and re-layouts: 10.4 us -> 10.4 us
  transfers between devices with their start and end apart: 9 -> 11, of which waited for: 3 -> 4; matrix products, arithmetic and copies ran while one was open for 3% -> 7% of each run, Pallas kernels for 0% -> 0%
where the time goes in v1:
time: 285 us; the launch traced here: 283 us
  blocking collectives  99.9 us (35%)
  local copies, waits for them, and re-layouts  72 us (25%)
  starting transfers between devices  51.3 us (18%)
  matrix products  29 us (10%)
  other arithmetic  16.1 us (6%)
  waiting for transfers between devices  13.6 us (5%)
    psum x1, blocking collectives, shards(): lax.psum(jnp.concatenate((grads[2].T, grads[3]), axis=1), ('lat', 'lon'))  99.9 us
    ppermute x8, starting transfers between devices, shifted_2(): return lax.ppermute(block, axis, route)  34 us
    all_to_all x3, starting transfers between devices, exchange(): return lax.all_to_all(tiles, axis, 0, 0, tiled=True)  17.3 us
    all_to_all x3, waiting for transfers between devices, exchange(): return lax.all_to_all(tiles, axis, 0, 0, tiled=True)  12.8 us
    reshape x2, local copies, waits for them, and re-layouts, window_attention(): packed.reshape(lat_windows, WIN_LAT, lon_windows, WIN_LON, 3, HEADS, head...  10.8 us
    unnamed x37, local copies, waits for them, and re-layouts  10.4 us
    reshape x1, local copies, waits for them, and re-layouts, forward(): argument.reshape(lat_cells, lon_cells, 3 * features)  7.73 us
    dot_general x6, matrix products, times_transpose(): lax.dot_general(left, right, (((1,), (1,)), ((), ())), preferred_element_...  7.58 us
  transfers between devices with their start and end apart: 11, of which 4 were waited for; matrix products, arithmetic and copies ran while one was open for 7% of the time, Pallas kernels for 0%

profile of v1, /device:TPU:1, one launch (start us, length us, event | category | flops | bytes accessed | tf_op | source)
XLA Modules:
  0.0 283.1 jit_solution(7370901318952690524)
XLA Ops:
  1.7 8.8 %collective-permute-start.4 = (bf16[18,6,512]{2,1,0:T(8,128)(2,1)S(1)}, bf16[18,6,512]{2,1,0:T(8,128)(2,1)S(1)}, u32[]{:S(2)}, u32[]{:S(2)}) collective-permute-start(bf16[18,6,512]{2,1,0:T(8,128)(2,1)S(1)} %slice.98), channel_id=1, source_target_pairs={{1,0},{2,1},{3,2},{4,3},{5,4},{6,5},{7,6},{8,7},{9,8},{10,9},{11,1... | collective-permute-start | bytes 331784 | tf_op jit(solution)/shard_map/ppermute | solution.py:16
  11.4 7.2 %collective-permute-start = (bf16[18,6,512]{2,1,0:T(8,128)(2,1)S(1)}, bf16[18,6,512]{2,1,0:T(8,128)(2,1)S(1)}, u32[]{:S(2)}, u32[]{:S(2)}) collective-permute-start(bf16[18,6,512]{2,1,0:T(8,128)(2,1)S(1)} %slice.85), channel_id=1, source_target_pairs={{1,0},{2,1},{3,2},{4,3},{5,4},{6,5},{7,6},{8,7},{9,8},{10,9},{11,1... | collective-permute-start | bytes 331784 | tf_op jit(solution)/shard_map/ppermute | solution.py:16
  21.3 6.0 %collective-permute-start.1 = (bf16[3,24,512]{2,1,0:T(8,128)(2,1)S(1)}, bf16[3,24,512]{2,1,0:T(8,128)(2,1)S(1)}, u32[]{:S(2)}, u32[]{:S(2)}) collective-permute-start(bf16[3,24,512]{2,1,0:T(8,128)(2,1)S(1)} %pad_maximum_fusion.6), channel_id=1, source_target_pairs={{32,0},{64,32},{96,64},{128,96},{160,128},{192,160},{224,192},{256... | collective-permute-start | bytes 221192 | tf_op jit(solution)/shard_map/ppermute | solution.py:16
  27.4 3.0 %collective-permute-start.5 = (bf16[3,24,512]{2,1,0:T(8,128)(2,1)S(1)}, bf16[3,24,512]{2,1,0:T(8,128)(2,1)S(1)}, u32[]{:S(2)}, u32[]{:S(2)}) collective-permute-start(bf16[3,24,512]{2,1,0:T(8,128)(2,1)S(1)} %pad_maximum_fusion.5), channel_id=1, source_target_pairs={{32,0},{64,32},{96,64},{128,96},{160,128},{192,160},{224,192},{256... | collective-permute-start | bytes 221192 | tf_op jit(solution)/shard_map/ppermute | solution.py:16
  33.7 2.0 reshape.144
  35.7 1.9 copy.43
  37.6 2.2 copy.45
  42.2 1.7 fusion.4
  43.8 6.8 %reshape.139 = bf16[3,6,2,12,3,16,32]{6,5,4,3,2,1,0:T(8,128)(2,1)} reshape(bf16[432,1536]{1,0:T(8,128)(2,1)} %fusion.4) | data formatting | bytes 2654208 | tf_op jit(solution)/shard_map/jvp()/reshape;jvp()/reshape | solution.py:44
  50.6 4.0 %copy.36 = bf16[3,6,2,12,3,16,32]{6,5,3,1,4,2,0:T(8,128)(2,1)S(1)} copy(bf16[3,6,2,12,3,16,32]{6,5,4,3,2,1,0:T(8,128)(2,1)} %reshape.139) | data formatting | bytes 2654208 | tf_op jit(solution)/shard_map/jvp()/reshape;jvp()/reshape | solution.py:44
  54.6 2.8 %fusion.48 = (bf16[3,2,1,16,72,32]{5,3,4,2,1,0:T(8,128)(2,1)}, bf16[3,2,1,16,72,32]{5,3,4,2,1,0:T(8,128)(2,1)}, bf16[3,2,1,16,72,32]{5,3,4,2,1,0:T(8,128)(2,1)}) fusion(bf16[3,2,3,16,72,32]{5,3,4,2,1,0:T(8,128)(2,1)S(1)} %bitcast.98), kind=kLoop, calls=%fused_computation.100 | loop fusion | bytes 2654208 | tf_op jit(solution)/shard_map/jvp()/slice | solution.py:50
  57.5 3.2 %copy.57 = bf16[3,2,1,16,72,32]{4,5,3,1,0,2:T(8,128)(2,1)} copy(bf16[3,2,1,16,72,32]{5,3,4,2,1,0:T(8,128)(2,1)} %get-tuple-element.12) | data formatting | bytes 884736
  60.7 3.2 %copy.56 = bf16[3,2,1,16,72,32]{4,5,3,1,0,2:T(8,128)(2,1)} copy(bf16[3,2,1,16,72,32]{5,3,4,2,1,0:T(8,128)(2,1)} %get-tuple-element.13) | data formatting | bytes 884736
  63.9 3.2 %copy.55 = bf16[3,2,1,16,72,32]{4,5,3,1,0,2:T(8,128)(2,1)} copy(bf16[3,2,1,16,72,32]{5,3,4,2,1,0:T(8,128)(2,1)} %get-tuple-element.14) | data formatting | bytes 884736
  67.1 2.6 fusion.6
  70.8 2.6 convert_reduce_fusion
  73.5 2.1 fusion.45
  75.7 1.8 fusion.20
  77.5 1.9 fusion.21
  79.4 2.0 fusion.22
  81.4 1.5 convolution_convert_fusion.2
  82.9 3.2 %copy.41 = bf16[3,2,16,72,32]{4,2,3,1,0:T(8,128)(2,1)} copy(bf16[3,2,16,72,32]{3,4,2,1,0:T(8,128)(2,1)} %convolution_convert_fusion.2) | data formatting | bytes 884736 | tf_op jit(solution)/shard_map/jvp()/convert_element_type | solution.py:64
  86.1 3.1 %copy.42 = bf16[3,6,2,12,16,32]{5,4,3,2,1,0:T(8,128)(2,1)} copy(bf16[3,6,2,12,16,32]{5,4,3,1,2,0:T(8,128)(2,1)} %bitcast.101) | data formatting | bytes 884736 | tf_op jit(solution)/shard_map/jvp()/transpose | solution.py:67
  89.1 3.0 %reshape.142 = bf16[432,512]{1,0:T(8,128)(2,1)S(1)} reshape(bf16[3,6,2,12,16,32]{5,4,3,2,1,0:T(8,128)(2,1)} %copy.42) | data formatting | bytes 884736 | tf_op jit(solution)/shard_map/jvp()/reshape | solution.py:68
  92.5 2.4 fusion.51
  94.9 3.7 %pad_add_fusion = bf16[3,2,3,16,72,32]{4,5,3,1,0,2:T(8,128)(2,1)} fusion(bf16[3,2,1,16,72,32]{4,5,3,1,0,2:T(8,128)(2,1)} %fusion.20, bf16[3,2,1,16,72,32]{4,5,3,1,0,2:T(8,128)(2,1)} %fusion.21, bf16[3,2,1,16,72,32]{4,5,3,1,0,2:T(8,128)(2,1)} %fusion.22), kind=kLoop, calls=%fused_computation.15 | loop fusion | flops 1327104 | bytes 2654208 | tf_op jit(solution)/shard_map/transpose(jvp())/add_any | solution.py:48
  98.6 7.1 %copy.49 = bf16[3,2,3,16,72,32]{5,3,4,2,1,0:T(8,128)(2,1)} copy(bf16[3,2,3,16,72,32]{4,5,3,1,0,2:T(8,128)(2,1)} %pad_add_fusion) | data formatting | bytes 2654208 | tf_op jit(solution)/shard_map/transpose(jvp())/add_any | solution.py:48
  105.7 5.9 %copy.50 = bf16[3,6,2,12,3,16,32]{6,5,4,3,2,1,0:T(8,128)(2,1)} copy(bf16[3,6,2,12,3,16,32]{6,5,3,1,4,2,0:T(8,128)(2,1)} %bitcast.99) | data formatting | bytes 2654208 | tf_op jit(solution)/shard_map/transpose(jvp())/transpose | solution.py:45
  111.6 7.7 %reshape.147 = bf16[432,1536]{1,0:T(8,128)(2,1)} reshape(bf16[3,6,2,12,3,16,32]{6,5,4,3,2,1,0:T(8,128)(2,1)} %copy.50) | data formatting | bytes 2654208 | tf_op jit(solution)/shard_map/transpose(jvp())/reshape;transpose(jvp())/reshape | solution.py:86
  119.3 1.8 convolution_convert_fusion.3
  121.1 1.6 fusion.55
  122.7 3.2 %fusion.53 = f32[432,512]{1,0:T(8,128)} fusion(bf16[432,1536]{1,0:T(8,128)(2,1)} %reshape.147, bf16[512,1536]{1,0:T(8,128)(2,1)S(1)} %copy-done), kind=kOutput, calls=%fused_computation.105 | convolution fusion | flops 679477248 | bytes 3784704 | tf_op jit(solution)/shard_map/dot_general | solution.py:32
  126.1 99.9 %psum.7 = f32[8,1024]{1,0:T(8,128)S(1)} all-reduce(f32[8,1024]{1,0:T(8,128)S(1)} %pad_maximum_fusion.7), channel_id=1, replica_groups=mesh['lat'=16,'lon'=32] {'lat','lon'}, use_global_device_ids=true, to_apply=%region_11.12 | all-reduce | flops 8192 | bytes 65536 | tf_op jit(solution)/shard_map/psum | solution.py:191
  226.0 1.5 fusion.23
  228.2 2.4 collective-permute-start.2
  230.8 1.6 multiply_reduce_fusion
  234.4 5.4 %all-to-all-start = ((f32[32,8,128]{2,1,0:T(8,128)}), f32[32,8,128]{2,1,0:T(8,128)S(1)}, u32[]{:S(2)}, u32[]{:S(2)}) async-start(f32[32,8,128]{2,1,0:T(8,128)} %fusion.37), calls=%async_computation | async-start | bytes 262144 | tf_op jit(solution)/shard_map/all_to_all | solution.py:155
  241.4 1.5 slice.121
  244.0 1.9 collective-permute-start.6
  245.9 4.5 %all-to-all-done = f32[32,8,128]{2,1,0:T(8,128)S(1)} async-done(((f32[32,8,128]{2,1,0:T(8,128)}), f32[32,8,128]{2,1,0:T(8,128)S(1)}, u32[]{:S(2)}, u32[]{:S(2)}) %all-to-all-start) | async-done | bytes 131104 | tf_op jit(solution)/shard_map/all_to_all | solution.py:155
  251.1 4.4 %all-to-all-start.1 = ((f32[16,8,128]{2,1,0:T(8,128)}), f32[16,8,128]{2,1,0:T(8,128)S(1)}, u32[]{:S(2)}, u32[]{:S(2)}) async-start(f32[16,8,128]{2,1,0:T(8,128)} %broadcast_in_dim.72), calls=%async_computation.1 | async-start | bytes 131072 | tf_op jit(solution)/shard_map/all_to_all | solution.py:155
  256.2 2.8 collective-permute-start.3
  259.7 1.9 collective-permute-start.7
  261.7 1.2 all-to-all-done.1
  263.6 7.6 %all-to-all-start.2 = ((f32[32,8,128]{2,1,0:T(8,128)}), f32[32,8,128]{2,1,0:T(8,128)S(1)}, u32[]{:S(2)}, u32[]{:S(2)}) async-start(f32[32,8,128]{2,1,0:T(8,128)} %broadcast_in_dim.73), calls=%async_computation.2 | async-start | bytes 262144 | tf_op jit(solution)/shard_map/all_to_all | solution.py:155
  271.2 1.9 add_convert_fusion.2
  273.1 1.9 add_convert_fusion
  274.9 7.0 %all-to-all-done.2 = f32[32,8,128]{2,1,0:T(8,128)S(1)} async-done(((f32[32,8,128]{2,1,0:T(8,128)}), f32[32,8,128]{2,1,0:T(8,128)S(1)}, u32[]{:S(2)}, u32[]{:S(2)}) %all-to-all-start.2) | async-done | bytes 131104 | tf_op jit(solution)/shard_map/all_to_all | solution.py:155
  (97 shorter events, 21.4 us)
Async XLA Ops:
  0.6 40.6 %copy-start = (bf16[512,1536]{1,0:T(8,128)(2,1)S(1)}, bf16[512,1536]{1,0:T(8,128)(2,1)}, u32[]{:S(2)}) copy-start(bf16[512,1536]{1,0:T(8,128)(2,1)} %param.12) | copy-start | bytes 4718596
  1.7 25.6 %collective-permute-start.4 = (bf16[18,6,512]{2,1,0:T(8,128)(2,1)S(1)}, bf16[18,6,512]{2,1,0:T(8,128)(2,1)S(1)}, u32[]{:S(2)}, u32[]{:S(2)}) collective-permute-start(bf16[18,6,512]{2,1,0:T(8,128)(2,1)S(1)} %slice.98), channel_id=1, source_target_pairs={{1,0},{2,1},{3,2},{4,3},{5,4},{6,5},{7,6},{8,7},{9,8},{10,9},{11,1... | collective-permute-start | bytes 331784 | tf_op jit(solution)/shard_map/ppermute | solution.py:16
  11.4 21.1 %copy-start.14 = (bf16[8,512]{1,0:T(8,128)(2,1)S(1)}, bf16[8,512]{1,0:T(8,128)(2,1)}, u32[]{:S(2)}) copy-start(bf16[8,512]{1,0:T(8,128)(2,1)} %param.17) | copy-start | bytes 24580
  11.4 9.9 %collective-permute-start = (bf16[18,6,512]{2,1,0:T(8,128)(2,1)S(1)}, bf16[18,6,512]{2,1,0:T(8,128)(2,1)S(1)}, u32[]{:S(2)}, u32[]{:S(2)}) collective-permute-start(bf16[18,6,512]{2,1,0:T(8,128)(2,1)S(1)} %slice.85), channel_id=1, source_target_pairs={{1,0},{2,1},{3,2},{4,3},{5,4},{6,5},{7,6},{8,7},{9,8},{10,9},{11,1... | collective-permute-start | bytes 331784 | tf_op jit(solution)/shard_map/ppermute | solution.py:16
  18.9 13.8 %copy-start.13 = (bf16[512,8]{0,1:T(8,128)(2,1)S(1)}, bf16[512,8]{0,1:T(8,128)(2,1)}, u32[]{:S(2)}) copy-start(bf16[512,8]{0,1:T(8,128)(2,1)} %param.16) | copy-start | bytes 24580
  20.1 13.2 %copy-start.10 = (bf16[512,512]{1,0:T(8,128)(2,1)S(1)}, bf16[512,512]{1,0:T(8,128)(2,1)}, u32[]{:S(2)}) copy-start(bf16[512,512]{1,0:T(8,128)(2,1)} %param.15) | copy-start | bytes 1572868
  21.3 9.2 %collective-permute-start.1 = (bf16[3,24,512]{2,1,0:T(8,128)(2,1)S(1)}, bf16[3,24,512]{2,1,0:T(8,128)(2,1)S(1)}, u32[]{:S(2)}, u32[]{:S(2)}) collective-permute-start(bf16[3,24,512]{2,1,0:T(8,128)(2,1)S(1)} %pad_maximum_fusion.6), channel_id=1, source_target_pairs={{32,0},{64,32},{96,64},{128,96},{160,128},{192,160},{224,192},{256... | collective-permute-start | bytes 221192 | tf_op jit(solution)/shard_map/ppermute | solution.py:16
  27.4 5.1 %collective-permute-start.5 = (bf16[3,24,512]{2,1,0:T(8,128)(2,1)S(1)}, bf16[3,24,512]{2,1,0:T(8,128)(2,1)S(1)}, u32[]{:S(2)}, u32[]{:S(2)}) collective-permute-start(bf16[3,24,512]{2,1,0:T(8,128)(2,1)S(1)} %pad_maximum_fusion.5), channel_id=1, source_target_pairs={{32,0},{64,32},{96,64},{128,96},{160,128},{192,160},{224,192},{256... | collective-permute-start | bytes 221192 | tf_op jit(solution)/shard_map/ppermute | solution.py:16
  30.4 0.7 copy-start.3
  32.5 0.8 copy-start.1
  35.7 5.1 %copy-start.16 = (f32[512]{0:T(512)S(1)}, f32[512]{0:T(512)}, u32[]{:S(2)}) copy-start(f32[512]{0:T(512)} %param.11) | copy-start | bytes 6148
  37.6 3.5 %copy-start.15 = (bf16[512,8]{0,1:T(8,128)(2,1)S(1)}, bf16[512,8]{0,1:T(8,128)(2,1)}, u32[]{:S(2)}) copy-start(bf16[512,8]{0,1:T(8,128)(2,1)} %param.13) | copy-start | bytes 24580
  40.8 1.3 copy-start.12
  67.1 3.8 %copy-start.4 = (bf16[3,2,16,72,32]{3,4,2,1,0:T(8,128)(2,1)S(1)}, bf16[3,2,16,72,32]{3,4,2,1,0:T(8,128)(2,1)}, u32[]{:S(2)}) copy-start(bf16[3,2,16,72,32]{3,4,2,1,0:T(8,128)(2,1)} %copy.45) | copy-start | bytes 1327108
  67.1 3.8 %copy-start.5 = (bf16[3,2,1,16,72,32]{4,5,3,1,0,2:T(8,128)(2,1)S(1)}, bf16[3,2,1,16,72,32]{4,5,3,1,0,2:T(8,128)(2,1)}, u32[]{:S(2)}) copy-start(bf16[3,2,1,16,72,32]{4,5,3,1,0,2:T(8,128)(2,1)} %copy.57) | copy-start | bytes 1327108
  73.5 2.2 copy-start.6
  75.7 1.8 copy-start.7
  122.7 3.2 %copy-start.2 = (bf16[18,24,512]{2,1,0:T(8,128)(2,1)S(1)}, bf16[18,24,512]{2,1,0:T(8,128)(2,1)}, u32[]{:S(2)}) copy-start(bf16[18,24,512]{2,1,0:T(8,128)(2,1)} %copy-done.1) | copy-start | bytes 1327108
  227.5 3.2 %copy-start.11 = (bf16[432,512]{1,0:T(8,128)(2,1)}, bf16[432,512]{1,0:T(8,128)(2,1)S(1)}, u32[]{:S(2)}) copy-start(bf16[432,512]{1,0:T(8,128)(2,1)S(1)} %fusion.23) | copy-start | bytes 1327108
  228.2 27.3 %collective-permute-start.2 = (bf16[3,24,512]{2,1,0:T(8,128)(2,1)}, bf16[3,24,512]{2,1,0:T(8,128)(2,1)S(1)}, u32[]{:S(2)}, u32[]{:S(2)}) collective-permute-start(bf16[3,24,512]{2,1,0:T(8,128)(2,1)} %bitcast.9), channel_id=1, source_target_pairs={{480,0},{0,32},{32,64},{64,96},{96,128},{128,160},{160,192},{192,2... | collective-permute-start | bytes 221192 | tf_op jit(solution)/shard_map/ppermute | solution.py:16
  232.7 38.4 %copy-start.8 = (bf16[18,24,512]{2,1,0:T(8,128)(2,1)S(1)}, bf16[18,24,512]{2,1,0:T(8,128)(2,1)}, u32[]{:S(2)}) copy-start(bf16[18,24,512]{2,1,0:T(8,128)(2,1)} %param.9) | copy-start | bytes 1327108
  232.7 40.3 %copy-start.9 = (bf16[18,24,512]{2,1,0:T(8,128)(2,1)S(1)}, bf16[18,24,512]{2,1,0:T(8,128)(2,1)}, u32[]{:S(2)}) copy-start(bf16[18,24,512]{2,1,0:T(8,128)(2,1)} %param.10) | copy-start | bytes 1327108
  234.4 16.0 %all-to-all-start = ((f32[32,8,128]{2,1,0:T(8,128)}), f32[32,8,128]{2,1,0:T(8,128)S(1)}, u32[]{:S(2)}, u32[]{:S(2)}) async-start(f32[32,8,128]{2,1,0:T(8,128)} %fusion.37), calls=%async_computation | async-start | bytes 262144 | tf_op jit(solution)/shard_map/all_to_all | solution.py:155
  244.0 15.1 %collective-permute-start.6 = (bf16[3,24,512]{2,1,0:T(8,128)(2,1)}, bf16[3,24,512]{2,1,0:T(8,128)(2,1)S(1)}, u32[]{:S(2)}, u32[]{:S(2)}) collective-permute-start(bf16[3,24,512]{2,1,0:T(8,128)(2,1)} %bitcast.20), channel_id=1, source_target_pairs={{480,0},{0,32},{32,64},{64,96},{96,128},{128,160},{160,192},{192,2... | collective-permute-start | bytes 221192 | tf_op jit(solution)/shard_map/ppermute | solution.py:16
  251.1 11.8 %all-to-all-start.1 = ((f32[16,8,128]{2,1,0:T(8,128)}), f32[16,8,128]{2,1,0:T(8,128)S(1)}, u32[]{:S(2)}, u32[]{:S(2)}) async-start(f32[16,8,128]{2,1,0:T(8,128)} %broadcast_in_dim.72), calls=%async_computation.1 | async-start | bytes 131072 | tf_op jit(solution)/shard_map/all_to_all | solution.py:155
  256.2 14.9 %collective-permute-start.3 = (bf16[18,6,512]{2,1,0:T(8,128)(2,1)}, bf16[18,6,512]{2,1,0:T(8,128)(2,1)}, u32[]{:S(2)}, u32[]{:S(2)}) collective-permute-start(bf16[18,6,512]{2,1,0:T(8,128)(2,1)} %pad_maximum_fusion.4), channel_id=1, source_target_pairs={{31,0},{0,1},{1,2},{2,3},{3,4},{4,5},{5,6},{6,7},{7,8},{8,9},{9,10... | collective-permute-start | bytes 331784 | tf_op jit(solution)/shard_map/ppermute | solution.py:16
  259.7 13.3 %collective-permute-start.7 = (bf16[18,6,512]{2,1,0:T(8,128)(2,1)}, bf16[18,6,512]{2,1,0:T(8,128)(2,1)}, u32[]{:S(2)}, u32[]{:S(2)}) collective-permute-start(bf16[18,6,512]{2,1,0:T(8,128)(2,1)} %pad_maximum_fusion.3), channel_id=1, source_target_pairs={{31,0},{0,1},{1,2},{2,3},{3,4},{4,5},{5,6},{6,7},{7,8},{8,9},{9,10... | collective-permute-start | bytes 331784 | tf_op jit(solution)/shard_map/ppermute | solution.py:16
  263.6 18.3 %all-to-all-start.2 = ((f32[32,8,128]{2,1,0:T(8,128)}), f32[32,8,128]{2,1,0:T(8,128)S(1)}, u32[]{:S(2)}, u32[]{:S(2)}) async-start(f32[32,8,128]{2,1,0:T(8,128)} %broadcast_in_dim.73), calls=%async_computation.2 | async-start | bytes 262144 | tf_op jit(solution)/shard_map/all_to_all | solution.py:155

commit v2 on v0

v2 whole, which is shorter than its diff:
```python
import math

import jax
import jax.numpy as jnp
from jax import lax
from jax.experimental import pallas as pl
from jax.experimental.pallas import tpu as pltpu
from jax.sharding import PartitionSpec as P

HEADS = 16
WIN_LAT = 6
WIN_LON = 12
HALF_LAT = WIN_LAT // 2
HALF_LON = WIN_LON // 2
LAT_CELLS = 18
LON_CELLS = 24
D = 512
RANK = 8
CELLS = WIN_LAT * WIN_LON
SLOT = 80
BANDS = LAT_CELLS // WIN_LAT
ACROSS = LON_CELLS // WIN_LON
WINDOWS = BANDS * ACROSS
EARLY = ((0, 0), (1, 0))
LATE = ((0, 1), (1, 1), (2, 0), (2, 1))
ORDER = EARLY + LATE
SPAN = 160
TOKENS = WINDOWS * SLOT
OWN = LAT_CELLS * LON_CELLS
HEAD_WIDTH = D // HEADS
GROUP = 256 // HEAD_WIDTH
GROUPS = HEADS // GROUP
STACK = GROUP * SLOT
ROW_IN, COL_IN, COR_IN = 80, 112, 32
COL_FROM, COL_PART = (16, 48, 64), 48
PACK = 2 * RANK
WIDTH = 6 * D
ROW_OUT, COL_OUT, COR_OUT = 64, 96, 32
BF16 = jnp.bfloat16
F32 = jnp.float32
VMEM_ASKED = {"send": 60, "early": 60, "late": 55, "finish": 60, "place": 55}
FIXED = ("x", "c", "gain", "qkv", "out")


def own_from(a):
    return 64 + 144 * a


def marks_at(shape, source):
    row = lax.broadcasted_iota(jnp.int32, shape, 0)
    lane = lax.broadcasted_iota(jnp.int32, shape, 1)
    return jnp.where(lane == source(row), 1.0, 0.0).astype(BF16)


def over(value, divisor):
    factor, shift = {6: (10923, 16), 12: (10923, 17), 18: (7282, 17), 24: (10923, 18)}[divisor]
    return jnp.right_shift(value * factor, shift)


def pick(test, one, other):
    return jnp.where(test, one, other)


def place_send():
    def source(row):
        at = pick(row < COL_IN, row, row - COL_IN)
        r = over(at, HALF_LON)
        ends = pick(row < COL_IN, HALF_LON * LAT_CELLS, HALF_LON * HALF_LAT)
        return pick(at < ends, LON_CELLS * r + at - HALF_LON * r, -1)

    return marks_at((COL_IN + COR_IN, OWN), source)


def place_in(window, width):
    a, b = window

    def source(cell):
        r = over(cell, WIN_LON)
        c = cell - WIN_LON * r
        row, col = WIN_LAT * a + r + HALF_LAT, WIN_LON * b + c + HALF_LON
        at = LON_CELLS * row + col - own_from(a)
        if b == ACROSS - 1:
            side = SPAN + HALF_LON * row + col - LON_CELLS - COL_FROM[a]
            corner = SPAN + COL_PART + HALF_LON * (row - LAT_CELLS) + col - LON_CELLS
            at = pick(col < LON_CELLS, at, pick(row < LAT_CELLS, side, corner))
        return pick(cell < CELLS, at, -1)

    return marks_at((SLOT, width), source)


def place_last():
    def source(row):
        rho = over(row, LON_CELLS - HALF_LON)
        j = row - (LON_CELLS - HALF_LON) * rho
        cell = WIN_LON * (HALF_LAT + rho) + j
        along = pick(j < WIN_LON, cell, cell + SLOT - WIN_LON)
        along = pick(row < (LON_CELLS - HALF_LON) * HALF_LAT, along, -1)
        at = row - ROW_OUT
        rho = over(jnp.maximum(at, 0), HALF_LON)
        corner = SLOT + WIN_LON * (HALF_LAT + rho) + HALF_LON + at - HALF_LON * rho
        corner = pick(at < HALF_LON * HALF_LAT, corner, -1)
        return pick(row < ROW_OUT, along, corner)

    return marks_at((ROW_OUT + COR_OUT, ACROSS * SLOT), source)


def place_side():
    def source(row):
        i = over(row, HALF_LON)
        a = over(i, WIN_LAT)
        cell = WIN_LON * (i - WIN_LAT * a) + HALF_LON + row - HALF_LON * i
        return pick(row < HALF_LON * (LAT_CELLS - HALF_LAT), SLOT * a + cell, -1)

    return marks_at((COL_OUT, BANDS * SLOT), source)


def place_out(at):
    def source(row):
        r = over(row, LON_CELLS)
        col = row - LON_CELLS * r
        i, j = WIN_LAT * at + r - HALF_LAT, col - HALF_LON
        late = r >= HALF_LAT
        cell = WIN_LON * pick(late, r - HALF_LAT, r + HALF_LAT) + j
        cell = pick(j < WIN_LON, cell, cell + SLOT - WIN_LON)
        inner = pick(late, SPAN + cell, cell)
        edge = 2 * SPAN + HALF_LON * i + col
        if at == 0:
            inner = pick(late, inner, (LON_CELLS - HALF_LON) * r + j)
            edge = pick(late, edge, ROW_OUT + HALF_LON * r + col)
        return pick(j < 0, edge, inner)

    return marks_at((WIN_LAT * LON_CELLS, 2 * SPAN + COL_OUT), source)


def head_marks():
    lane = lax.broadcasted_iota(jnp.int32, (16, 256), 1)
    heads = [
        jnp.where(jnp.right_shift(lane, 5) == head, 1.0, 0.0).astype(BF16)
        for head in range(GROUP)
    ]
    return jnp.stack(heads, axis=0)


def nn(left, right):
    return lax.dot_general(left, right, (((1,), (0,)), ((), ())), preferred_element_type=F32)


def nt(left, right):
    return lax.dot_general(left, right, (((1,), (1,)), ((), ())), preferred_element_type=F32)


class Staged:
    def __init__(self, names, outside, buffers, sem):
        self.copies = {x: (outside[x], buffers[x], sem[x]) for x in names if x in buffers}
        self.buffers = {x: buffers.get(x, outside[x]) for x in names}
        self.open = {}

    def fetch(self):
        for name, (ref, buffer, sem) in self.copies.items():
            self.open[name] = pltpu.make_async_copy(ref, buffer, sem)
            self.open[name].start()

    def __getitem__(self, name):
        if name in self.open:
            self.open.pop(name).wait()
        return self.buffers[name]

    def send(self, *names):
        for name in names:
            if name not in self.copies:
                continue
            ref, buffer, sem = self.copies[name]
            self.open[name] = pltpu.make_async_copy(buffer, ref, sem)
            self.open[name].start()

    def close(self):
        for name in list(self.open):
            self.open.pop(name).wait()


def call(body, ins, outs, name, scratch=(), scalars=0, near=(), flops=0):
    in_names, out_names = list(ins)[scalars:], list(outs)
    arrays = list(ins.values())
    shapes = [jax.ShapeDtypeStruct(shape, dtype) for shape, dtype in outs.values()]
    names = in_names + out_names
    far = [x for x in names if x not in near]
    kinds = dict(zip(names, arrays[scalars:] + shapes))

    def kernel(*refs):
        heads, refs = refs[:scalars], refs[scalars:]
        outside, refs = dict(zip(names, refs)), refs[len(names) :]
        buffers, refs = dict(zip(far, refs)), refs[len(far) :]
        sems, rest = refs[0], refs[1:]
        sem = {x: sems.at[at] for at, x in enumerate(far)}
        given = Staged(in_names, outside, buffers, sem)
        made = Staged(out_names, outside, buffers, sem)
        given.fetch()
        body(given, made, *heads, *rest)
        given.close()
        made.close()

    def spec(x):
        if x in near:
            return pl.BlockSpec(memory_space=pltpu.VMEM)
        return pl.BlockSpec(memory_space=pltpu.HBM if x in FIXED else pl.ANY)

    return pl.pallas_call(
        kernel,
        out_shape=shapes,
        in_specs=[pl.BlockSpec(memory_space=pltpu.SMEM)] * scalars + [spec(x) for x in in_names],
        out_specs=[spec(x) for x in out_names],
        scratch_shapes=[pltpu.VMEM(kinds[x].shape, kinds[x].dtype) for x in far]
        + [pltpu.SemaphoreType.DMA((max(len(far), 1),))]
        + list(scratch),
        compiler_params=pltpu.CompilerParams(vmem_limit_bytes=VMEM_ASKED[name] << 20),
        cost_estimate=pl.CostEstimate(
            flops=flops, bytes_accessed=4 * 1024 * 1024, transcendentals=0
        ),
        name=name,
    )(*arrays)


def send_body(given, made):
    place = place_send()
    for at, name in enumerate(("x", "c")):
        ref = given[name]
        made["row"][ROW_IN * at : ROW_IN * (at + 1)] = ref[:ROW_IN]
        picked = nn(place, ref[...]).astype(BF16)
        made["col"][COL_IN * at : COL_IN * (at + 1)] = picked[:COL_IN]
        made["cor"][COR_IN * at : COR_IN * (at + 1)] = picked[COL_IN:]
    made.send("col", "row", "cor")


def split_heads(block, marks):
    tiles = block.reshape(1, SLOT // 16, 16, 256) * marks[:, None]
    return tiles.reshape(STACK, 256)


def join_heads(stacked):
    lane = lax.broadcasted_iota(jnp.int32, (SLOT, 128), 1)
    parts = [stacked[SLOT * h : SLOT * (h + 1)] for h in range(4)]
    low = jnp.where(lane < 32, parts[0], parts[1])
    high = jnp.where(lane < 96, parts[2], parts[3])
    return jnp.where(lane < 64, low, high)


def per_query(weights, block):
    turned = weights.T
    half = STACK // 2
    return jnp.concatenate(
        (
            join_heads(nn(turned[:half], block[:, :128])),
            join_heads(nn(turned[half:], block[:, 128:])),
        ),
        axis=1,
    )


def adapters(pack_ref):
    return (
        pack_ref[:, :D],
        pack_ref[:, D : 4 * D],
        pack_ref[:, 4 * D : 5 * D],
        pack_ref[:, 5 * D :],
    )


def attend(given, made, windows, blocks, pole, hidden, packed, bblend, marks_ref):
    count = len(windows)
    for first in range(0, count, 2):
        rows = pl.ds(SLOT * first, 2 * SLOT)
        for at, (source, into) in enumerate((("x", "xw"), ("c", "cw"))):
            blocks(given, made, source, at, into, first)
        wide = made["xw"][rows].astype(F32)
        center = wide - jnp.mean(wide, axis=-1, keepdims=True)
        spread = jnp.mean(center * center, axis=-1, keepdims=True)
        normed = (center * lax.rsqrt(spread + 1e-05) * given["gain"][...]).astype(BF16)
        hidden[rows] = normed
        down, up, odown, oup = adapters(given["pack"])
        low = nt(normed, down).astype(BF16)
        packed[rows] = (nn(normed, given["qkv"][...]) + nn(low, up)).astype(BF16)
        cot = made["cw"][rows]
        back_low = nt(cot, oup).astype(BF16)
        bblend[rows] = (nt(cot, given["out"][...]) + nn(back_low, odown)).astype(BF16)
    made.send("xw", "cw")

    marks_ref[...] = head_marks()
    blended_ref, back_ref = made["blended"], made["back"]
    rest = jnp.zeros((SLOT - CELLS, STACK), F32)
    scale = 1.0 / math.sqrt(HEAD_WIDTH)
    if pole is not None:
        key_late = lax.broadcasted_iota(jnp.int32, (CELLS, STACK), 0) >= CELLS // 2
        query_at = lax.rem(lax.broadcasted_iota(jnp.int32, (CELLS, STACK), 1), SLOT)
        apart = (key_late != (query_at >= CELLS // 2)).astype(F32) * -1e30

    def one_window(w, carry):
        rows = pl.ds(pl.multiple_of(w * SLOT, SLOT), SLOT)
        marks = marks_ref[...]
        for g in range(GROUPS):
            at = 256 * g
            query = packed[rows, at : at + 256]
            key = packed[rows, D + at : D + at + 256]
            value = packed[rows, 2 * D + at : 2 * D + at + 256]
            back = bblend[rows, at : at + 256]
            queries = split_heads(query, marks)
            backs = split_heads(back, marks)
            scores = nt(key, queries)[:CELLS] * scale
            if pole is not None:
                late = w >= sum(a < BANDS - 1 for a, _ in windows)
                scores = scores + apart * jnp.where(jnp.logical_and(pole > 0, late), 1.0, 0.0)
            top = jnp.max(scores, axis=0, keepdims=True)
            exponent = jnp.exp(scores - top)
            weights = exponent * (1.0 / jnp.sum(exponent, axis=0, keepdims=True))
            rounded = jnp.concatenate((weights, rest), axis=0).astype(BF16)
            blended_ref[rows, at : at + 256] = per_query(rounded, value).astype(BF16)
            back_weights = nt(value, backs)[:CELLS].astype(BF16).astype(F32)
            product = weights * back_weights
            total = jnp.sum(product, axis=0, keepdims=True)
            back_scores = (product - weights * total) * scale
            back_scores = jnp.concatenate((back_scores, rest), axis=0).astype(BF16)
            back_ref[rows, at : at + 256] = per_query(back_scores, key).astype(BF16)
            back_ref[rows, D + at : D + at + 256] = nn(back_scores, queries).astype(BF16)
            back_ref[rows, 2 * D + at : 2 * D + at + 256] = nn(rounded, backs).astype(BF16)
        return carry

    lax.fori_loop(0, count, one_window, 0, unroll=2)
    made.send("blended", "back")

    down, up, odown, oup = adapters(given["pack"])
    cot = made.buffers["cw"][...]
    blended = blended_ref[...]
    back = back_ref[...]
    return jnp.concatenate(
        (
            nn(nt(up, back).astype(BF16), hidden[...])[:RANK],
            nn(nt(down, hidden[...]).astype(BF16), back)[:RANK],
            nn(nt(oup, cot).astype(BF16), blended)[:RANK],
            nn(nt(odown, blended).astype(BF16), cot)[:RANK],
        ),
        axis=1,
    )


def early_blocks(given, made, source, at, into, first):
    for k in range(first, first + 2):
        begin = own_from(EARLY[k][0])
        own = given[source][begin : begin + SPAN]
        place = place_in(EARLY[k], SPAN)
        made[into][SLOT * k : SLOT * (k + 1)] = nn(place, own).astype(BF16)


def late_blocks(given, made, source, at, into, first):
    for k in range(first, first + 2):
        a, b = LATE[k]
        ref = given[source]
        begin = own_from(a)
        if a < BANDS - 1:
            own = ref[begin : begin + SPAN]
        else:
            row = given["row"][ROW_IN * at : ROW_IN * (at + 1)]
            own = jnp.concatenate((ref[begin:], row), axis=0)
        side = given["col"][pl.ds(COL_IN * at + COL_FROM[a], COL_PART)]
        corner = given["cor"][COR_IN * at : COR_IN * (at + 1)]
        block = jnp.concatenate((own, side, corner), axis=0)
        place = place_in(LATE[k], SPAN + COL_PART + COR_IN)
        made[into][SLOT * k : SLOT * (k + 1)] = nn(place, block).astype(BF16)


def early_body(given, made, *scratch):
    grads = attend(given, made, EARLY, early_blocks, None, *scratch)
    made["grads"][...] = grads
    made.send("grads")


def late_body(given, made, pole_ref, *scratch):
    grads = attend(given, made, LATE, late_blocks, pole_ref[0], *scratch)
    grads = grads + given["grads"][...]
    tiles = made["tiles"]
    for owner in range(16):
        at = 256 * owner
        if at < WIDTH:
            both = (grads[:, at : at + 128], grads[:, at + 128 : at + 256])
            tiles[owner] = jnp.concatenate(both, axis=0).astype(BF16)
        else:
            tiles[owner] = jnp.zeros((16, 128), BF16)
    made.send("tiles")


def finish_body(given, made):
    down, up, odown, oup = adapters(given["pack"])
    for part, first, count in (("1", 0, 1), ("2", 1, 2)):
        for k in range(count):
            rows = pl.ds(2 * SLOT * k, 2 * SLOT)
            into = pl.ds(2 * SLOT * (first + k), 2 * SLOT)
            wide = given["xw" + part][rows].astype(F32)
            blended = given["blended" + part][rows]
            low = nt(blended, odown).astype(BF16)
            update = (nn(blended, given["out"][...]) + nn(low, oup)).astype(BF16)
            made["mixed"][into] = (wide + update.astype(F32)).astype(BF16)
            back = given["back" + part][rows]
            back_low = nt(back, up).astype(BF16)
            back_hidden = nt(back, given["qkv"][...]) + nn(back_low, down)
            center = wide - jnp.mean(wide, axis=-1, keepdims=True)
            spread = jnp.mean(center * center, axis=-1, keepdims=True)
            inverse = lax.rsqrt(spread + 1e-05)
            normed = center * inverse
            scaled = back_hidden * given["gain"][...]
            along = jnp.mean(scaled * normed, axis=-1, keepdims=True)
            tokens = scaled - jnp.mean(scaled, axis=-1, keepdims=True) - normed * along
            tokens = (inverse * tokens).astype(BF16).astype(F32)
            cot = given["cw" + part][rows].astype(F32)
            made["grad"][into] = (cot + tokens).astype(BF16)
    last, side_place = place_last(), place_side()
    for at, name in enumerate(("mixed", "grad")):
        ref = made[name]
        ends = nn(last, ref[SLOT * 4 :]).astype(BF16)
        made["row"][ROW_OUT * at : ROW_OUT * (at + 1)] = ends[:ROW_OUT]
        made["cor"][COR_OUT * at : COR_OUT * (at + 1)] = ends[ROW_OUT:]
        ends = [ref[SLOT * k : SLOT * (k + 1)] for k in (2, 3, 5)]
        side = nn(side_place, jnp.concatenate(ends, axis=0)).astype(BF16)
        made["col"][COL_OUT * at : COL_OUT * (at + 1)] = side
    made.send("col", "row", "cor", "mixed", "grad")


def place_body(given, made):
    rows = WIN_LAT * LON_CELLS
    places = [place_out(a) for a in range(BANDS)]
    for at, name in enumerate(("mixed", "grad")):
        ref = given[name]

        def band(a):
            slots = [ORDER.index((a, b)) for b in range(ACROSS)]
            return [ref[SLOT * k : SLOT * (k + 1)] for k in slots]

        for a in range(BANDS):
            if a:
                before = band(a - 1)
            else:
                before = [
                    given["row"][ROW_OUT * at : ROW_OUT * (at + 1)],
                    given["cor"][COR_OUT * at : COR_OUT * (at + 1)],
                    ref[: SPAN - ROW_OUT - COR_OUT],
                ]
            side = given["col"][COL_OUT * at : COL_OUT * (at + 1)]
            source = jnp.concatenate((*before, *band(a), side), axis=0)
            out = made["all_" + name]
            out[rows * a : rows * (a + 1)] = nn(places[a], source).astype(BF16)
        made.send("all_" + name)


def grads_kernel(scale, tiles_ref, *outs):
    tile = 0
    for ref in outs:
        for at in range(ref.shape[1] // 128):
            both = tiles_ref[tile // 2].astype(F32) * scale
            part = both[8 * (tile % 2) : 8 * (tile % 2) + 8]
            ref[:, 128 * at : 128 * (at + 1)] = part
            tile += 1


def exchange(tiles, axis):
    return lax.all_to_all(tiles, axis, 0, 0, tiled=True)


def sum_tiles(tiles):
    return jnp.sum(tiles.astype(F32), axis=0).astype(BF16)


def gather_tiles(tile, axis):
    spread = jnp.broadcast_to(tile[None], (lax.axis_size(axis),) + tile.shape)
    return exchange(spread, axis)


def start_total(tiles):
    return exchange(tiles, "lat")


def total_over_mesh(own):
    own = sum_tiles(gather_tiles(sum_tiles(own), "lon"))
    return gather_tiles(own, "lat")


def moved(block, lat_step, lon_step):
    lats, lons = lax.axis_size("lat"), lax.axis_size("lon")
    if lat_step == 0:
        return lax.ppermute(block, "lon", [(i, (i + lon_step) % lons) for i in range(lons)])
    if lon_step == 0:
        return lax.ppermute(block, "lat", [(i, (i + lat_step) % lats) for i in range(lats)])
    route = [
        (i * lons + j, (i + lat_step) % lats * lons + (j + lon_step) % lons)
        for i in range(lats)
        for j in range(lons)
    ]
    return lax.ppermute(block, ("lat", "lon"), route)


def attended(count, last):
    outs = {
        "xw": ((SLOT * count, D), BF16),
        "cw": ((SLOT * count, D), BF16),
        "blended": ((SLOT * count, D), BF16),
        "back": ((SLOT * count, 3 * D), BF16),
    }
    outs.update(last)
    scratch = [
        pltpu.VMEM((SLOT * count, D), BF16),
        pltpu.VMEM((SLOT * count, 3 * D), BF16),
        pltpu.VMEM((SLOT * count, D), BF16),
        pltpu.VMEM((GROUP, 16, 256), BF16),
    ]
    return outs, scratch


def shards(
    fine_tokens, cotangent, norm_gain, qkv_weight, qkv_down, qkv_up, out_weight, out_down, out_up
):
    lats, lons = lax.axis_size("lat"), lax.axis_size("lon")
    tokens = fine_tokens.reshape(OWN, D)
    cots = cotangent.reshape(OWN, D)
    pack = jnp.concatenate((qkv_down.T, qkv_up, out_down.T, out_up), axis=1)
    pack = jnp.pad(pack, ((0, PACK - RANK), (0, 0)))
    weights = {
        "gain": norm_gain.reshape(1, D),
        "pack": pack,
        "qkv": qkv_weight,
        "out": out_weight,
    }
    pole = (lax.axis_index("lat") == lats - 1).astype(jnp.int32).reshape(1)
    row, col, cor = call(
        send_body,
        {"x": tokens, "c": cots},
        {
            "row": ((2 * ROW_IN, D), BF16),
            "col": ((2 * COL_IN, D), BF16),
            "cor": ((2 * COR_IN, D), BF16),
        },
        "send",
        near=("row", "col", "cor"),
        flops=10**8,
    )
    col = moved(col, 0, -1)
    row = moved(row, -1, 0)
    cor = moved(cor, -1, -1)
    outs, scratch = attended(len(EARLY), {"grads": ((RANK, WIDTH), F32)})
    xw1, cw1, blended1, back1, grads = call(
        early_body,
        {"x": tokens, "c": cots, **weights},
        outs,
        "early",
        scratch=scratch,
        flops=4 * 10**9,
    )
    outs, scratch = attended(len(LATE), {"tiles": ((16, 16, 128), BF16)})
    xw2, cw2, blended2, back2, tiles = call(
        late_body,
        {
            "pole": pole,
            "x": tokens,
            "col": col,
            "row": row,
            "cor": cor,
            "c": cots,
            **weights,
            "grads": grads,
        },
        outs,
        "late",
        scratch=scratch,
        scalars=1,
        near=("row", "col", "cor", "tiles"),
        flops=8 * 10**9,
    )
    own = start_total(tiles)
    mixed, grad, row, col, cor = call(
        finish_body,
        {
            "xw1": xw1,
            "blended1": blended1,
            "pack": pack,
            "out": out_weight,
            "back1": back1,
            "qkv": qkv_weight,
            "gain": weights["gain"],
            "cw1": cw1,
            "xw2": xw2,
            "blended2": blended2,
            "back2": back2,
            "cw2": cw2,
        },
        {
            "mixed": ((TOKENS, D), BF16),
            "grad": ((TOKENS, D), BF16),
            "row": ((2 * ROW_OUT, D), BF16),
            "col": ((2 * COL_OUT, D), BF16),
            "cor": ((2 * COR_OUT, D), BF16),
        },
        "finish",
        near=("row", "col", "cor"),
        flops=3 * 10**9,
    )
    own, mixed, grad, row, col, cor = lax.optimization_barrier((own, mixed, grad, row, col, cor))
    col = moved(col, 0, 1)
    row = moved(row, 1, 0)
    cor = moved(cor, 1, 1)
    tiles = total_over_mesh(own)
    mixed, grad = call(
        place_body,
        {"mixed": mixed, "row": row, "cor": cor, "col": col, "grad": grad},
        {"all_mixed": ((OWN, D), BF16), "all_grad": ((OWN, D), BF16)},
        "place",
        near=("row", "col", "cor"),
        flops=10**9,
    )
    scale = 1.0 / math.sqrt(OWN * lats * lons)

    def last_grads(*refs):
        grads_kernel(scale, *refs)

    grads = pl.pallas_call(
        last_grads,
        out_shape=[
            jax.ShapeDtypeStruct((RANK, D), F32),
            jax.ShapeDtypeStruct((RANK, 3 * D), F32),
            jax.ShapeDtypeStruct((RANK, D), F32),
            jax.ShapeDtypeStruct((RANK, D), F32),
        ],
        name="grads",
    )(tiles)
    shape = (LAT_CELLS, LON_CELLS, D)
    return (
        mixed.reshape(shape),
        grad.reshape(shape),
        grads[0].T,
        grads[1],
        grads[2].T,
        grads[3],
    )


def solution(mesh):
    in_specs = (P("lat", "lon", None), P("lat", "lon", None), P(), P(), P(), P(), P(), P(), P())
    out_specs = (P("lat", "lon", None), P("lat", "lon", None), P(), P(), P(), P())
    return jax.shard_map(shards, mesh=mesh, in_specs=in_specs, out_specs=out_specs, check_vma=False)
```

time: 427 us -> 96.5 us (0.23)
  waiting for transfers between devices: 258 us -> 3.07 us
  local copies, waits for them, and re-layouts: 66.6 us -> 3.97 us
  Pallas kernels: 0 us -> 36.4 us
  matrix products: 30.3 us -> 0 us
  other arithmetic: 18.4 us -> 1.47 us
  starting transfers between devices: 34.7 us -> 50 us
  between operations: 14.5 us -> 0.86 us
    psum x1 -> x0, waiting for transfers between devices: 255 us -> none  [shards(): summed = lax.psum((grads[0], grads[1], grads[2], grads[3]), ('lat', 'lon'))]
    pallas_call x0 -> x6, Pallas kernels: none -> 36.4 us  [the longest x5 34.9 us: call(): pl.pallas_call(kernel, out_shape=shapes, in_specs=[pl.BlockSpec(memory_sp...]
    dot_general x22 -> x0, matrix products: 30.3 us -> none  [the longest x6 7.59 us: times_transpose(): lax.dot_general(left, right, (((1,), (1,)), ((), ())), preferred_element_...]
    reshape x7 -> x0, local copies, waits for them, and re-layouts: 27.5 us -> none  [the longest x2 10.8 us: window_attention(): packed.reshape(lat_windows, WIN_LAT, lon_windows, WIN_LON, 3, HEADS, head...]
    all_to_all x0 -> x3, starting transfers between devices: none -> 16.3 us  [exchange(): return lax.all_to_all(tiles, axis, 0, 0, tiled=True)]
    slice x9 -> x0, local copies, waits for them, and re-layouts: 9.08 us -> none  [the longest x1 2.85 us: window_attention(): value_rows = window_tiles[:, :, 2]]
    transpose x2 -> x0, local copies, waits for them, and re-layouts: 9 us -> none  [the longest x1 5.92 us: window_attention(): window_tiles.transpose(0, 2, 4, 5, 1, 3, 6)]
    unnamed x33 -> x14, local copies, waits for them, and re-layouts: 10.4 us -> 2.67 us
  transfers between devices with their start and end apart: 9 -> 9, of which waited for: 3 -> 2; matrix products, arithmetic and copies ran while one was open for 3% -> 2% of each run, Pallas kernels for 0% -> 20%
where the time goes in v2:
time: 96.5 us; the launch traced here: 95.7 us
  starting transfers between devices  50 us (52%)
  Pallas kernels  36.4 us (38%)
  local copies, waits for them, and re-layouts  3.97 us (4%)
  waiting for transfers between devices  3.07 us (3%)
  other arithmetic  1.47 us (2%)
    pallas_call x5, Pallas kernels, call(): pl.pallas_call(kernel, out_shape=shapes, in_specs=[pl.BlockSpec(memory_sp...  34.9 us
    all_to_all x3, starting transfers between devices, exchange(): return lax.all_to_all(tiles, axis, 0, 0, tiled=True)  16.3 us
    ppermute x2, starting transfers between devices, moved(): lax.ppermute(block, 'lon', [(i, (i + lon_step) % lons) for i in range(lon...  16.2 us
    ppermute x2, starting transfers between devices, moved(): return lax.ppermute(block, ('lat', 'lon'), route)  11.5 us
    ppermute x2, starting transfers between devices, moved(): lax.ppermute(block, 'lat', [(i, (i + lat_step) % lats) for i in range(lat...  5.95 us
    all_to_all x3, waiting for transfers between devices, exchange(): return lax.all_to_all(tiles, axis, 0, 0, tiled=True)  3.06 us
    unnamed x14, local copies, waits for them, and re-layouts  2.67 us
  transfers between devices with their start and end apart: 9, of which 2 were waited for; matrix products, arithmetic and copies ran while one was open for 2% of the time, Pallas kernels for 20%

profile of v2, /device:TPU:1, one launch (start us, length us, event | category | flops | bytes accessed | tf_op | source)
XLA Modules:
  0.0 95.7 jit_solution(2150914980754538682)
XLA Ops:
  0.6 2.2 %send.1 = (bf16[160,512]{1,0:T(8,128)(2,1)}, bf16[224,512]{1,0:T(8,128)(2,1)}, bf16[64,512]{1,0:T(8,128)(2,1)}) custom-call(bf16[432,512]{1,0:T(8,128)(2,1)} %bitcast.10, bf16[432,512]{1,0:T(8,128)(2,1)} %bitcast.13), custom_call_target="tpu_custom_call" | custom-call | flops 100000000 | bytes 4194304 | tf_op jit(solution)/shard_map/send/pallas_call | solution.py:207
  2.8 8.3 %collective-permute-start.2 = (bf16[64,512]{1,0:T(8,128)(2,1)}, bf16[64,512]{1,0:T(8,128)(2,1)S(1)}, u32[]{:S(2)}, u32[]{:S(2)}) collective-permute-start(bf16[64,512]{1,0:T(8,128)(2,1)} %get-tuple-element.38), channel_id=1, source_target_pairs={{0,511},{1,480},{2,481},{3,482},{4,483},{5,484},{6,485},{7,486},{8... | collective-permute-start | bytes 196616 | tf_op jit(solution)/shard_map/ppermute | solution.py:494
  11.2 3.0 %collective-permute-start.1 = (bf16[160,512]{1,0:T(8,128)(2,1)}, bf16[160,512]{1,0:T(8,128)(2,1)S(1)}, u32[]{:S(2)}, u32[]{:S(2)}) collective-permute-start(bf16[160,512]{1,0:T(8,128)(2,1)} %get-tuple-element.37), channel_id=1, source_target_pairs={{0,480},{32,0},{64,32},{96,64},{128,96},{160,128},{192,160},{224,1... | collective-permute-start | bytes 491528 | tf_op jit(solution)/shard_map/ppermute | solution.py:488
  14.1 11.8 %collective-permute-start = (bf16[224,512]{1,0:T(8,128)(2,1)}, bf16[224,512]{1,0:T(8,128)(2,1)S(1)}, u32[]{:S(2)}, u32[]{:S(2)}) collective-permute-start(bf16[224,512]{1,0:T(8,128)(2,1)} %get-tuple-element.36), channel_id=1, source_target_pairs={{0,31},{1,0},{2,1},{3,2},{4,3},{5,4},{6,5},{7,6},{8,7},{9,8},{10,9... | collective-permute-start | bytes 688136 | tf_op jit(solution)/shard_map/ppermute | solution.py:486
  25.9 1.4 %fusion.6.refs_3_.refs_7_.refs_2_ = bf16[16,3072]{1,0:T(8,128)(2,1)} fusion(bf16[8,512]{1,0:T(8,128)(2,1)} %param.17, bf16[8,512]{1,0:T(8,128)(2,1)} %bitcast.16, bf16[8,1536]{1,0:T(8,128)(2,1)} %param.14, bf16[8,512]{1,0:T(8,128)(2,1)} %bitcast.17), kind=kLoop, calls=%fused_computation.7 | loop fusion | flops 638976 | bytes 147456 | tf_op jit(solution)/shard_map/concatenate | solution.py:520
  27.3 7.2 %early.1 = (bf16[160,512]{1,0:T(8,128)(2,1)}, bf16[160,512]{1,0:T(8,128)(2,1)}, bf16[160,512]{1,0:T(8,128)(2,1)}, bf16[160,1536]{1,0:T(8,128)(2,1)}, f32[8,3072]{1,0:T(8,128)}) custom-call(bf16[432,512]{1,0:T(8,128)(2,1)} %bitcast.11, bf16[432,512]{1,0:T(8,128)(2,1)} %bitcast.14, f32[1,512]{1,0:T(1,128)} %bitcast.20, ...), custom_call_target="tpu_custom_call" | custom-call | flops 4000000000 | bytes 4194304 | tf_op jit(solution)/shard_map/early/pallas_call | solution.py:207
  34.5 0.0 collective-permute-done.2.refs_4_
  34.5 0.0 copy-start.5
  34.5 0.0 collective-permute-done.1.refs_3_
  34.6 0.0 copy-start.3
  34.6 0.0 collective-permute-done.refs_2_
  34.6 0.0 copy-start.1
  34.6 0.6 copy-done.5
  35.2 0.1 copy-done.3
  35.2 0.1 copy-done.1
  35.3 13.2 %late.1 = (bf16[320,512]{1,0:T(8,128)(2,1)}, bf16[320,512]{1,0:T(8,128)(2,1)}, bf16[320,512]{1,0:T(8,128)(2,1)}, bf16[320,1536]{1,0:T(8,128)(2,1)}, bf16[16,16,128]{2,1,0:T(8,128)(2,1)}) custom-call(s32[1]{0:T(128)} %bitcast.refs_0_, bf16[432,512]{1,0:T(8,128)(2,1)} %bitcast.12, bf16[224,512]{1,0:T(8,128)(2,1)} %copy-done.1, bf16[160,512]{1,0:T(8,128)(2,1)} %copy-done.3, ...), custom_call_target="tpu_custom_call" | custom-call | flops 8000000000 | bytes 4194304 | tf_op jit(solution)/shard_map/late/pallas_call | solution.py:207
  48.5 3.7 %all-to-all-start = ((bf16[16,16,128]{2,1,0:T(8,128)(2,1)}), bf16[16,16,128]{2,1,0:T(8,128)(2,1)S(1)}, u32[]{:S(2)}, u32[]{:S(2)}) async-start(bf16[16,16,128]{2,1,0:T(8,128)(2,1)} %get-tuple-element.40), calls=%async_computation | async-start | bytes 131072 | tf_op jit(solution)/shard_map/all_to_all | solution.py:462
  52.2 8.7 %finish.1 = (bf16[480,512]{1,0:T(8,128)(2,1)}, bf16[480,512]{1,0:T(8,128)(2,1)}, bf16[128,512]{1,0:T(8,128)(2,1)}, bf16[192,512]{1,0:T(8,128)(2,1)}, bf16[64,512]{1,0:T(8,128)(2,1)}) custom-call(bf16[160,512]{1,0:T(8,128)(2,1)} %get-tuple-element.41.refs_0_, bf16[160,512]{1,0:T(8,128)(2,1)} %get-tuple-element.42.refs_1_, ...), custom_call_target="tpu_custom_call" | custom-call | flops 3000000000 | bytes 4194304 | tf_op jit(solution)/shard_map/finish/pallas_call | solution.py:207
  60.9 0.0 all-to-all-done
  60.9 0.7 broadcast_in_dim.4
  61.6 5.6 %all-to-all-start.1 = ((bf16[32,16,128]{2,1,0:T(8,128)(2,1)}), bf16[32,16,128]{2,1,0:T(8,128)(2,1)S(1)}, u32[]{:S(2)}, u32[]{:S(2)}) async-start(bf16[32,16,128]{2,1,0:T(8,128)(2,1)} %broadcast_in_dim.4), calls=%async_computation.1 | async-start | bytes 262144 | tf_op jit(solution)/shard_map/all_to_all | solution.py:462
  67.2 4.4 %collective-permute-start.5 = (bf16[192,512]{1,0:T(8,128)(2,1)}, bf16[192,512]{1,0:T(8,128)(2,1)S(1)}, u32[]{:S(2)}, u32[]{:S(2)}) collective-permute-start(bf16[192,512]{1,0:T(8,128)(2,1)} %get-tuple-element.57), channel_id=1, source_target_pairs={{0,1},{1,2},{2,3},{3,4},{4,5},{5,6},{6,7},{7,8},{8,9},{9,10},{10,1... | collective-permute-start | bytes 589832 | tf_op jit(solution)/shard_map/ppermute | solution.py:486
  71.7 3.0 %collective-permute-start.3 = (bf16[128,512]{1,0:T(8,128)(2,1)}, bf16[128,512]{1,0:T(8,128)(2,1)S(1)}, u32[]{:S(2)}, u32[]{:S(2)}) collective-permute-start(bf16[128,512]{1,0:T(8,128)(2,1)} %get-tuple-element.55), channel_id=1, source_target_pairs={{0,32},{32,64},{64,96},{96,128},{128,160},{160,192},{192,224},{224... | collective-permute-start | bytes 393224 | tf_op jit(solution)/shard_map/ppermute | solution.py:488
  74.6 3.2 %collective-permute-start.4 = (bf16[64,512]{1,0:T(8,128)(2,1)}, bf16[64,512]{1,0:T(8,128)(2,1)S(1)}, u32[]{:S(2)}, u32[]{:S(2)}) collective-permute-start(bf16[64,512]{1,0:T(8,128)(2,1)} %get-tuple-element.56), channel_id=1, source_target_pairs={{0,33},{1,34},{2,35},{3,36},{4,37},{5,38},{6,39},{7,40},{8,41},{9,... | collective-permute-start | bytes 196616 | tf_op jit(solution)/shard_map/ppermute | solution.py:494
  77.9 0.6 all-to-all-done.1
  78.5 0.6 broadcast_in_dim.5
  79.2 7.0 %all-to-all-start.2 = ((bf16[16,16,128]{2,1,0:T(8,128)(2,1)}), bf16[16,16,128]{2,1,0:T(8,128)(2,1)S(1)}, u32[]{:S(2)}, u32[]{:S(2)}) async-start(bf16[16,16,128]{2,1,0:T(8,128)(2,1)} %broadcast_in_dim.5), calls=%async_computation.2 | async-start | bytes 131072 | tf_op jit(solution)/shard_map/all_to_all | solution.py:462
  86.2 0.0 collective-permute-done.4.refs_2_
  86.2 0.0 copy-start.6
  86.2 0.0 collective-permute-done.3.refs_1_
  86.2 0.0 copy-start.4
  86.2 0.0 collective-permute-done.5.refs_3_
  86.2 0.6 copy-done.6
  86.8 0.1 copy-done.4
  86.9 0.0 copy-start.2
  86.9 0.7 copy-done.2
  87.5 3.6 %place.1 = (bf16[432,512]{1,0:T(8,128)(2,1)}, bf16[432,512]{1,0:T(8,128)(2,1)}) custom-call(bf16[480,512]{1,0:T(8,128)(2,1)} %get-tuple-element.54.refs_0_, bf16[128,512]{1,0:T(8,128)(2,1)} %copy-done.4, bf16[64,512]{1,0:T(8,128)(2,1)} %copy-done.6, bf16[192,512]{1,0:T(8,128)(2,1)} %copy-done.2, bf16[480,512]{1,0:T(8,128)(2,1)} %get-tuple-element.58.refs_4_), custom_call_target="tpu_custom_call" | custom-call | flops 1000000000 | bytes 4194304 | tf_op jit(solution)/shard_map/place/pallas_call | solution.py:207
  91.2 2.5 %all-to-all-done.2.refs_0_ = bf16[16,16,128]{2,1,0:T(8,128)(2,1)S(1)} async-done(((bf16[16,16,128]{2,1,0:T(8,128)(2,1)}), bf16[16,16,128]{2,1,0:T(8,128)(2,1)S(1)}, u32[]{:S(2)}, u32[]{:S(2)}) %all-to-all-start.2) | async-done | bytes 65568 | tf_op jit(solution)/shard_map/all_to_all | solution.py:462
  93.6 0.0 copy-start
  93.6 0.6 copy-done
  94.3 1.5 %grads.1 = (f32[8,512]{1,0:T(8,128)}, f32[8,1536]{1,0:T(8,128)}, f32[8,512]{1,0:T(8,128)}, f32[8,512]{1,0:T(8,128)}) custom-call(bf16[16,16,128]{2,1,0:T(8,128)(2,1)} %copy-done), custom_call_target="tpu_custom_call" | custom-call | tf_op jit(solution)/shard_map/grads/pallas_call | solution.py:619
  (2 shorter events, 0.1 us)
Async XLA Ops:
  2.8 31.7 %collective-permute-start.2 = (bf16[64,512]{1,0:T(8,128)(2,1)}, bf16[64,512]{1,0:T(8,128)(2,1)S(1)}, u32[]{:S(2)}, u32[]{:S(2)}) collective-permute-start(bf16[64,512]{1,0:T(8,128)(2,1)} %get-tuple-element.38), channel_id=1, source_target_pairs={{0,511},{1,480},{2,481},{3,482},{4,483},{5,484},{6,485},{7,486},{8... | collective-permute-start | bytes 196616 | tf_op jit(solution)/shard_map/ppermute | solution.py:494
  11.2 23.4 %collective-permute-start.1 = (bf16[160,512]{1,0:T(8,128)(2,1)}, bf16[160,512]{1,0:T(8,128)(2,1)S(1)}, u32[]{:S(2)}, u32[]{:S(2)}) collective-permute-start(bf16[160,512]{1,0:T(8,128)(2,1)} %get-tuple-element.37), channel_id=1, source_target_pairs={{0,480},{32,0},{64,32},{96,64},{128,96},{160,128},{192,160},{224,1... | collective-permute-start | bytes 491528 | tf_op jit(solution)/shard_map/ppermute | solution.py:488
  14.1 20.4 %collective-permute-start = (bf16[224,512]{1,0:T(8,128)(2,1)}, bf16[224,512]{1,0:T(8,128)(2,1)S(1)}, u32[]{:S(2)}, u32[]{:S(2)}) collective-permute-start(bf16[224,512]{1,0:T(8,128)(2,1)} %get-tuple-element.36), channel_id=1, source_target_pairs={{0,31},{1,0},{2,1},{3,2},{4,3},{5,4},{6,5},{7,6},{8,7},{9,8},{10,9... | collective-permute-start | bytes 688136 | tf_op jit(solution)/shard_map/ppermute | solution.py:486
  34.5 0.6 copy-start.5
  34.6 0.7 copy-start.3
  34.6 0.7 copy-start.1
  48.5 12.4 %all-to-all-start = ((bf16[16,16,128]{2,1,0:T(8,128)(2,1)}), bf16[16,16,128]{2,1,0:T(8,128)(2,1)S(1)}, u32[]{:S(2)}, u32[]{:S(2)}) async-start(bf16[16,16,128]{2,1,0:T(8,128)(2,1)} %get-tuple-element.40), calls=%async_computation | async-start | bytes 131072 | tf_op jit(solution)/shard_map/all_to_all | solution.py:462
  61.6 16.9 %all-to-all-start.1 = ((bf16[32,16,128]{2,1,0:T(8,128)(2,1)}), bf16[32,16,128]{2,1,0:T(8,128)(2,1)S(1)}, u32[]{:S(2)}, u32[]{:S(2)}) async-start(bf16[32,16,128]{2,1,0:T(8,128)(2,1)} %broadcast_in_dim.4), calls=%async_computation.1 | async-start | bytes 262144 | tf_op jit(solution)/shard_map/all_to_all | solution.py:462
  67.2 19.0 %collective-permute-start.5 = (bf16[192,512]{1,0:T(8,128)(2,1)}, bf16[192,512]{1,0:T(8,128)(2,1)S(1)}, u32[]{:S(2)}, u32[]{:S(2)}) collective-permute-start(bf16[192,512]{1,0:T(8,128)(2,1)} %get-tuple-element.57), channel_id=1, source_target_pairs={{0,1},{1,2},{2,3},{3,4},{4,5},{5,6},{6,7},{7,8},{8,9},{9,10},{10,1... | collective-permute-start | bytes 589832 | tf_op jit(solution)/shard_map/ppermute | solution.py:486
  71.7 14.5 %collective-permute-start.3 = (bf16[128,512]{1,0:T(8,128)(2,1)}, bf16[128,512]{1,0:T(8,128)(2,1)S(1)}, u32[]{:S(2)}, u32[]{:S(2)}) collective-permute-start(bf16[128,512]{1,0:T(8,128)(2,1)} %get-tuple-element.55), channel_id=1, source_target_pairs={{0,32},{32,64},{64,96},{96,128},{128,160},{160,192},{192,224},{224... | collective-permute-start | bytes 393224 | tf_op jit(solution)/shard_map/ppermute | solution.py:488
  74.6 11.5 %collective-permute-start.4 = (bf16[64,512]{1,0:T(8,128)(2,1)}, bf16[64,512]{1,0:T(8,128)(2,1)S(1)}, u32[]{:S(2)}, u32[]{:S(2)}) collective-permute-start(bf16[64,512]{1,0:T(8,128)(2,1)} %get-tuple-element.56), channel_id=1, source_target_pairs={{0,33},{1,34},{2,35},{3,36},{4,37},{5,38},{6,39},{7,40},{8,41},{9,... | collective-permute-start | bytes 196616 | tf_op jit(solution)/shard_map/ppermute | solution.py:494
  79.2 14.5 %all-to-all-start.2 = ((bf16[16,16,128]{2,1,0:T(8,128)(2,1)}), bf16[16,16,128]{2,1,0:T(8,128)(2,1)S(1)}, u32[]{:S(2)}, u32[]{:S(2)}) async-start(bf16[16,16,128]{2,1,0:T(8,128)(2,1)} %broadcast_in_dim.5), calls=%async_computation.2 | async-start | bytes 131072 | tf_op jit(solution)/shard_map/all_to_all | solution.py:462
  86.2 0.6 copy-start.6
  86.2 0.7 copy-start.4
  86.9 0.7 copy-start.2
  93.6 0.6 copy-start

commit v3 on v2

--- a/solution.py
+++ b/solution.py
@@ -33,13 +33,13 @@
 STACK = GROUP * SLOT
 ROW_IN, COL_IN, COR_IN = 80, 112, 32
 COL_FROM, COL_PART = (16, 48, 64), 48
-PACK = 2 * RANK
 WIDTH = 6 * D
 ROW_OUT, COL_OUT, COR_OUT = 64, 96, 32
 BF16 = jnp.bfloat16
 F32 = jnp.float32
-VMEM_ASKED = {"send": 60, "early": 60, "late": 55, "finish": 60, "place": 55}
-FIXED = ("x", "c", "gain", "qkv", "out")
+VMEM_ASKED = {"send": 60, "early": 53, "late": 52, "finish": 50, "place": 52, "grads": 52}
+GRADS = ("qkv_down", "qkv_up", "out_down", "out_up")
+FIXED = ("x", "c", "gain", "qkv", "out", "xw", "cw", "blended", "back", "mixed", "grad", "xw1", "xw2", "cw1", "cw2", "blended1", "blended2", "back1", "back2")
 
 
 def own_from(a):
@@ -155,8 +155,11 @@
         self.buffers = {x: buffers.get(x, outside[x]) for x in names}
         self.open = {}
 
-    def fetch(self):
-        for name, (ref, buffer, sem) in self.copies.items():
+    def fetch(self, names):
+        for name in names:
+            if name not in self.copies:
+                continue
+            ref, buffer, sem = self.copies[name]
             self.open[name] = pltpu.make_async_copy(ref, buffer, sem)
             self.open[name].start()
 
@@ -178,23 +181,27 @@
             self.open.pop(name).wait()
 
 
-def call(body, ins, outs, name, scratch=(), scalars=0, near=(), flops=0):
+def call(body, ins, outs, name, scratch=(), scalars=0, near=(), keep=(), first=(), flops=0):
+    arrays = list(ins.values())
+    outs = dict(outs, **{x + "_kept": (ins[x].shape, ins[x].dtype) for x in keep})
     in_names, out_names = list(ins)[scalars:], list(outs)
-    arrays = list(ins.values())
+    near = (*near, *(x + "_kept" for x in keep))
     shapes = [jax.ShapeDtypeStruct(shape, dtype) for shape, dtype in outs.values()]
     names = in_names + out_names
     far = [x for x in names if x not in near]
+    own = [x for x in far if x not in keep]
     kinds = dict(zip(names, arrays[scalars:] + shapes))
 
     def kernel(*refs):
         heads, refs = refs[:scalars], refs[scalars:]
         outside, refs = dict(zip(names, refs)), refs[len(names) :]
-        buffers, refs = dict(zip(far, refs)), refs[len(far) :]
+        buffers, refs = dict(zip(own, refs)), refs[len(own) :]
+        buffers.update({x: outside[x + "_kept"] for x in keep})
         sems, rest = refs[0], refs[1:]
         sem = {x: sems.at[at] for at, x in enumerate(far)}
         given = Staged(in_names, outside, buffers, sem)
         made = Staged(out_names, outside, buffers, sem)
-        given.fetch()
+        given.fetch(first or list(ins)[scalars:])
         body(given, made, *heads, *rest)
         given.close()
         made.close()
@@ -209,7 +216,7 @@
         out_shape=shapes,
         in_specs=[pl.BlockSpec(memory_space=pltpu.SMEM)] * scalars + [spec(x) for x in in_names],
         out_specs=[spec(x) for x in out_names],
-        scratch_shapes=[pltpu.VMEM(kinds[x].shape, kinds[x].dtype) for x in far]
+        scratch_shapes=[pltpu.VMEM(kinds[x].shape, kinds[x].dtype) for x in own]
         + [pltpu.SemaphoreType.DMA((max(len(far), 1),))]
         + list(scratch),
         compiler_params=pltpu.CompilerParams(vmem_limit_bytes=VMEM_ASKED[name] << 20),
@@ -257,28 +264,28 @@
 
 
 def adapters(pack_ref):
-    return (
-        pack_ref[:, :D],
-        pack_ref[:, D : 4 * D],
-        pack_ref[:, 4 * D : 5 * D],
-        pack_ref[:, 5 * D :],
-    )
+    wide = pack_ref[:, :WIDTH]
+    factors = jnp.concatenate((wide, jnp.zeros_like(wide)), axis=0).astype(BF16)
+    cuts = (0, D, 4 * D, 5 * D, WIDTH)
+    return *(factors[:, a:b] for a, b in zip(cuts, cuts[1:])), pack_ref[:1, WIDTH:]
 
 
 def attend(given, made, windows, blocks, pole, hidden, packed, bblend, marks_ref):
     count = len(windows)
     for first in range(0, count, 2):
         rows = pl.ds(SLOT * first, 2 * SLOT)
-        for at, (source, into) in enumerate((("x", "xw"), ("c", "cw"))):
-            blocks(given, made, source, at, into, first)
+        blocks(given, made, "x", 0, "xw", first)
+        if first == 0:
+            given.fetch(("qkv", "c", "out"))
+            down, up, odown, oup, gain = adapters(given["pack"])
         wide = made["xw"][rows].astype(F32)
         center = wide - jnp.mean(wide, axis=-1, keepdims=True)
         spread = jnp.mean(center * center, axis=-1, keepdims=True)
-        normed = (center * lax.rsqrt(spread + 1e-05) * given["gain"][...]).astype(BF16)
+        normed = (center * lax.rsqrt(spread + 1e-05) * gain).astype(BF16)
         hidden[rows] = normed
-        down, up, odown, oup = adapters(given["pack"])
         low = nt(normed, down).astype(BF16)
         packed[rows] = (nn(normed, given["qkv"][...]) + nn(low, up)).astype(BF16)
+        blocks(given, made, "c", 1, "cw", first)
         cot = made["cw"][rows]
         back_low = nt(cot, oup).astype(BF16)
         bblend[rows] = (nt(cot, given["out"][...]) + nn(back_low, odown)).astype(BF16)
@@ -326,7 +333,6 @@
     lax.fori_loop(0, count, one_window, 0, unroll=2)
     made.send("blended", "back")
 
-    down, up, odown, oup = adapters(given["pack"])
     cot = made.buffers["cw"][...]
     blended = blended_ref[...]
     back = back_ref[...]
@@ -357,10 +363,10 @@
         if a < BANDS - 1:
             own = ref[begin : begin + SPAN]
         else:
-            row = given["row"][ROW_IN * at : ROW_IN * (at + 1)]
+            row = given["row_in"][ROW_IN * at : ROW_IN * (at + 1)]
             own = jnp.concatenate((ref[begin:], row), axis=0)
-        side = given["col"][pl.ds(COL_IN * at + COL_FROM[a], COL_PART)]
-        corner = given["cor"][COR_IN * at : COR_IN * (at + 1)]
+        side = given["col_in"][pl.ds(COL_IN * at + COL_FROM[a], COL_PART)]
+        corner = given["cor_in"][COR_IN * at : COR_IN * (at + 1)]
         block = jnp.concatenate((own, side, corner), axis=0)
         place = place_in(LATE[k], SPAN + COL_PART + COR_IN)
         made[into][SLOT * k : SLOT * (k + 1)] = nn(place, block).astype(BF16)
@@ -387,8 +393,11 @@
 
 
 def finish_body(given, made):
-    down, up, odown, oup = adapters(given["pack"])
-    for part, first, count in (("1", 0, 1), ("2", 1, 2)):
+    parts = (("1", 0, 1), ("2", 1, 2))
+    given["xw1"], given["blended1"], given["out"]
+    given.fetch(("xw2", "blended2", "qkv", "back1", "cw1"))
+    down, up, odown, oup, gain = adapters(given["pack"])
+    for part, first, count in parts:
         for k in range(count):
             rows = pl.ds(2 * SLOT * k, 2 * SLOT)
             into = pl.ds(2 * SLOT * (first + k), 2 * SLOT)
@@ -397,6 +406,13 @@
             low = nt(blended, odown).astype(BF16)
             update = (nn(blended, given["out"][...]) + nn(low, oup)).astype(BF16)
             made["mixed"][into] = (wide + update.astype(F32)).astype(BF16)
+    given.fetch(("back2", "cw2"))
+    made.send("mixed")
+    for part, first, count in parts:
+        for k in range(count):
+            rows = pl.ds(2 * SLOT * k, 2 * SLOT)
+            into = pl.ds(2 * SLOT * (first + k), 2 * SLOT)
+            wide = given["xw" + part][rows].astype(F32)
             back = given["back" + part][rows]
             back_low = nt(back, up).astype(BF16)
             back_hidden = nt(back, given["qkv"][...]) + nn(back_low, down)
@@ -404,22 +420,23 @@
             spread = jnp.mean(center * center, axis=-1, keepdims=True)
             inverse = lax.rsqrt(spread + 1e-05)
             normed = center * inverse
-            scaled = back_hidden * given["gain"][...]
+            scaled = back_hidden * gain
             along = jnp.mean(scaled * normed, axis=-1, keepdims=True)
             tokens = scaled - jnp.mean(scaled, axis=-1, keepdims=True) - normed * along
             tokens = (inverse * tokens).astype(BF16).astype(F32)
             cot = given["cw" + part][rows].astype(F32)
             made["grad"][into] = (cot + tokens).astype(BF16)
+    made.send("grad")
     last, side_place = place_last(), place_side()
     for at, name in enumerate(("mixed", "grad")):
-        ref = made[name]
+        ref = made.buffers[name]
         ends = nn(last, ref[SLOT * 4 :]).astype(BF16)
         made["row"][ROW_OUT * at : ROW_OUT * (at + 1)] = ends[:ROW_OUT]
         made["cor"][COR_OUT * at : COR_OUT * (at + 1)] = ends[ROW_OUT:]
         ends = [ref[SLOT * k : SLOT * (k + 1)] for k in (2, 3, 5)]
         side = nn(side_place, jnp.concatenate(ends, axis=0)).astype(BF16)
         made["col"][COL_OUT * at : COL_OUT * (at + 1)] = side
-    made.send("col", "row", "cor", "mixed", "grad")
+    made.send("col", "row", "cor")
 
 
 def place_body(given, made):
@@ -448,14 +465,16 @@
         made.send("all_" + name)
 
 
-def grads_kernel(scale, tiles_ref, *outs):
+def grads_body(scale, given, made):
     tile = 0
-    for ref in outs:
+    for name in GRADS:
+        ref = made[name]
         for at in range(ref.shape[1] // 128):
-            both = tiles_ref[tile // 2].astype(F32) * scale
-            part = both[8 * (tile % 2) : 8 * (tile % 2) + 8]
-            ref[:, 128 * at : 128 * (at + 1)] = part
+            owner, row = tile // 2, RANK * (tile % 2)
+            wide = given["tiles"][owner].astype(F32) * scale
+            ref[:, 128 * at : 128 * (at + 1)] = wide[row : row + RANK]
             tile += 1
+    made.send(*GRADS)
 
 
 def exchange(tiles, axis):
@@ -517,10 +536,9 @@
     lats, lons = lax.axis_size("lat"), lax.axis_size("lon")
     tokens = fine_tokens.reshape(OWN, D)
     cots = cotangent.reshape(OWN, D)
-    pack = jnp.concatenate((qkv_down.T, qkv_up, out_down.T, out_up), axis=1)
-    pack = jnp.pad(pack, ((0, PACK - RANK), (0, 0)))
+    factors = [x.astype(F32) for x in (qkv_down.T, qkv_up, out_down.T, out_up)]
+    pack = jnp.concatenate((*factors, jnp.broadcast_to(norm_gain, (RANK, D))), axis=1)
     weights = {
-        "gain": norm_gain.reshape(1, D),
         "pack": pack,
         "qkv": qkv_weight,
         "out": out_weight,
@@ -542,12 +560,14 @@
     row = moved(row, -1, 0)
     cor = moved(cor, -1, -1)
     outs, scratch = attended(len(EARLY), {"grads": ((RANK, WIDTH), F32)})
-    xw1, cw1, blended1, back1, grads = call(
+    xw1, cw1, blended1, back1, grads, kept_pack, kept_qkv, kept_out = call(
         early_body,
         {"x": tokens, "c": cots, **weights},
         outs,
         "early",
         scratch=scratch,
+        keep=("pack", "qkv", "out"),
+        first=("x", "pack"),
         flops=4 * 10**9,
     )
     outs, scratch = attended(len(LATE), {"tiles": ((16, 16, 128), BF16)})
@@ -556,18 +576,21 @@
         {
             "pole": pole,
             "x": tokens,
-            "col": col,
-            "row": row,
-            "cor": cor,
             "c": cots,
-            **weights,
             "grads": grads,
+            "row_in": row,
+            "col_in": col,
+            "cor_in": cor,
+            "pack": kept_pack,
+            "qkv": kept_qkv,
+            "out": kept_out,
         },
         outs,
         "late",
         scratch=scratch,
         scalars=1,
-        near=("row", "col", "cor", "tiles"),
+        near=("row_in", "col_in", "cor_in", "tiles", "pack", "qkv", "out"),
+        first=("x", "grads"),
         flops=8 * 10**9,
     )
     own = start_total(tiles)
@@ -580,7 +603,6 @@
             "out": out_weight,
             "back1": back1,
             "qkv": qkv_weight,
-            "gain": weights["gain"],
             "cw1": cw1,
             "xw2": xw2,
             "blended2": blended2,
@@ -595,6 +617,7 @@
             "cor": ((2 * COR_OUT, D), BF16),
         },
         "finish",
+        first=("xw1", "blended1", "pack", "out"),
         near=("row", "col", "cor"),
         flops=3 * 10**9,
     )
@@ -614,18 +637,14 @@
     scale = 1.0 / math.sqrt(OWN * lats * lons)
 
     def last_grads(*refs):
-        grads_kernel(scale, *refs)
-
-    grads = pl.pallas_call(
+        grads_body(scale, *refs)
+
+    grads = call(
         last_grads,
-        out_shape=[
-            jax.ShapeDtypeStruct((RANK, D), F32),
-            jax.ShapeDtypeStruct((RANK, 3 * D), F32),
-            jax.ShapeDtypeStruct((RANK, D), F32),
-            jax.ShapeDtypeStruct((RANK, D), F32),
-        ],
-        name="grads",
-    )(tiles)
+        {"tiles": tiles},
+        dict(zip(GRADS, (((RANK, width), F32) for width in (D, 3 * D, D, D)))),
+        "grads",
+    )
     shape = (LAT_CELLS, LON_CELLS, D)
     return (
         mixed.reshape(shape),

time: 96.5 us -> 104 us (1.078)
  local copies, waits for them, and re-layouts: 3.97 us -> 6.72 us
  waiting for transfers between devices: 3.07 us -> 5.48 us
  Pallas kernels: 36.4 us -> 38.3 us
  other arithmetic: 1.47 us -> 2.9 us
    pallas_call x5 -> x6, Pallas kernels: 34.9 us -> 38.3 us  [call(): pl.pallas_call(kernel, out_shape=shapes, in_specs=[pl.BlockSpec(memory_sp...]
    unnamed x0 -> x4, other arithmetic: none -> 2.84 us
    all_to_all x3, waiting for transfers between devices: 3.06 us -> 5.47 us  [exchange(): return lax.all_to_all(tiles, axis, 0, 0, tiled=True)]
    unnamed x14 -> x16, local copies, waits for them, and re-layouts: 2.67 us -> 4.74 us
    pallas_call x1 -> x0, Pallas kernels: 1.48 us -> none  [shards(): pl.pallas_call(last_grads, out_shape=[jax.ShapeDtypeStruct((RANK, D), F32...]
    concatenate x1 -> x0, other arithmetic: 1.41 us -> none  [shards(): pack = jnp.concatenate((qkv_down.T, qkv_up, out_down.T, out_up), axis=1)]
    all_to_all x3, starting transfers between devices: 16.3 us -> 14.9 us  [exchange(): return lax.all_to_all(tiles, axis, 0, 0, tiled=True)]
  transfers between devices with their start and end apart: 9 -> 9, of which waited for: 2 -> 2; matrix products, arithmetic and copies ran while one was open for 2% -> 4% of each run, Pallas kernels for 20% -> 20%
where the time goes in v3:
time: 104 us; the launch traced here: 103 us
  starting transfers between devices  49 us (47%)
  Pallas kernels  38.3 us (37%)
  local copies, waits for them, and re-layouts  6.72 us (6%)
  waiting for transfers between devices  5.48 us (5%)
  other arithmetic  2.9 us (3%)
    pallas_call x6, Pallas kernels, call(): pl.pallas_call(kernel, out_shape=shapes, in_specs=[pl.BlockSpec(memory_sp...  38.3 us
    ppermute x2, starting transfers between devices, moved(): lax.ppermute(block, 'lon', [(i, (i + lon_step) % lons) for i in range(lon...  16.2 us
    all_to_all x3, starting transfers between devices, exchange(): return lax.all_to_all(tiles, axis, 0, 0, tiled=True)  14.9 us
    ppermute x2, starting transfers between devices, moved(): return lax.ppermute(block, ('lat', 'lon'), route)  11.5 us
    ppermute x2, starting transfers between devices, moved(): lax.ppermute(block, 'lat', [(i, (i + lat_step) % lats) for i in range(lat...  6.33 us
    all_to_all x3, waiting for transfers between devices, exchange(): return lax.all_to_all(tiles, axis, 0, 0, tiled=True)  5.47 us
    unnamed x16, local copies, waits for them, and re-layouts  4.74 us
    unnamed x4, other arithmetic  2.84 us
  transfers between devices with their start and end apart: 9, of which 2 were waited for; matrix products, arithmetic and copies ran while one was open for 4% of the time, Pallas kernels for 20%

profile of v3, /device:TPU:1, one launch (start us, length us, event | category | flops | bytes accessed | tf_op | source)
XLA Modules:
  0.0 103.4 jit_solution(7332549809815370943)
XLA Ops:
  0.6 2.2 %send.1 = (bf16[160,512]{1,0:T(8,128)(2,1)}, bf16[224,512]{1,0:T(8,128)(2,1)}, bf16[64,512]{1,0:T(8,128)(2,1)}) custom-call(bf16[432,512]{1,0:T(8,128)(2,1)} %bitcast.11, bf16[432,512]{1,0:T(8,128)(2,1)} %bitcast.14), custom_call_target="tpu_custom_call" | custom-call | flops 100000000 | bytes 4194304 | tf_op jit(solution)/shard_map/send/pallas_call | solution.py:214
  2.8 8.3 %collective-permute-start.2 = (bf16[64,512]{1,0:T(8,128)(2,1)}, bf16[64,512]{1,0:T(8,128)(2,1)S(1)}, u32[]{:S(2)}, u32[]{:S(2)}) collective-permute-start(bf16[64,512]{1,0:T(8,128)(2,1)} %get-tuple-element.42), channel_id=1, source_target_pairs={{0,511},{1,480},{2,481},{3,482},{4,483},{5,484},{6,485},{7,486},{8... | collective-permute-start | bytes 196616 | tf_op jit(solution)/shard_map/ppermute | solution.py:513
  11.1 3.0 %collective-permute-start = (bf16[160,512]{1,0:T(8,128)(2,1)}, bf16[160,512]{1,0:T(8,128)(2,1)S(1)}, u32[]{:S(2)}, u32[]{:S(2)}) collective-permute-start(bf16[160,512]{1,0:T(8,128)(2,1)} %get-tuple-element.40), channel_id=1, source_target_pairs={{0,480},{32,0},{64,32},{96,64},{128,96},{160,128},{192,160},{224,1... | collective-permute-start | bytes 491528 | tf_op jit(solution)/shard_map/ppermute | solution.py:507
  14.1 11.8 %collective-permute-start.1 = (bf16[224,512]{1,0:T(8,128)(2,1)}, bf16[224,512]{1,0:T(8,128)(2,1)S(1)}, u32[]{:S(2)}, u32[]{:S(2)}) collective-permute-start(bf16[224,512]{1,0:T(8,128)(2,1)} %get-tuple-element.41), channel_id=1, source_target_pairs={{0,31},{1,0},{2,1},{3,2},{4,3},{5,4},{6,5},{7,6},{8,7},{9,8},{10,9... | collective-permute-start | bytes 688136 | tf_op jit(solution)/shard_map/ppermute | solution.py:505
  25.9 0.7 bitcast_dynamic-update-slice_fusion.1
  26.6 0.7 convert_dynamic-update-slice_fusion
  27.4 0.7 bitcast_dynamic-update-slice_fusion
  28.1 0.7 convert_dynamic-update-slice_fusion.1
  28.8 0.7 constant_dynamic-update-slice_fusion.refs_2_
  29.5 10.1 %early.1 = (bf16[160,512]{1,0:T(8,128)(2,1)S(1)}, bf16[160,512]{1,0:T(8,128)(2,1)S(1)}, bf16[160,512]{1,0:T(8,128)(2,1)S(1)}, bf16[160,1536]{1,0:T(8,128)(2,1)},...) custom-call(bf16[432,512]{1,0:T(8,128)(2,1)} %bitcast.12, ...), custom_call_target="tpu_custom_call" | custom-call | flops 4000000000 | bytes 4194304 | tf_op jit(solution)/shard_map/early/pallas_call | solution.py:214
  39.5 0.0 copy-start.2
  39.6 0.7 copy-done.2
  40.2 0.0 copy-start.4
  40.2 0.7 copy-done.4
  40.9 0.0 copy-start.6
  40.9 0.7 copy-done.6
  41.5 0.0 collective-permute-done.2.refs_6_
  41.5 0.0 collective-permute-done.refs_4_
  41.5 0.0 collective-permute-done.1.refs_5_
  41.6 0.0 copy-start
  41.6 0.0 copy-start.1
  41.6 14.9 %late.1 = (bf16[320,512]{1,0:T(8,128)(2,1)S(1)}, bf16[320,512]{1,0:T(8,128)(2,1)S(1)}, bf16[320,512]{1,0:T(8,128)(2,1)S(1)}, bf16[320,1536]{1,0:T(8,128)(2,1)}, bf16[16,16,128]{2,1,0:T(8,128)(2,1)}) custom-call(s32[1]{0:T(128)} %bitcast.refs_0_, bf16[432,512]{1,0:T(8,128)(2,1)} %bitcast.13, bf16[432,512]{1,0:T(8,128)(2,1)} %bitcast.16, ...), custom_call_target="tpu_custom_call" | custom-call | flops 8000000000 | bytes 4194304 | tf_op jit(solution)/shard_map/late/pallas_call | solution.py:214
  56.5 3.7 %all-to-all-start = ((bf16[16,16,128]{2,1,0:T(8,128)(2,1)}), bf16[16,16,128]{2,1,0:T(8,128)(2,1)S(1)}, u32[]{:S(2)}, u32[]{:S(2)}) async-start(bf16[16,16,128]{2,1,0:T(8,128)(2,1)} %get-tuple-element.46), calls=%async_computation | async-start | bytes 131072 | tf_op jit(solution)/shard_map/all_to_all | solution.py:481
  60.2 0.0 copy-done
  60.2 0.0 copy-done.1
  60.2 0.0 copy-start.3
  60.2 0.9 copy-done.3
  61.1 0.0 copy-start.5
  61.1 0.9 copy-done.5
  62.0 0.0 copy-start.7
  62.1 0.9 copy-done.7
  63.0 7.9 %finish.1 = (bf16[480,512]{1,0:T(8,128)(2,1)S(1)}, bf16[480,512]{1,0:T(8,128)(2,1)S(1)}, bf16[128,512]{1,0:T(8,128)(2,1)S(1)}, bf16[192,512]{1,0:T(8,128)(2,1)S(1)}, bf16[64,512]{1,0:T(8,128)(2,1)S(1)}) custom-call(bf16[160,512]{1,0:T(8,128)(2,1)S(1)} %copy-done.3, bf16[160,512]{1,0:T(8,128)(2,1)S(1)} %copy-done.7, ...), custom_call_target="tpu_custom_call" | custom-call | flops 3000000000 | bytes 4194304 | tf_op jit(solution)/shard_map/finish/pallas_call | solution.py:214
  70.9 0.0 all-to-all-done
  71.0 0.7 broadcast_in_dim.7
  71.6 4.1 %all-to-all-start.1 = ((bf16[32,16,128]{2,1,0:T(8,128)(2,1)}), bf16[32,16,128]{2,1,0:T(8,128)(2,1)S(1)}, u32[]{:S(2)}, u32[]{:S(2)}) async-start(bf16[32,16,128]{2,1,0:T(8,128)(2,1)} %broadcast_in_dim.7), calls=%async_computation.1 | async-start | bytes 262144 | tf_op jit(solution)/shard_map/all_to_all | solution.py:481
  75.7 4.4 %collective-permute-start.5 = (bf16[192,512]{1,0:T(8,128)(2,1)S(1)}, bf16[192,512]{1,0:T(8,128)(2,1)S(1)}, u32[]{:S(2)}, u32[]{:S(2)}) collective-permute-start(bf16[192,512]{1,0:T(8,128)(2,1)S(1)} %get-tuple-element.63), channel_id=1, source_target_pairs={{0,1},{1,2},{2,3},{3,4},{4,5},{5,6},{6,7},{7,8},{8,9},{9,10},{10,1... | collective-permute-start | bytes 589832 | tf_op jit(solution)/shard_map/ppermute | solution.py:505
  80.2 3.4 %collective-permute-start.3 = (bf16[128,512]{1,0:T(8,128)(2,1)S(1)}, bf16[128,512]{1,0:T(8,128)(2,1)S(1)}, u32[]{:S(2)}, u32[]{:S(2)}) collective-permute-start(bf16[128,512]{1,0:T(8,128)(2,1)S(1)} %get-tuple-element.61), channel_id=1, source_target_pairs={{0,32},{32,64},{64,96},{96,128},{128,160},{160,192},{192,224},{224... | collective-permute-start | bytes 393224 | tf_op jit(solution)/shard_map/ppermute | solution.py:507
  83.5 3.2 %collective-permute-start.4 = (bf16[64,512]{1,0:T(8,128)(2,1)S(1)}, bf16[64,512]{1,0:T(8,128)(2,1)S(1)}, u32[]{:S(2)}, u32[]{:S(2)}) collective-permute-start(bf16[64,512]{1,0:T(8,128)(2,1)S(1)} %get-tuple-element.62), channel_id=1, source_target_pairs={{0,33},{1,34},{2,35},{3,36},{4,37},{5,38},{6,39},{7,40},{8,41},{9,... | collective-permute-start | bytes 196616 | tf_op jit(solution)/shard_map/ppermute | solution.py:513
  86.8 0.5 all-to-all-done.1
  87.3 0.6 broadcast_in_dim.8
  88.0 7.1 %all-to-all-start.2 = ((bf16[16,16,128]{2,1,0:T(8,128)(2,1)}), bf16[16,16,128]{2,1,0:T(8,128)(2,1)S(1)}, u32[]{:S(2)}, u32[]{:S(2)}) async-start(bf16[16,16,128]{2,1,0:T(8,128)(2,1)} %broadcast_in_dim.8), calls=%async_computation.2 | async-start | bytes 131072 | tf_op jit(solution)/shard_map/all_to_all | solution.py:481
  95.1 0.0 collective-permute-done.4.refs_2_
  95.1 0.0 collective-permute-done.3.refs_1_
  95.1 0.0 collective-permute-done.5.refs_3_
  95.1 2.4 %place.1 = (bf16[432,512]{1,0:T(8,128)(2,1)}, bf16[432,512]{1,0:T(8,128)(2,1)}) custom-call(bf16[480,512]{1,0:T(8,128)(2,1)S(1)} %get-tuple-element.60.refs_0_, bf16[128,512]{1,0:T(8,128)(2,1)S(1)} %collective-permute-done.3.refs_1_, bf16[64,512]{1,0:T(8,128)(2,1)S(1)} %collective-permute-done.4.refs_2_, ...), custom_call_target="tpu_custom_call" | custom-call | flops 1000000000 | bytes 4194304 | tf_op jit(solution)/shard_map/place/pallas_call | solution.py:214
  97.6 4.9 %all-to-all-done.2.refs_0_ = bf16[16,16,128]{2,1,0:T(8,128)(2,1)S(1)} async-done(((bf16[16,16,128]{2,1,0:T(8,128)(2,1)}), bf16[16,16,128]{2,1,0:T(8,128)(2,1)S(1)}, u32[]{:S(2)}, u32[]{:S(2)}) %all-to-all-start.2) | async-done | bytes 65568 | tf_op jit(solution)/shard_map/all_to_all | solution.py:481
  102.5 0.7 grads.1
  (2 shorter events, 0.1 us)
Async XLA Ops:
  2.8 38.7 %collective-permute-start.2 = (bf16[64,512]{1,0:T(8,128)(2,1)}, bf16[64,512]{1,0:T(8,128)(2,1)S(1)}, u32[]{:S(2)}, u32[]{:S(2)}) collective-permute-start(bf16[64,512]{1,0:T(8,128)(2,1)} %get-tuple-element.42), channel_id=1, source_target_pairs={{0,511},{1,480},{2,481},{3,482},{4,483},{5,484},{6,485},{7,486},{8... | collective-permute-start | bytes 196616 | tf_op jit(solution)/shard_map/ppermute | solution.py:513
  11.1 30.4 %collective-permute-start = (bf16[160,512]{1,0:T(8,128)(2,1)}, bf16[160,512]{1,0:T(8,128)(2,1)S(1)}, u32[]{:S(2)}, u32[]{:S(2)}) collective-permute-start(bf16[160,512]{1,0:T(8,128)(2,1)} %get-tuple-element.40), channel_id=1, source_target_pairs={{0,480},{32,0},{64,32},{96,64},{128,96},{160,128},{192,160},{224,1... | collective-permute-start | bytes 491528 | tf_op jit(solution)/shard_map/ppermute | solution.py:507
  14.1 27.4 %collective-permute-start.1 = (bf16[224,512]{1,0:T(8,128)(2,1)}, bf16[224,512]{1,0:T(8,128)(2,1)S(1)}, u32[]{:S(2)}, u32[]{:S(2)}) collective-permute-start(bf16[224,512]{1,0:T(8,128)(2,1)} %get-tuple-element.41), channel_id=1, source_target_pairs={{0,31},{1,0},{2,1},{3,2},{4,3},{5,4},{6,5},{7,6},{8,7},{9,8},{10,9... | collective-permute-start | bytes 688136 | tf_op jit(solution)/shard_map/ppermute | solution.py:505
  39.5 0.7 copy-start.2
  40.2 0.7 copy-start.4
  40.9 0.7 copy-start.6
  41.6 18.6 %copy-start = (bf16[512,512]{1,0:T(8,128)(2,1)S(1)}, bf16[512,512]{1,0:T(8,128)(2,1)}, u32[]{:S(2)}) copy-start(bf16[512,512]{1,0:T(8,128)(2,1)} %refs_3_.3) | copy-start | bytes 1572868
  41.6 18.6 %copy-start.1 = (bf16[160,1536]{1,0:T(8,128)(2,1)S(1)}, bf16[160,1536]{1,0:T(8,128)(2,1)}, u32[]{:S(2)}) copy-start(bf16[160,1536]{1,0:T(8,128)(2,1)} %get-tuple-element.49.refs_4_) | copy-start | bytes 1474564
  56.5 14.4 %all-to-all-start = ((bf16[16,16,128]{2,1,0:T(8,128)(2,1)}), bf16[16,16,128]{2,1,0:T(8,128)(2,1)S(1)}, u32[]{:S(2)}, u32[]{:S(2)}) async-start(bf16[16,16,128]{2,1,0:T(8,128)(2,1)} %get-tuple-element.46), calls=%async_computation | async-start | bytes 131072 | tf_op jit(solution)/shard_map/all_to_all | solution.py:481
  60.2 0.9 copy-start.3
  61.1 0.9 copy-start.5
  62.0 0.9 copy-start.7
  71.6 15.7 %all-to-all-start.1 = ((bf16[32,16,128]{2,1,0:T(8,128)(2,1)}), bf16[32,16,128]{2,1,0:T(8,128)(2,1)S(1)}, u32[]{:S(2)}, u32[]{:S(2)}) async-start(bf16[32,16,128]{2,1,0:T(8,128)(2,1)} %broadcast_in_dim.7), calls=%async_computation.1 | async-start | bytes 262144 | tf_op jit(solution)/shard_map/all_to_all | solution.py:481
  75.7 19.4 %collective-permute-start.5 = (bf16[192,512]{1,0:T(8,128)(2,1)S(1)}, bf16[192,512]{1,0:T(8,128)(2,1)S(1)}, u32[]{:S(2)}, u32[]{:S(2)}) collective-permute-start(bf16[192,512]{1,0:T(8,128)(2,1)S(1)} %get-tuple-element.63), channel_id=1, source_target_pairs={{0,1},{1,2},{2,3},{3,4},{4,5},{5,6},{6,7},{7,8},{8,9},{9,10},{10,1... | collective-permute-start | bytes 589832 | tf_op jit(solution)/shard_map/ppermute | solution.py:505
  80.2 14.9 %collective-permute-start.3 = (bf16[128,512]{1,0:T(8,128)(2,1)S(1)}, bf16[128,512]{1,0:T(8,128)(2,1)S(1)}, u32[]{:S(2)}, u32[]{:S(2)}) collective-permute-start(bf16[128,512]{1,0:T(8,128)(2,1)S(1)} %get-tuple-element.61), channel_id=1, source_target_pairs={{0,32},{32,64},{64,96},{96,128},{128,160},{160,192},{192,224},{224... | collective-permute-start | bytes 393224 | tf_op jit(solution)/shard_map/ppermute | solution.py:507
  83.5 11.6 %collective-permute-start.4 = (bf16[64,512]{1,0:T(8,128)(2,1)S(1)}, bf16[64,512]{1,0:T(8,128)(2,1)S(1)}, u32[]{:S(2)}, u32[]{:S(2)}) collective-permute-start(bf16[64,512]{1,0:T(8,128)(2,1)S(1)} %get-tuple-element.62), channel_id=1, source_target_pairs={{0,33},{1,34},{2,35},{3,36},{4,37},{5,38},{6,39},{7,40},{8,41},{9,... | collective-permute-start | bytes 196616 | tf_op jit(solution)/shard_map/ppermute | solution.py:513
  88.0 14.5 %all-to-all-start.2 = ((bf16[16,16,128]{2,1,0:T(8,128)(2,1)}), bf16[16,16,128]{2,1,0:T(8,128)(2,1)S(1)}, u32[]{:S(2)}, u32[]{:S(2)}) async-start(bf16[16,16,128]{2,1,0:T(8,128)(2,1)} %broadcast_in_dim.8), calls=%async_computation.2 | async-start | bytes 131072 | tf_op jit(solution)/shard_map/all_to_all | solution.py:481

commit v4 on v2

--- a/solution.py
+++ b/solution.py
@@ -38,7 +38,8 @@
 ROW_OUT, COL_OUT, COR_OUT = 64, 96, 32
 BF16 = jnp.bfloat16
 F32 = jnp.float32
-VMEM_ASKED = {"send": 60, "early": 60, "late": 55, "finish": 60, "place": 55}
+VMEM_ASKED = {"send": 60, "early": 60, "late": 52, "place": 52, "grads": 52}
+GRADS = ("qkv_down", "qkv_up", "out_down", "out_up")
 FIXED = ("x", "c", "gain", "qkv", "out")
 
 
@@ -178,18 +179,22 @@
             self.open.pop(name).wait()
 
 
-def call(body, ins, outs, name, scratch=(), scalars=0, near=(), flops=0):
+def call(body, ins, outs, name, scratch=(), scalars=0, near=(), keep=(), flops=0):
+    arrays = list(ins.values())
+    outs = dict(outs, **{x + "_kept": (ins[x].shape, ins[x].dtype) for x in keep})
     in_names, out_names = list(ins)[scalars:], list(outs)
-    arrays = list(ins.values())
+    near = (*near, *(x + "_kept" for x in keep))
     shapes = [jax.ShapeDtypeStruct(shape, dtype) for shape, dtype in outs.values()]
     names = in_names + out_names
     far = [x for x in names if x not in near]
+    own = [x for x in far if x not in keep]
     kinds = dict(zip(names, arrays[scalars:] + shapes))
 
     def kernel(*refs):
         heads, refs = refs[:scalars], refs[scalars:]
         outside, refs = dict(zip(names, refs)), refs[len(names) :]
-        buffers, refs = dict(zip(far, refs)), refs[len(far) :]
+        buffers, refs = dict(zip(own, refs)), refs[len(own) :]
+        buffers.update({x: outside[x + "_kept"] for x in keep})
         sems, rest = refs[0], refs[1:]
         sem = {x: sems.at[at] for at, x in enumerate(far)}
         given = Staged(in_names, outside, buffers, sem)
@@ -209,7 +214,7 @@
         out_shape=shapes,
         in_specs=[pl.BlockSpec(memory_space=pltpu.SMEM)] * scalars + [spec(x) for x in in_names],
         out_specs=[spec(x) for x in out_names],
-        scratch_shapes=[pltpu.VMEM(kinds[x].shape, kinds[x].dtype) for x in far]
+        scratch_shapes=[pltpu.VMEM(kinds[x].shape, kinds[x].dtype) for x in own]
         + [pltpu.SemaphoreType.DMA((max(len(far), 1),))]
         + list(scratch),
         compiler_params=pltpu.CompilerParams(vmem_limit_bytes=VMEM_ASKED[name] << 20),
@@ -265,13 +270,12 @@
     )
 
 
-def attend(given, made, windows, blocks, pole, hidden, packed, bblend, marks_ref):
+def attend(given, made, windows, blocks, ended, pole, tokens, cots, hidden, packed, bblend, blended_ref, back_ref, marks_ref, apart_ref):
     count = len(windows)
     for first in range(0, count, 2):
         rows = pl.ds(SLOT * first, 2 * SLOT)
-        for at, (source, into) in enumerate((("x", "xw"), ("c", "cw"))):
-            blocks(given, made, source, at, into, first)
-        wide = made["xw"][rows].astype(F32)
+        blocks(given, tokens, cots, first)
+        wide = tokens[rows].astype(F32)
         center = wide - jnp.mean(wide, axis=-1, keepdims=True)
         spread = jnp.mean(center * center, axis=-1, keepdims=True)
         normed = (center * lax.rsqrt(spread + 1e-05) * given["gain"][...]).astype(BF16)
@@ -279,23 +283,22 @@
         down, up, odown, oup = adapters(given["pack"])
         low = nt(normed, down).astype(BF16)
         packed[rows] = (nn(normed, given["qkv"][...]) + nn(low, up)).astype(BF16)
-        cot = made["cw"][rows]
+        cot = cots[rows]
         back_low = nt(cot, oup).astype(BF16)
         bblend[rows] = (nt(cot, given["out"][...]) + nn(back_low, odown)).astype(BF16)
-    made.send("xw", "cw")
 
     marks_ref[...] = head_marks()
-    blended_ref, back_ref = made["blended"], made["back"]
     rest = jnp.zeros((SLOT - CELLS, STACK), F32)
     scale = 1.0 / math.sqrt(HEAD_WIDTH)
+    marks = marks_ref[...]
     if pole is not None:
         key_late = lax.broadcasted_iota(jnp.int32, (CELLS, STACK), 0) >= CELLS // 2
         query_at = lax.rem(lax.broadcasted_iota(jnp.int32, (CELLS, STACK), 1), SLOT)
-        apart = (key_late != (query_at >= CELLS // 2)).astype(F32) * -1e30
-
-    def one_window(w, carry):
-        rows = pl.ds(pl.multiple_of(w * SLOT, SLOT), SLOT)
-        marks = marks_ref[...]
+        cut = jnp.where(pole > 0, -1e30, 0.0)
+        apart_ref[...] = (key_late != (query_at >= CELLS // 2)).astype(F32) * cut
+
+    for w, (a, _) in enumerate(windows):
+        rows = pl.ds(w * SLOT, SLOT)
         for g in range(GROUPS):
             at = 256 * g
             query = packed[rows, at : at + 256]
@@ -304,30 +307,44 @@
             back = bblend[rows, at : at + 256]
             queries = split_heads(query, marks)
             backs = split_heads(back, marks)
-            scores = nt(key, queries)[:CELLS] * scale
-            if pole is not None:
-                late = w >= sum(a < BANDS - 1 for a, _ in windows)
-                scores = scores + apart * jnp.where(jnp.logical_and(pole > 0, late), 1.0, 0.0)
+            scores = nt(key, queries)[:CELLS]
+            if a == BANDS - 1:
+                scores = scores + apart_ref[...]
             top = jnp.max(scores, axis=0, keepdims=True)
-            exponent = jnp.exp(scores - top)
+            exponent = jnp.exp2((scores - top) * (scale * math.log2(math.e)))
             weights = exponent * (1.0 / jnp.sum(exponent, axis=0, keepdims=True))
             rounded = jnp.concatenate((weights, rest), axis=0).astype(BF16)
             blended_ref[rows, at : at + 256] = per_query(rounded, value).astype(BF16)
             back_weights = nt(value, backs)[:CELLS].astype(BF16).astype(F32)
-            product = weights * back_weights
-            total = jnp.sum(product, axis=0, keepdims=True)
-            back_scores = (product - weights * total) * scale
+            total = jnp.sum(weights * back_weights, axis=0, keepdims=True)
+            back_scores = (weights * scale) * (back_weights - total)
             back_scores = jnp.concatenate((back_scores, rest), axis=0).astype(BF16)
             back_ref[rows, at : at + 256] = per_query(back_scores, key).astype(BF16)
             back_ref[rows, D + at : D + at + 256] = nn(back_scores, queries).astype(BF16)
             back_ref[rows, 2 * D + at : 2 * D + at + 256] = nn(rounded, backs).astype(BF16)
-        return carry
-
-    lax.fori_loop(0, count, one_window, 0, unroll=2)
-    made.send("blended", "back")
-
-    down, up, odown, oup = adapters(given["pack"])
-    cot = made.buffers["cw"][...]
+
+    for first in range(0, count, 2):
+        rows = pl.ds(SLOT * first, 2 * SLOT)
+        wide = tokens[rows].astype(F32)
+        blended = blended_ref[rows]
+        low = nt(blended, odown).astype(BF16)
+        update = (nn(blended, given["out"][...]) + nn(low, oup)).astype(BF16)
+        made["mixed"][rows] = (wide + update.astype(F32)).astype(BF16)
+        back = back_ref[rows]
+        back_low = nt(back, up).astype(BF16)
+        back_hidden = nt(back, given["qkv"][...]) + nn(back_low, down)
+        center = wide - jnp.mean(wide, axis=-1, keepdims=True)
+        spread = jnp.mean(center * center, axis=-1, keepdims=True)
+        inverse = lax.rsqrt(spread + 1e-05)
+        normed = center * inverse
+        scaled = back_hidden * given["gain"][...]
+        along = jnp.mean(scaled * normed, axis=-1, keepdims=True)
+        across = jnp.mean(scaled, axis=-1, keepdims=True)
+        change = (inverse * (scaled - across - normed * along)).astype(BF16).astype(F32)
+        made["grad"][rows] = (cots[rows].astype(F32) + change).astype(BF16)
+    made.send("mixed", "grad")
+    ended(made)
+    cot = cots[...]
     blended = blended_ref[...]
     back = back_ref[...]
     return jnp.concatenate(
@@ -341,39 +358,57 @@
     )
 
 
-def early_blocks(given, made, source, at, into, first):
+def early_blocks(given, tokens, cots, first):
     for k in range(first, first + 2):
         begin = own_from(EARLY[k][0])
-        own = given[source][begin : begin + SPAN]
         place = place_in(EARLY[k], SPAN)
-        made[into][SLOT * k : SLOT * (k + 1)] = nn(place, own).astype(BF16)
-
-
-def late_blocks(given, made, source, at, into, first):
+        for source, into in (("x", tokens), ("c", cots)):
+            own = given[source][begin : begin + SPAN]
+            into[SLOT * k : SLOT * (k + 1)] = nn(place, own).astype(BF16)
+
+
+def late_blocks(given, tokens, cots, first):
     for k in range(first, first + 2):
         a, b = LATE[k]
-        ref = given[source]
         begin = own_from(a)
-        if a < BANDS - 1:
-            own = ref[begin : begin + SPAN]
-        else:
-            row = given["row"][ROW_IN * at : ROW_IN * (at + 1)]
-            own = jnp.concatenate((ref[begin:], row), axis=0)
-        side = given["col"][pl.ds(COL_IN * at + COL_FROM[a], COL_PART)]
-        corner = given["cor"][COR_IN * at : COR_IN * (at + 1)]
-        block = jnp.concatenate((own, side, corner), axis=0)
         place = place_in(LATE[k], SPAN + COL_PART + COR_IN)
-        made[into][SLOT * k : SLOT * (k + 1)] = nn(place, block).astype(BF16)
+        for at, (source, into) in enumerate((("x", tokens), ("c", cots))):
+            if a < BANDS - 1:
+                own = given[source][begin : begin + SPAN]
+            else:
+                row = given["row_in"][ROW_IN * at : ROW_IN * (at + 1)]
+                own = jnp.concatenate((given[source][begin:], row), axis=0)
+            side = given["col_in"][pl.ds(COL_IN * at + COL_FROM[a], COL_PART)]
+            corner = given["cor_in"][COR_IN * at : COR_IN * (at + 1)]
+            block = jnp.concatenate((own, side, corner), axis=0)
+            into[SLOT * k : SLOT * (k + 1)] = nn(place, block).astype(BF16)
+
+
+def early_ended(made):
+    pass
+
+
+def late_ended(made):
+    last, side = place_last(), place_side()
+    for at, name in enumerate(("mixed", "grad")):
+        ref = made.buffers[name]
+        ends = nn(last, ref[SLOT * (len(LATE) - 2) :]).astype(BF16)
+        made["row"][ROW_OUT * at : ROW_OUT * (at + 1)] = ends[:ROW_OUT]
+        made["cor"][COR_OUT * at : COR_OUT * (at + 1)] = ends[ROW_OUT:]
+        beyond = [ref[SLOT * k : SLOT * (k + 1)] for k in (0, 1, 3)]
+        picked = nn(side, jnp.concatenate(beyond, axis=0)).astype(BF16)
+        made["col"][COL_OUT * at : COL_OUT * (at + 1)] = picked
+    made.send("col", "row", "cor")
 
 
 def early_body(given, made, *scratch):
-    grads = attend(given, made, EARLY, early_blocks, None, *scratch)
+    grads = attend(given, made, EARLY, early_blocks, early_ended, None, *scratch)
     made["grads"][...] = grads
     made.send("grads")
 
 
 def late_body(given, made, pole_ref, *scratch):
-    grads = attend(given, made, LATE, late_blocks, pole_ref[0], *scratch)
+    grads = attend(given, made, LATE, late_blocks, late_ended, pole_ref[0], *scratch)
     grads = grads + given["grads"][...]
     tiles = made["tiles"]
     for owner in range(16):
@@ -386,51 +421,19 @@
     made.send("tiles")
 
 
-def finish_body(given, made):
-    down, up, odown, oup = adapters(given["pack"])
-    for part, first, count in (("1", 0, 1), ("2", 1, 2)):
-        for k in range(count):
-            rows = pl.ds(2 * SLOT * k, 2 * SLOT)
-            into = pl.ds(2 * SLOT * (first + k), 2 * SLOT)
-            wide = given["xw" + part][rows].astype(F32)
-            blended = given["blended" + part][rows]
-            low = nt(blended, odown).astype(BF16)
-            update = (nn(blended, given["out"][...]) + nn(low, oup)).astype(BF16)
-            made["mixed"][into] = (wide + update.astype(F32)).astype(BF16)
-            back = given["back" + part][rows]
-            back_low = nt(back, up).astype(BF16)
-            back_hidden = nt(back, given["qkv"][...]) + nn(back_low, down)
-            center = wide - jnp.mean(wide, axis=-1, keepdims=True)
-            spread = jnp.mean(center * center, axis=-1, keepdims=True)
-            inverse = lax.rsqrt(spread + 1e-05)
-            normed = center * inverse
-            scaled = back_hidden * given["gain"][...]
-            along = jnp.mean(scaled * normed, axis=-1, keepdims=True)
-            tokens = scaled - jnp.mean(scaled, axis=-1, keepdims=True) - normed * along
-            tokens = (inverse * tokens).astype(BF16).astype(F32)
-            cot = given["cw" + part][rows].astype(F32)
-            made["grad"][into] = (cot + tokens).astype(BF16)
-    last, side_place = place_last(), place_side()
-    for at, name in enumerate(("mixed", "grad")):
-        ref = made[name]
-        ends = nn(last, ref[SLOT * 4 :]).astype(BF16)
-        made["row"][ROW_OUT * at : ROW_OUT * (at + 1)] = ends[:ROW_OUT]
-        made["cor"][COR_OUT * at : COR_OUT * (at + 1)] = ends[ROW_OUT:]
-        ends = [ref[SLOT * k : SLOT * (k + 1)] for k in (2, 3, 5)]
-        side = nn(side_place, jnp.concatenate(ends, axis=0)).astype(BF16)
-        made["col"][COL_OUT * at : COL_OUT * (at + 1)] = side
-    made.send("col", "row", "cor", "mixed", "grad")
-
-
 def place_body(given, made):
     rows = WIN_LAT * LON_CELLS
     places = [place_out(a) for a in range(BANDS)]
     for at, name in enumerate(("mixed", "grad")):
-        ref = given[name]
+        parts = {EARLY: given[name + "1"], LATE: given[name + "2"]}
+
+        def window(where):
+            part = EARLY if where in EARLY else LATE
+            k = part.index(where)
+            return parts[part][SLOT * k : SLOT * (k + 1)]
 
         def band(a):
-            slots = [ORDER.index((a, b)) for b in range(ACROSS)]
-            return [ref[SLOT * k : SLOT * (k + 1)] for k in slots]
+            return [window((a, b)) for b in range(ACROSS)]
 
         for a in range(BANDS):
             if a:
@@ -439,7 +442,7 @@
                 before = [
                     given["row"][ROW_OUT * at : ROW_OUT * (at + 1)],
                     given["cor"][COR_OUT * at : COR_OUT * (at + 1)],
-                    ref[: SPAN - ROW_OUT - COR_OUT],
+                    window((0, 0))[: SPAN - ROW_OUT - COR_OUT],
                 ]
             side = given["col"][COL_OUT * at : COL_OUT * (at + 1)]
             source = jnp.concatenate((*before, *band(a), side), axis=0)
@@ -448,14 +451,16 @@
         made.send("all_" + name)
 
 
-def grads_kernel(scale, tiles_ref, *outs):
+def grads_body(scale, given, made):
     tile = 0
-    for ref in outs:
+    for name in GRADS:
+        ref = made[name]
         for at in range(ref.shape[1] // 128):
-            both = tiles_ref[tile // 2].astype(F32) * scale
-            part = both[8 * (tile % 2) : 8 * (tile % 2) + 8]
-            ref[:, 128 * at : 128 * (at + 1)] = part
+            owner, row = tile // 2, RANK * (tile % 2)
+            wide = given["tiles"][owner].astype(F32) * scale
+            ref[:, 128 * at : 128 * (at + 1)] = wide[row : row + RANK]
             tile += 1
+    made.send(*GRADS)
 
 
 def exchange(tiles, axis):
@@ -495,20 +500,11 @@
 
 
 def attended(count, last):
-    outs = {
-        "xw": ((SLOT * count, D), BF16),
-        "cw": ((SLOT * count, D), BF16),
-        "blended": ((SLOT * count, D), BF16),
-        "back": ((SLOT * count, 3 * D), BF16),
-    }
+    outs = {"mixed": ((SLOT * count, D), BF16), "grad": ((SLOT * count, D), BF16)}
     outs.update(last)
-    scratch = [
-        pltpu.VMEM((SLOT * count, D), BF16),
-        pltpu.VMEM((SLOT * count, 3 * D), BF16),
-        pltpu.VMEM((SLOT * count, D), BF16),
-        pltpu.VMEM((GROUP, 16, 256), BF16),
-    ]
-    return outs, scratch
+    widths = (D, D, D, 3 * D, D, D, 3 * D)
+    scratch = [pltpu.VMEM((SLOT * count, width), BF16) for width in widths]
+    return outs, scratch + [pltpu.VMEM((GROUP, 16, 256), BF16), pltpu.VMEM((CELLS, STACK), F32)]
 
 
 def shards(
@@ -542,7 +538,7 @@
     row = moved(row, -1, 0)
     cor = moved(cor, -1, -1)
     outs, scratch = attended(len(EARLY), {"grads": ((RANK, WIDTH), F32)})
-    xw1, cw1, blended1, back1, grads = call(
+    mixed1, grad1, grads = call(
         early_body,
         {"x": tokens, "c": cots, **weights},
         outs,
@@ -550,62 +546,49 @@
         scratch=scratch,
         flops=4 * 10**9,
     )
-    outs, scratch = attended(len(LATE), {"tiles": ((16, 16, 128), BF16)})
-    xw2, cw2, blended2, back2, tiles = call(
+    last = {
+        "tiles": ((16, 16, 128), BF16),
+        "row": ((2 * ROW_OUT, D), BF16),
+        "col": ((2 * COL_OUT, D), BF16),
+        "cor": ((2 * COR_OUT, D), BF16),
+    }
+    outs, scratch = attended(len(LATE), last)
+    mixed2, grad2, tiles, row, col, cor = call(
         late_body,
         {
             "pole": pole,
             "x": tokens,
-            "col": col,
-            "row": row,
-            "cor": cor,
             "c": cots,
             **weights,
             "grads": grads,
+            "row_in": row,
+            "col_in": col,
+            "cor_in": cor,
         },
         outs,
         "late",
         scratch=scratch,
         scalars=1,
-        near=("row", "col", "cor", "tiles"),
+        near=("row_in", "col_in", "cor_in"),
         flops=8 * 10**9,
     )
     own = start_total(tiles)
-    mixed, grad, row, col, cor = call(
-        finish_body,
-        {
-            "xw1": xw1,
-            "blended1": blended1,
-            "pack": pack,
-            "out": out_weight,
-            "back1": back1,
-            "qkv": qkv_weight,
-            "gain": weights["gain"],
-            "cw1": cw1,
-            "xw2": xw2,
-            "blended2": blended2,
-            "back2": back2,
-            "cw2": cw2,
-        },
-        {
-            "mixed": ((TOKENS, D), BF16),
-            "grad": ((TOKENS, D), BF16),
-            "row": ((2 * ROW_OUT, D), BF16),
-            "col": ((2 * COL_OUT, D), BF16),
-            "cor": ((2 * COR_OUT, D), BF16),
-        },
-        "finish",
-        near=("row", "col", "cor"),
-        flops=3 * 10**9,
-    )
-    own, mixed, grad, row, col, cor = lax.optimization_barrier((own, mixed, grad, row, col, cor))
     col = moved(col, 0, 1)
+    own, row, cor = lax.optimization_barrier((own, row, cor))
     row = moved(row, 1, 0)
     cor = moved(cor, 1, 1)
     tiles = total_over_mesh(own)
     mixed, grad = call(
         place_body,
-        {"mixed": mixed, "row": row, "cor": cor, "col": col, "grad": grad},
+        {
+            "mixed1": mixed1,
+            "mixed2": mixed2,
+            "row": row,
+            "cor": cor,
+            "col": col,
+            "grad1": grad1,
+            "grad2": grad2,
+        },
         {"all_mixed": ((OWN, D), BF16), "all_grad": ((OWN, D), BF16)},
         "place",
         near=("row", "col", "cor"),
@@ -614,18 +597,14 @@
     scale = 1.0 / math.sqrt(OWN * lats * lons)
 
     def last_grads(*refs):
-        grads_kernel(scale, *refs)
-
-    grads = pl.pallas_call(
+        grads_body(scale, *refs)
+
+    grads = call(
         last_grads,
-        out_shape=[
-            jax.ShapeDtypeStruct((RANK, D), F32),
-            jax.ShapeDtypeStruct((RANK, 3 * D), F32),
-            jax.ShapeDtypeStruct((RANK, D), F32),
-            jax.ShapeDtypeStruct((RANK, D), F32),
-        ],
-        name="grads",
-    )(tiles)
+        {"tiles": tiles},
+        dict(zip(GRADS, (((RANK, width), F32) for width in (D, 3 * D, D, D)))),
+        "grads",
+    )
     shape = (LAT_CELLS, LON_CELLS, D)
     return (
         mixed.reshape(shape),

time: 96.5 us -> 91.8 us (0.951)
  blocking collectives: 0 us -> 10.4 us
  starting transfers between devices: 50 us -> 41.4 us
  Pallas kernels: 36.4 us -> 28.1 us
  waiting for transfers between devices: 3.07 us -> 6.42 us
  local copies, waits for them, and re-layouts: 3.97 us -> 2.21 us
    all_to_all x0 -> x1, blocking collectives: none -> 10.4 us  [exchange(): return lax.all_to_all(tiles, axis, 0, 0, tiled=True)]
    all_to_all x3 -> x2, starting transfers between devices: 16.3 us -> 8.82 us  [exchange(): return lax.all_to_all(tiles, axis, 0, 0, tiled=True)]
    pallas_call x5, Pallas kernels: 34.9 us -> 28.1 us  [call(): pl.pallas_call(kernel, out_shape=shapes, in_specs=[pl.BlockSpec(memory_sp...]
    all_to_all x3 -> x2, waiting for transfers between devices: 3.06 us -> 6.41 us  [exchange(): return lax.all_to_all(tiles, axis, 0, 0, tiled=True)]
    ppermute x2, starting transfers between devices: 11.5 us -> 14.8 us  [moved(): return lax.ppermute(block, ('lat', 'lon'), route)]
    ppermute x2, starting transfers between devices: 16.2 us -> 13.2 us  [moved(): lax.ppermute(block, 'lon', [(i, (i + lon_step) % lons) for i in range(lon...]
    unnamed x14 -> x10, local copies, waits for them, and re-layouts: 2.67 us -> 0.9 us
    pallas_call x1 -> x0, Pallas kernels: 1.48 us -> none  [shards(): pl.pallas_call(last_grads, out_shape=[jax.ShapeDtypeStruct((RANK, D), F32...]
  transfers between devices with their start and end apart: 9 -> 8, of which waited for: 2 -> 2; matrix products, arithmetic and copies ran while one was open for 2% -> 2% of each run, Pallas kernels for 20% -> 11%
where the time goes in v4:
time: 91.8 us; the launch traced here: 91 us
  starting transfers between devices  41.4 us (45%)
  Pallas kernels  28.1 us (31%)
  blocking collectives  10.4 us (11%)
  waiting for transfers between devices  6.42 us (7%)
  local copies, waits for them, and re-layouts  2.21 us (2%)
  other arithmetic  1.48 us (2%)
  between operations  0.99 us (1%)
    pallas_call x5, Pallas kernels, call(): pl.pallas_call(kernel, out_shape=shapes, in_specs=[pl.BlockSpec(memory_sp...  28.1 us
    ppermute x2, starting transfers between devices, moved(): return lax.ppermute(block, ('lat', 'lon'), route)  14.8 us
    ppermute x2, starting transfers between devices, moved(): lax.ppermute(block, 'lon', [(i, (i + lon_step) % lons) for i in range(lon...  13.2 us
    all_to_all x1, blocking collectives, exchange(): return lax.all_to_all(tiles, axis, 0, 0, tiled=True)  10.4 us
    all_to_all x2, starting transfers between devices, exchange(): return lax.all_to_all(tiles, axis, 0, 0, tiled=True)  8.82 us
    all_to_all x2, waiting for transfers between devices, exchange(): return lax.all_to_all(tiles, axis, 0, 0, tiled=True)  6.41 us
    ppermute x2, starting transfers between devices, moved(): lax.ppermute(block, 'lat', [(i, (i + lat_step) % lats) for i in range(lat...  4.55 us
  transfers between devices with their start and end apart: 8, of which 2 were waited for; matrix products, arithmetic and copies ran while one was open for 2% of the time, Pallas kernels for 11%

profile of v4, /device:TPU:1, one launch (start us, length us, event | category | flops | bytes accessed | tf_op | source)
XLA Modules:
  0.0 91.0 jit_solution(10297528943524270127)
XLA Ops:
  0.6 2.2 %send.1 = (bf16[160,512]{1,0:T(8,128)(2,1)}, bf16[224,512]{1,0:T(8,128)(2,1)}, bf16[64,512]{1,0:T(8,128)(2,1)}) custom-call(bf16[432,512]{1,0:T(8,128)(2,1)} %bitcast.12, bf16[432,512]{1,0:T(8,128)(2,1)} %bitcast.15), custom_call_target="tpu_custom_call" | custom-call | flops 100000000 | bytes 4194304 | tf_op jit(solution)/shard_map/send/pallas_call | solution.py:212
  2.8 8.8 %collective-permute-start.1 = (bf16[224,512]{1,0:T(8,128)(2,1)}, bf16[224,512]{1,0:T(8,128)(2,1)S(1)}, u32[]{:S(2)}, u32[]{:S(2)}) collective-permute-start(bf16[224,512]{1,0:T(8,128)(2,1)} %get-tuple-element.30), channel_id=1, source_target_pairs={{0,31},{1,0},{2,1},{3,2},{4,3},{5,4},{6,5},{7,6},{8,7},{9,8},{10,9... | collective-permute-start | bytes 688136 | tf_op jit(solution)/shard_map/ppermute | solution.py:491
  11.6 1.9 %collective-permute-start = (bf16[160,512]{1,0:T(8,128)(2,1)}, bf16[160,512]{1,0:T(8,128)(2,1)S(1)}, u32[]{:S(2)}, u32[]{:S(2)}) collective-permute-start(bf16[160,512]{1,0:T(8,128)(2,1)} %get-tuple-element.29), channel_id=1, source_target_pairs={{0,480},{32,0},{64,32},{96,64},{128,96},{160,128},{192,160},{224,1... | collective-permute-start | bytes 491528 | tf_op jit(solution)/shard_map/ppermute | solution.py:493
  13.6 12.5 %collective-permute-start.2 = (bf16[64,512]{1,0:T(8,128)(2,1)}, bf16[64,512]{1,0:T(8,128)(2,1)S(1)}, u32[]{:S(2)}, u32[]{:S(2)}) collective-permute-start(bf16[64,512]{1,0:T(8,128)(2,1)} %get-tuple-element.31), channel_id=1, source_target_pairs={{0,511},{1,480},{2,481},{3,482},{4,483},{5,484},{6,485},{7,486},{8... | collective-permute-start | bytes 196616 | tf_op jit(solution)/shard_map/ppermute | solution.py:499
  26.1 1.4 %fusion.6.refs_3_.refs_4_ = bf16[16,3072]{1,0:T(8,128)(2,1)} fusion(bf16[8,512]{1,0:T(8,128)(2,1)} %param.17, bf16[8,512]{1,0:T(8,128)(2,1)} %bitcast.18, bf16[8,1536]{1,0:T(8,128)(2,1)} %param.14, bf16[8,512]{1,0:T(8,128)(2,1)} %bitcast.19), kind=kLoop, calls=%fused_computation.7 | loop fusion | flops 638976 | bytes 147456 | tf_op jit(solution)/shard_map/concatenate | solution.py:516
  27.5 0.0 copy-start
  27.5 0.0 copy-start.1
  27.5 7.8 %early.1 = (bf16[160,512]{1,0:T(8,128)(2,1)}, bf16[160,512]{1,0:T(8,128)(2,1)}, f32[8,3072]{1,0:T(8,128)}) custom-call(bf16[432,512]{1,0:T(8,128)(2,1)} %bitcast.13, bf16[432,512]{1,0:T(8,128)(2,1)} %bitcast.16, f32[1,512]{1,0:T(1,128)} %bitcast.10, bf16[16,3072]{1,0:T(8,128)(2,1)} %fusion.6.refs_3_.refs_4_, bf16[512,1536]{1,0:T(8,128)(2,1)} %refs_5_.3, ...), custom_call_target="tpu_custom_call" | custom-call | flops 4000000000 | bytes 4194304 | tf_op jit(solution)/shard_map/early/pallas_call | solution.py:212
  35.3 0.0 collective-permute-done.2.refs_10_
  35.3 0.0 collective-permute-done.refs_8_
  35.3 0.0 collective-permute-done.1.refs_9_
  35.3 0.0 copy-done
  35.3 0.0 copy-done.1
  35.3 0.0 copy-start.4
  35.4 0.9 copy-done.4
  36.2 0.0 copy-start.2
  36.2 0.0 copy-start.3
  36.2 14.9 %late.1 = (bf16[320,512]{1,0:T(8,128)(2,1)S(1)}, bf16[320,512]{1,0:T(8,128)(2,1)S(1)}, bf16[16,16,128]{2,1,0:T(8,128)(2,1)S(1)}, bf16[128,512]{1,0:T(8,128)(2,1)...) custom-call(s32[1]{0:T(128)} %bitcast.5.refs_0_, bf16[432,512]{1,0:T(8,128)(2,1)} %bitcast.14, ...), custom_call_target="tpu_custom_call" | custom-call | flops 8000000000 | bytes 4194304 | tf_op jit(solution)/shard_map/late/pallas_call | solution.py:212
  51.2 10.4 %all_to_all.15 = bf16[16,16,128]{2,1,0:T(8,128)(2,1)S(1)} all-to-all(bf16[16,16,128]{2,1,0:T(8,128)(2,1)S(1)} %get-tuple-element.33), channel_id=1, replica_groups=mesh['lat'=16,'lon'=32] {'lat'}, dimensions={0} | all-to-all | bytes 131072 | tf_op jit(solution)/shard_map/all_to_all | solution.py:467
  61.6 0.7 broadcast_in_dim.4
  62.3 5.2 %all-to-all-start.1 = ((bf16[32,16,128]{2,1,0:T(8,128)(2,1)}), bf16[32,16,128]{2,1,0:T(8,128)(2,1)S(1)}, u32[]{:S(2)}, u32[]{:S(2)}) async-start(bf16[32,16,128]{2,1,0:T(8,128)(2,1)} %broadcast_in_dim.4), calls=%async_computation.1 | async-start | bytes 262144 | tf_op jit(solution)/shard_map/all_to_all | solution.py:467
  67.5 4.4 %collective-permute-start.5 = (bf16[192,512]{1,0:T(8,128)(2,1)S(1)}, bf16[192,512]{1,0:T(8,128)(2,1)S(1)}, u32[]{:S(2)}, u32[]{:S(2)}) collective-permute-start(bf16[192,512]{1,0:T(8,128)(2,1)S(1)} %get-tuple-element.38), channel_id=1, source_target_pairs={{0,1},{1,2},{2,3},{3,4},{4,5},{5,6},{6,7},{7,8},{8,9},{9,10},{10,1... | collective-permute-start | bytes 589832 | tf_op jit(solution)/shard_map/ppermute | solution.py:491
  71.9 2.6 %collective-permute-start.3 = (bf16[128,512]{1,0:T(8,128)(2,1)S(1)}, bf16[128,512]{1,0:T(8,128)(2,1)S(1)}, u32[]{:S(2)}, u32[]{:S(2)}) collective-permute-start(bf16[128,512]{1,0:T(8,128)(2,1)S(1)} %get-tuple-element.36), channel_id=1, source_target_pairs={{0,32},{32,64},{64,96},{96,128},{128,160},{160,192},{192,224},{224... | collective-permute-start | bytes 393224 | tf_op jit(solution)/shard_map/ppermute | solution.py:493
  74.6 2.3 %collective-permute-start.4 = (bf16[64,512]{1,0:T(8,128)(2,1)S(1)}, bf16[64,512]{1,0:T(8,128)(2,1)S(1)}, u32[]{:S(2)}, u32[]{:S(2)}) collective-permute-start(bf16[64,512]{1,0:T(8,128)(2,1)S(1)} %get-tuple-element.37), channel_id=1, source_target_pairs={{0,33},{1,34},{2,35},{3,36},{4,37},{5,38},{6,39},{7,40},{8,41},{9,... | collective-permute-start | bytes 196616 | tf_op jit(solution)/shard_map/ppermute | solution.py:499
  76.9 1.6 %all-to-all-done.1 = bf16[32,16,128]{2,1,0:T(8,128)(2,1)S(1)} async-done(((bf16[32,16,128]{2,1,0:T(8,128)(2,1)}), bf16[32,16,128]{2,1,0:T(8,128)(2,1)S(1)}, u32[]{:S(2)}, u32[]{:S(2)}) %all-to-all-start.1) | async-done | bytes 131104 | tf_op jit(solution)/shard_map/all_to_all | solution.py:467
  78.4 0.6 broadcast_in_dim.5
  79.1 3.7 %all-to-all-start.2 = ((bf16[16,16,128]{2,1,0:T(8,128)(2,1)}), bf16[16,16,128]{2,1,0:T(8,128)(2,1)S(1)}, u32[]{:S(2)}, u32[]{:S(2)}) async-start(bf16[16,16,128]{2,1,0:T(8,128)(2,1)} %broadcast_in_dim.5), calls=%async_computation.2 | async-start | bytes 131072 | tf_op jit(solution)/shard_map/all_to_all | solution.py:467
  82.7 0.0 collective-permute-done.4.refs_3_
  82.8 0.0 collective-permute-done.5.refs_4_
  82.8 0.0 collective-permute-done.3.refs_2_
  82.8 0.0 copy-done.2
  82.8 0.0 copy-done.3
  82.8 2.5 %place.1 = (bf16[432,512]{1,0:T(8,128)(2,1)}, bf16[432,512]{1,0:T(8,128)(2,1)}) custom-call(bf16[160,512]{1,0:T(8,128)(2,1)S(1)} %copy-done.2, bf16[320,512]{1,0:T(8,128)(2,1)S(1)} %get-tuple-element.32.refs_1_, bf16[128,512]{1,0:T(8,128)(2,1)S(1)} %collective-permute-done.3.refs_2_, bf16[64,512]{1,0:T(8,128)(2,1)S(1)} %collective-permute-done.4.refs_3_, ...), custom_call_target="tpu_custom_call" | custom-call | flops 1000000000 | bytes 4194304 | tf_op jit(solution)/shard_map/place/pallas_call | solution.py:212
  85.3 4.9 %all-to-all-done.2.refs_0_ = bf16[16,16,128]{2,1,0:T(8,128)(2,1)S(1)} async-done(((bf16[16,16,128]{2,1,0:T(8,128)(2,1)}), bf16[16,16,128]{2,1,0:T(8,128)(2,1)S(1)}, u32[]{:S(2)}, u32[]{:S(2)}) %all-to-all-start.2) | async-done | bytes 65568 | tf_op jit(solution)/shard_map/all_to_all | solution.py:467
  90.1 0.7 grads.1
  (2 shorter events, 0.1 us)
Async XLA Ops:
  2.8 32.5 %collective-permute-start.1 = (bf16[224,512]{1,0:T(8,128)(2,1)}, bf16[224,512]{1,0:T(8,128)(2,1)S(1)}, u32[]{:S(2)}, u32[]{:S(2)}) collective-permute-start(bf16[224,512]{1,0:T(8,128)(2,1)} %get-tuple-element.30), channel_id=1, source_target_pairs={{0,31},{1,0},{2,1},{3,2},{4,3},{5,4},{6,5},{7,6},{8,7},{9,8},{10,9... | collective-permute-start | bytes 688136 | tf_op jit(solution)/shard_map/ppermute | solution.py:491
  11.6 23.7 %collective-permute-start = (bf16[160,512]{1,0:T(8,128)(2,1)}, bf16[160,512]{1,0:T(8,128)(2,1)S(1)}, u32[]{:S(2)}, u32[]{:S(2)}) collective-permute-start(bf16[160,512]{1,0:T(8,128)(2,1)} %get-tuple-element.29), channel_id=1, source_target_pairs={{0,480},{32,0},{64,32},{96,64},{128,96},{160,128},{192,160},{224,1... | collective-permute-start | bytes 491528 | tf_op jit(solution)/shard_map/ppermute | solution.py:493
  13.6 21.7 %collective-permute-start.2 = (bf16[64,512]{1,0:T(8,128)(2,1)}, bf16[64,512]{1,0:T(8,128)(2,1)S(1)}, u32[]{:S(2)}, u32[]{:S(2)}) collective-permute-start(bf16[64,512]{1,0:T(8,128)(2,1)} %get-tuple-element.31), channel_id=1, source_target_pairs={{0,511},{1,480},{2,481},{3,482},{4,483},{5,484},{6,485},{7,486},{8... | collective-permute-start | bytes 196616 | tf_op jit(solution)/shard_map/ppermute | solution.py:499
  27.5 7.8 %copy-start = (bf16[16,3072]{1,0:T(8,128)(2,1)S(1)}, bf16[16,3072]{1,0:T(8,128)(2,1)}, u32[]{:S(2)}) copy-start(bf16[16,3072]{1,0:T(8,128)(2,1)} %fusion.6.refs_3_.refs_4_) | copy-start | bytes 294916
  27.5 7.8 %copy-start.1 = (f32[512]{0:T(512)S(1)}, f32[512]{0:T(512)}, u32[]{:S(2)}) copy-start(f32[512]{0:T(512)} %param.11) | copy-start | bytes 6148
  35.3 0.9 copy-start.4
  36.2 46.5 %copy-start.2 = (bf16[160,512]{1,0:T(8,128)(2,1)S(1)}, bf16[160,512]{1,0:T(8,128)(2,1)}, u32[]{:S(2)}) copy-start(bf16[160,512]{1,0:T(8,128)(2,1)} %get-tuple-element.27.refs_0_) | copy-start | bytes 491524
  36.2 46.5 %copy-start.3 = (bf16[160,512]{1,0:T(8,128)(2,1)S(1)}, bf16[160,512]{1,0:T(8,128)(2,1)}, u32[]{:S(2)}) copy-start(bf16[160,512]{1,0:T(8,128)(2,1)} %get-tuple-element.39.refs_5_) | copy-start | bytes 491524
  62.3 16.1 %all-to-all-start.1 = ((bf16[32,16,128]{2,1,0:T(8,128)(2,1)}), bf16[32,16,128]{2,1,0:T(8,128)(2,1)S(1)}, u32[]{:S(2)}, u32[]{:S(2)}) async-start(bf16[32,16,128]{2,1,0:T(8,128)(2,1)} %broadcast_in_dim.4), calls=%async_computation.1 | async-start | bytes 262144 | tf_op jit(solution)/shard_map/all_to_all | solution.py:467
  67.5 15.3 %collective-permute-start.5 = (bf16[192,512]{1,0:T(8,128)(2,1)S(1)}, bf16[192,512]{1,0:T(8,128)(2,1)S(1)}, u32[]{:S(2)}, u32[]{:S(2)}) collective-permute-start(bf16[192,512]{1,0:T(8,128)(2,1)S(1)} %get-tuple-element.38), channel_id=1, source_target_pairs={{0,1},{1,2},{2,3},{3,4},{4,5},{5,6},{6,7},{7,8},{8,9},{9,10},{10,1... | collective-permute-start | bytes 589832 | tf_op jit(solution)/shard_map/ppermute | solution.py:491
  71.9 10.8 %collective-permute-start.3 = (bf16[128,512]{1,0:T(8,128)(2,1)S(1)}, bf16[128,512]{1,0:T(8,128)(2,1)S(1)}, u32[]{:S(2)}, u32[]{:S(2)}) collective-permute-start(bf16[128,512]{1,0:T(8,128)(2,1)S(1)} %get-tuple-element.36), channel_id=1, source_target_pairs={{0,32},{32,64},{64,96},{96,128},{128,160},{160,192},{192,224},{224... | collective-permute-start | bytes 393224 | tf_op jit(solution)/shard_map/ppermute | solution.py:493
  74.6 8.2 %collective-permute-start.4 = (bf16[64,512]{1,0:T(8,128)(2,1)S(1)}, bf16[64,512]{1,0:T(8,128)(2,1)S(1)}, u32[]{:S(2)}, u32[]{:S(2)}) collective-permute-start(bf16[64,512]{1,0:T(8,128)(2,1)S(1)} %get-tuple-element.37), channel_id=1, source_target_pairs={{0,33},{1,34},{2,35},{3,36},{4,37},{5,38},{6,39},{7,40},{8,41},{9,... | collective-permute-start | bytes 196616 | tf_op jit(solution)/shard_map/ppermute | solution.py:499
  79.1 11.0 %all-to-all-start.2 = ((bf16[16,16,128]{2,1,0:T(8,128)(2,1)}), bf16[16,16,128]{2,1,0:T(8,128)(2,1)S(1)}, u32[]{:S(2)}, u32[]{:S(2)}) async-start(bf16[16,16,128]{2,1,0:T(8,128)(2,1)} %broadcast_in_dim.5), calls=%async_computation.2 | async-start | bytes 131072 | tf_op jit(solution)/shard_map/all_to_all | solution.py:467

commit v5 on v4

--- a/solution.py
+++ b/solution.py
@@ -38,7 +38,7 @@
 ROW_OUT, COL_OUT, COR_OUT = 64, 96, 32
 BF16 = jnp.bfloat16
 F32 = jnp.float32
-VMEM_ASKED = {"send": 60, "early": 60, "late": 52, "place": 52, "grads": 52}
+VMEM_ASKED = {"send": 60, "early": 60, "late": 52, "finish": 50, "place": 52, "grads": 52}
 GRADS = ("qkv_down", "qkv_up", "out_down", "out_up")
 FIXED = ("x", "c", "gain", "qkv", "out")
 
@@ -270,7 +270,35 @@
     )
 
 
-def attend(given, made, windows, blocks, ended, pole, tokens, cots, hidden, packed, bblend, blended_ref, back_ref, marks_ref, apart_ref):
+def finish(given, made, count, tokens, cots, blended_ref, back_ref):
+    down, up, odown, oup = adapters(given["pack"])
+    blocks = [pl.ds(SLOT * first, 2 * SLOT) for first in range(0, count, 2)]
+    for rows in blocks:
+        wide = tokens()[rows].astype(F32)
+        blended = blended_ref()[rows]
+        low = nt(blended, odown).astype(BF16)
+        update = (nn(blended, given["out"][...]) + nn(low, oup)).astype(BF16)
+        made["mixed"][rows] = (wide + update.astype(F32)).astype(BF16)
+    made.send("mixed")
+    for rows in blocks:
+        wide = tokens()[rows].astype(F32)
+        back = back_ref()[rows]
+        back_low = nt(back, up).astype(BF16)
+        back_hidden = nt(back, given["qkv"][...]) + nn(back_low, down)
+        center = wide - jnp.mean(wide, axis=-1, keepdims=True)
+        spread = jnp.mean(center * center, axis=-1, keepdims=True)
+        inverse = lax.rsqrt(spread + 1e-05)
+        normed = center * inverse
+        scaled = back_hidden * given["gain"][...]
+        along = jnp.mean(scaled * normed, axis=-1, keepdims=True)
+        across = jnp.mean(scaled, axis=-1, keepdims=True)
+        change = (inverse * (scaled - across - normed * along)).astype(BF16).astype(F32)
+        made["grad"][rows] = (cots()[rows].astype(F32) + change).astype(BF16)
+    made.send("grad")
+
+
+def attend(given, made, windows, blocks, pole, places, hidden, packed, bblend, marks_ref, apart_ref):
+    tokens, cots, blended_ref, back_ref = places
     count = len(windows)
     for first in range(0, count, 2):
         rows = pl.ds(SLOT * first, 2 * SLOT)
@@ -323,27 +351,10 @@
             back_ref[rows, D + at : D + at + 256] = nn(back_scores, queries).astype(BF16)
             back_ref[rows, 2 * D + at : 2 * D + at + 256] = nn(rounded, backs).astype(BF16)
 
-    for first in range(0, count, 2):
-        rows = pl.ds(SLOT * first, 2 * SLOT)
-        wide = tokens[rows].astype(F32)
-        blended = blended_ref[rows]
-        low = nt(blended, odown).astype(BF16)
-        update = (nn(blended, given["out"][...]) + nn(low, oup)).astype(BF16)
-        made["mixed"][rows] = (wide + update.astype(F32)).astype(BF16)
-        back = back_ref[rows]
-        back_low = nt(back, up).astype(BF16)
-        back_hidden = nt(back, given["qkv"][...]) + nn(back_low, down)
-        center = wide - jnp.mean(wide, axis=-1, keepdims=True)
-        spread = jnp.mean(center * center, axis=-1, keepdims=True)
-        inverse = lax.rsqrt(spread + 1e-05)
-        normed = center * inverse
-        scaled = back_hidden * given["gain"][...]
-        along = jnp.mean(scaled * normed, axis=-1, keepdims=True)
-        across = jnp.mean(scaled, axis=-1, keepdims=True)
-        change = (inverse * (scaled - across - normed * along)).astype(BF16).astype(F32)
-        made["grad"][rows] = (cots[rows].astype(F32) + change).astype(BF16)
-    made.send("mixed", "grad")
-    ended(made)
+    made.send("xw", "cw", "blended", "back")
+    down, up, odown, oup = adapters(given["pack"])
+    if "mixed" in made.buffers:
+        finish(given, made, count, *(lambda x=x: x for x in places))
     cot = cots[...]
     blended = blended_ref[...]
     back = back_ref[...]
@@ -384,11 +395,7 @@
             into[SLOT * k : SLOT * (k + 1)] = nn(place, block).astype(BF16)
 
 
-def early_ended(made):
-    pass
-
-
-def late_ended(made):
+def send_back(made):
     last, side = place_last(), place_side()
     for at, name in enumerate(("mixed", "grad")):
         ref = made.buffers[name]
@@ -402,13 +409,14 @@
 
 
 def early_body(given, made, *scratch):
-    grads = attend(given, made, EARLY, early_blocks, early_ended, None, *scratch)
-    made["grads"][...] = grads
+    places, rest = scratch[:4], scratch[4:]
+    made["grads"][...] = attend(given, made, EARLY, early_blocks, None, places, *rest)
     made.send("grads")
 
 
 def late_body(given, made, pole_ref, *scratch):
-    grads = attend(given, made, LATE, late_blocks, late_ended, pole_ref[0], *scratch)
+    places = [made.buffers[x] for x in ("xw", "cw", "blended", "back")]
+    grads = attend(given, made, LATE, late_blocks, pole_ref[0], places, *scratch)
     grads = grads + given["grads"][...]
     tiles = made["tiles"]
     for owner in range(16):
@@ -419,6 +427,16 @@
         else:
             tiles[owner] = jnp.zeros((16, 128), BF16)
     made.send("tiles")
+
+
+def finish_body(given, made):
+    finish(
+        given,
+        made,
+        len(LATE),
+        *(lambda x=x: given[x] for x in ("xw", "cw", "blended", "back")),
+    )
+    send_back(made)
 
 
 def place_body(given, made):
@@ -499,12 +517,13 @@
     return lax.ppermute(block, ("lat", "lon"), route)
 
 
-def attended(count, last):
-    outs = {"mixed": ((SLOT * count, D), BF16), "grad": ((SLOT * count, D), BF16)}
-    outs.update(last)
-    widths = (D, D, D, 3 * D, D, D, 3 * D)
-    scratch = [pltpu.VMEM((SLOT * count, width), BF16) for width in widths]
-    return outs, scratch + [pltpu.VMEM((GROUP, 16, 256), BF16), pltpu.VMEM((CELLS, STACK), F32)]
+def shapes_of(count, *widths):
+    return [((SLOT * count, width), BF16) for width in widths]
+
+
+def scratch_of(count, *widths):
+    buffers = [pltpu.VMEM(*x) for x in shapes_of(count, *widths, D, 3 * D, D)]
+    return [*buffers, pltpu.VMEM((GROUP, 16, 256), BF16), pltpu.VMEM((CELLS, STACK), F32)]
 
 
 def shards(
@@ -537,7 +556,9 @@
     col = moved(col, 0, -1)
     row = moved(row, -1, 0)
     cor = moved(cor, -1, -1)
-    outs, scratch = attended(len(EARLY), {"grads": ((RANK, WIDTH), F32)})
+    outs = dict(zip(("mixed", "grad"), shapes_of(len(EARLY), D, D)))
+    outs["grads"] = ((RANK, WIDTH), F32)
+    scratch = scratch_of(len(EARLY), D, D, D, 3 * D)
     mixed1, grad1, grads = call(
         early_body,
         {"x": tokens, "c": cots, **weights},
@@ -546,14 +567,10 @@
         scratch=scratch,
         flops=4 * 10**9,
     )
-    last = {
-        "tiles": ((16, 16, 128), BF16),
-        "row": ((2 * ROW_OUT, D), BF16),
-        "col": ((2 * COL_OUT, D), BF16),
-        "cor": ((2 * COR_OUT, D), BF16),
-    }
-    outs, scratch = attended(len(LATE), last)
-    mixed2, grad2, tiles, row, col, cor = call(
+    outs = dict(zip(("xw", "cw", "blended", "back"), shapes_of(len(LATE), D, D, D, 3 * D)))
+    outs["tiles"] = ((16, 16, 128), BF16)
+    scratch = scratch_of(len(LATE))
+    xw, cw, blended, back, tiles = call(
         late_body,
         {
             "pole": pole,
@@ -573,6 +590,27 @@
         flops=8 * 10**9,
     )
     own = start_total(tiles)
+    outs = dict(zip(("mixed", "grad"), shapes_of(len(LATE), D, D)))
+    outs["row"] = ((2 * ROW_OUT, D), BF16)
+    outs["col"] = ((2 * COL_OUT, D), BF16)
+    outs["cor"] = ((2 * COR_OUT, D), BF16)
+    mixed2, grad2, row, col, cor = call(
+        finish_body,
+        {
+            "xw": xw,
+            "blended": blended,
+            "pack": pack,
+            "out": out_weight,
+            "back": back,
+            "qkv": qkv_weight,
+            "gain": weights["gain"],
+            "cw": cw,
+        },
+        outs,
+        "finish",
+        near=("row", "col", "cor"),
+        flops=2 * 10**9,
+    )
     col = moved(col, 0, 1)
     own, row, cor = lax.optimization_barrier((own, row, cor))
     row = moved(row, 1, 0)

time: 91.8 us -> 92.7 us (level)
  blocking collectives: 10.4 us -> 0 us
  starting transfers between devices: 41.4 us -> 48.5 us
  Pallas kernels: 28.1 us -> 30.9 us
  local copies, waits for them, and re-layouts: 2.21 us -> 3.41 us
    all_to_all x1 -> x0, blocking collectives: 10.4 us -> none  [exchange(): return lax.all_to_all(tiles, axis, 0, 0, tiled=True)]
    all_to_all x2 -> x3, starting transfers between devices: 8.82 us -> 15.6 us  [exchange(): return lax.all_to_all(tiles, axis, 0, 0, tiled=True)]
    ppermute x2, starting transfers between devices: 14.8 us -> 11.1 us  [moved(): return lax.ppermute(block, ('lat', 'lon'), route)]
    ppermute x2, starting transfers between devices: 13.2 us -> 16.2 us  [moved(): lax.ppermute(block, 'lon', [(i, (i + lon_step) % lons) for i in range(lon...]
    pallas_call x5 -> x6, Pallas kernels: 28.1 us -> 30.9 us  [call(): pl.pallas_call(kernel, out_shape=shapes, in_specs=[pl.BlockSpec(memory_sp...]
    unnamed x10 -> x14, local copies, waits for them, and re-layouts: 0.9 us -> 2.1 us
    ppermute x2, starting transfers between devices: 4.55 us -> 5.57 us  [moved(): lax.ppermute(block, 'lat', [(i, (i + lat_step) % lats) for i in range(lat...]
    all_to_all x2 -> x3, waiting for transfers between devices: 6.41 us -> 6.7 us  [exchange(): return lax.all_to_all(tiles, axis, 0, 0, tiled=True)]
  transfers between devices with their start and end apart: 8 -> 9, of which waited for: 2 -> 3; matrix products, arithmetic and copies ran while one was open for 2% -> 2% of each run, Pallas kernels for 11% -> 17%
where the time goes in v5:
time: 92.7 us; the launch traced here: 92 us
  starting transfers between devices  48.5 us (52%)
  Pallas kernels  30.9 us (33%)
  waiting for transfers between devices  6.71 us (7%)
  local copies, waits for them, and re-layouts  3.41 us (4%)
  other arithmetic  1.47 us (2%)
  between operations  1.02 us (1%)
    pallas_call x6, Pallas kernels, call(): pl.pallas_call(kernel, out_shape=shapes, in_specs=[pl.BlockSpec(memory_sp...  30.9 us
    ppermute x2, starting transfers between devices, moved(): lax.ppermute(block, 'lon', [(i, (i + lon_step) % lons) for i in range(lon...  16.2 us
    all_to_all x3, starting transfers between devices, exchange(): return lax.all_to_all(tiles, axis, 0, 0, tiled=True)  15.6 us
    ppermute x2, starting transfers between devices, moved(): return lax.ppermute(block, ('lat', 'lon'), route)  11.1 us
    all_to_all x3, waiting for transfers between devices, exchange(): return lax.all_to_all(tiles, axis, 0, 0, tiled=True)  6.7 us
    ppermute x2, starting transfers between devices, moved(): lax.ppermute(block, 'lat', [(i, (i + lat_step) % lats) for i in range(lat...  5.57 us
    unnamed x14, local copies, waits for them, and re-layouts  2.1 us
  transfers between devices with their start and end apart: 9, of which 3 were waited for; matrix products, arithmetic and copies ran while one was open for 2% of the time, Pallas kernels for 17%

profile of v5, /device:TPU:1, one launch (start us, length us, event | category | flops | bytes accessed | tf_op | source)
XLA Modules:
  0.0 92.0 jit_solution(4935269861143144301)
XLA Ops:
  0.6 2.2 %send.1 = (bf16[160,512]{1,0:T(8,128)(2,1)}, bf16[224,512]{1,0:T(8,128)(2,1)}, bf16[64,512]{1,0:T(8,128)(2,1)}) custom-call(bf16[432,512]{1,0:T(8,128)(2,1)} %bitcast.13, bf16[432,512]{1,0:T(8,128)(2,1)} %bitcast.16), custom_call_target="tpu_custom_call" | custom-call | flops 100000000 | bytes 4194304 | tf_op jit(solution)/shard_map/send/pallas_call | solution.py:212
  2.8 8.3 %collective-permute-start.2 = (bf16[64,512]{1,0:T(8,128)(2,1)}, bf16[64,512]{1,0:T(8,128)(2,1)S(1)}, u32[]{:S(2)}, u32[]{:S(2)}) collective-permute-start(bf16[64,512]{1,0:T(8,128)(2,1)} %get-tuple-element.35), channel_id=1, source_target_pairs={{0,511},{1,480},{2,481},{3,482},{4,483},{5,484},{6,485},{7,486},{8... | collective-permute-start | bytes 196616 | tf_op jit(solution)/shard_map/ppermute | solution.py:517
  11.2 3.0 %collective-permute-start = (bf16[160,512]{1,0:T(8,128)(2,1)}, bf16[160,512]{1,0:T(8,128)(2,1)S(1)}, u32[]{:S(2)}, u32[]{:S(2)}) collective-permute-start(bf16[160,512]{1,0:T(8,128)(2,1)} %get-tuple-element.33), channel_id=1, source_target_pairs={{0,480},{32,0},{64,32},{96,64},{128,96},{160,128},{192,160},{224,1... | collective-permute-start | bytes 491528 | tf_op jit(solution)/shard_map/ppermute | solution.py:511
  14.1 11.8 %collective-permute-start.1 = (bf16[224,512]{1,0:T(8,128)(2,1)}, bf16[224,512]{1,0:T(8,128)(2,1)S(1)}, u32[]{:S(2)}, u32[]{:S(2)}) collective-permute-start(bf16[224,512]{1,0:T(8,128)(2,1)} %get-tuple-element.34), channel_id=1, source_target_pairs={{0,31},{1,0},{2,1},{3,2},{4,3},{5,4},{6,5},{7,6},{8,7},{9,8},{10,9... | collective-permute-start | bytes 688136 | tf_op jit(solution)/shard_map/ppermute | solution.py:509
  25.9 1.4 %fusion.6.refs_3_.refs_4_.refs_2_ = bf16[16,3072]{1,0:T(8,128)(2,1)} fusion(bf16[8,512]{1,0:T(8,128)(2,1)} %param.17, bf16[8,512]{1,0:T(8,128)(2,1)} %bitcast.19, bf16[8,1536]{1,0:T(8,128)(2,1)} %param.14, bf16[8,512]{1,0:T(8,128)(2,1)} %bitcast.20), kind=kLoop, calls=%fused_computation.7 | loop fusion | flops 638976 | bytes 147456 | tf_op jit(solution)/shard_map/concatenate | solution.py:535
  27.3 0.0 copy-start
  27.3 0.0 copy-start.2
  27.3 7.8 %early.1 = (bf16[160,512]{1,0:T(8,128)(2,1)}, bf16[160,512]{1,0:T(8,128)(2,1)}, f32[8,3072]{1,0:T(8,128)}) custom-call(bf16[432,512]{1,0:T(8,128)(2,1)} %bitcast.14, bf16[432,512]{1,0:T(8,128)(2,1)} %bitcast.17, f32[1,512]{1,0:T(1,128)} %bitcast.10, bf16[16,3072]{1,0:T(8,128)(2,1)} %fusion.6.refs_3_.refs_4_.refs_2_, bf16[512,1536]{1,0:T(8,128)(2,1)} %refs_5_.5, ...), custom_call_target="tpu_custom_call" | custom-call | flops 4000000000 | bytes 4194304 | tf_op jit(solution)/shard_map/early/pallas_call | solution.py:212
  35.1 0.0 collective-permute-done.2.refs_10_
  35.2 0.0 collective-permute-done.refs_8_
  35.2 0.0 collective-permute-done.1.refs_9_
  35.2 0.0 copy-done
  35.2 0.0 copy-done.2
  35.2 0.0 copy-start.6
  35.2 0.9 copy-done.6
  36.1 0.0 copy-start.1
  36.1 12.4 %late.1 = (bf16[320,512]{1,0:T(8,128)(2,1)S(1)}, bf16[320,512]{1,0:T(8,128)(2,1)S(1)}, bf16[320,512]{1,0:T(8,128)(2,1)S(1)}, bf16[320,1536]{1,0:T(8,128)(2,1)}, bf16[16,16,128]{2,1,0:T(8,128)(2,1)}) custom-call(s32[1]{0:T(128)} %bitcast.5.refs_0_, bf16[432,512]{1,0:T(8,128)(2,1)} %bitcast.15, bf16[432,512]{1,0:T(8,128)(2,1)} %bitcast.18, ...), custom_call_target="tpu_custom_call" | custom-call | flops 8000000000 | bytes 4194304 | tf_op jit(solution)/shard_map/late/pallas_call | solution.py:212
  48.5 3.7 %all-to-all-start = ((bf16[16,16,128]{2,1,0:T(8,128)(2,1)}), bf16[16,16,128]{2,1,0:T(8,128)(2,1)S(1)}, u32[]{:S(2)}, u32[]{:S(2)}) async-start(bf16[16,16,128]{2,1,0:T(8,128)(2,1)} %get-tuple-element.41), calls=%async_computation | async-start | bytes 131072 | tf_op jit(solution)/shard_map/all_to_all | solution.py:485
  52.2 0.0 copy-done.1
  52.2 0.0 copy-start.3
  52.2 1.2 %copy-done.3 = bf16[320,1536]{1,0:T(8,128)(2,1)S(1)} copy-done((bf16[320,1536]{1,0:T(8,128)(2,1)S(1)}, bf16[320,1536]{1,0:T(8,128)(2,1)}, u32[]{:S(2)}) %copy-start.3) | copy-done | bytes 983064
  53.4 0.0 copy-start.4
  53.4 0.0 copy-start.5
  53.4 5.4 %finish.1 = (bf16[320,512]{1,0:T(8,128)(2,1)S(1)}, bf16[320,512]{1,0:T(8,128)(2,1)S(1)}, bf16[128,512]{1,0:T(8,128)(2,1)S(1)}, bf16[192,512]{1,0:T(8,128)(2,1)S(1)}, bf16[64,512]{1,0:T(8,128)(2,1)S(1)}) custom-call(bf16[320,512]{1,0:T(8,128)(2,1)S(1)} %get-tuple-element.36.refs_0_, bf16[320,512]{1,0:T(8,128)(2,1)S(1)} %get-tuple-element.37.refs_1_, ...), custom_call_target="tpu_custom_call" | custom-call | flops 2000000000 | bytes 4194304 | tf_op jit(solution)/shard_map/finish/pallas_call | solution.py:212
  58.8 0.7 all-to-all-done
  59.5 0.7 broadcast_in_dim.4
  60.2 5.3 %all-to-all-start.1 = ((bf16[32,16,128]{2,1,0:T(8,128)(2,1)}), bf16[32,16,128]{2,1,0:T(8,128)(2,1)S(1)}, u32[]{:S(2)}, u32[]{:S(2)}) async-start(bf16[32,16,128]{2,1,0:T(8,128)(2,1)} %broadcast_in_dim.4), calls=%async_computation.1 | async-start | bytes 262144 | tf_op jit(solution)/shard_map/all_to_all | solution.py:485
  65.5 4.4 %collective-permute-start.5 = (bf16[192,512]{1,0:T(8,128)(2,1)S(1)}, bf16[192,512]{1,0:T(8,128)(2,1)S(1)}, u32[]{:S(2)}, u32[]{:S(2)}) collective-permute-start(bf16[192,512]{1,0:T(8,128)(2,1)S(1)} %get-tuple-element.46), channel_id=1, source_target_pairs={{0,1},{1,2},{2,3},{3,4},{4,5},{5,6},{6,7},{7,8},{8,9},{9,10},{10,1... | collective-permute-start | bytes 589832 | tf_op jit(solution)/shard_map/ppermute | solution.py:509
  69.9 2.6 %collective-permute-start.3 = (bf16[128,512]{1,0:T(8,128)(2,1)S(1)}, bf16[128,512]{1,0:T(8,128)(2,1)S(1)}, u32[]{:S(2)}, u32[]{:S(2)}) collective-permute-start(bf16[128,512]{1,0:T(8,128)(2,1)S(1)} %get-tuple-element.44), channel_id=1, source_target_pairs={{0,32},{32,64},{64,96},{96,128},{128,160},{160,192},{192,224},{224... | collective-permute-start | bytes 393224 | tf_op jit(solution)/shard_map/ppermute | solution.py:511
  72.5 2.8 %collective-permute-start.4 = (bf16[64,512]{1,0:T(8,128)(2,1)S(1)}, bf16[64,512]{1,0:T(8,128)(2,1)S(1)}, u32[]{:S(2)}, u32[]{:S(2)}) collective-permute-start(bf16[64,512]{1,0:T(8,128)(2,1)S(1)} %get-tuple-element.45), channel_id=1, source_target_pairs={{0,33},{1,34},{2,35},{3,36},{4,37},{5,38},{6,39},{7,40},{8,41},{9,... | collective-permute-start | bytes 196616 | tf_op jit(solution)/shard_map/ppermute | solution.py:517
  75.4 1.0 %all-to-all-done.1 = bf16[32,16,128]{2,1,0:T(8,128)(2,1)S(1)} async-done(((bf16[32,16,128]{2,1,0:T(8,128)(2,1)}), bf16[32,16,128]{2,1,0:T(8,128)(2,1)S(1)}, u32[]{:S(2)}, u32[]{:S(2)}) %all-to-all-start.1) | async-done | bytes 131104 | tf_op jit(solution)/shard_map/all_to_all | solution.py:485
  76.4 0.6 broadcast_in_dim.5
  77.1 6.6 %all-to-all-start.2 = ((bf16[16,16,128]{2,1,0:T(8,128)(2,1)}), bf16[16,16,128]{2,1,0:T(8,128)(2,1)S(1)}, u32[]{:S(2)}, u32[]{:S(2)}) async-start(bf16[16,16,128]{2,1,0:T(8,128)(2,1)} %broadcast_in_dim.5), calls=%async_computation.2 | async-start | bytes 131072 | tf_op jit(solution)/shard_map/all_to_all | solution.py:485
  83.7 0.0 collective-permute-done.4.refs_3_
  83.7 0.0 collective-permute-done.5.refs_4_
  83.7 0.0 collective-permute-done.3.refs_2_
  83.7 0.0 copy-done.4
  83.7 0.0 copy-done.5
  83.7 2.4 %place.1 = (bf16[432,512]{1,0:T(8,128)(2,1)}, bf16[432,512]{1,0:T(8,128)(2,1)}) custom-call(bf16[160,512]{1,0:T(8,128)(2,1)S(1)} %copy-done.4, bf16[320,512]{1,0:T(8,128)(2,1)S(1)} %get-tuple-element.40.refs_1_, bf16[128,512]{1,0:T(8,128)(2,1)S(1)} %collective-permute-done.3.refs_2_, bf16[64,512]{1,0:T(8,128)(2,1)S(1)} %collective-permute-done.4.refs_3_, ...), custom_call_target="tpu_custom_call" | custom-call | flops 1000000000 | bytes 4194304 | tf_op jit(solution)/shard_map/place/pallas_call | solution.py:212
  86.2 5.0 %all-to-all-done.2.refs_0_ = bf16[16,16,128]{2,1,0:T(8,128)(2,1)S(1)} async-done(((bf16[16,16,128]{2,1,0:T(8,128)(2,1)}), bf16[16,16,128]{2,1,0:T(8,128)(2,1)S(1)}, u32[]{:S(2)}, u32[]{:S(2)}) %all-to-all-start.2) | async-done | bytes 65568 | tf_op jit(solution)/shard_map/all_to_all | solution.py:485
  91.1 0.7 grads.1
  (2 shorter events, 0.1 us)
Async XLA Ops:
  2.8 32.3 %collective-permute-start.2 = (bf16[64,512]{1,0:T(8,128)(2,1)}, bf16[64,512]{1,0:T(8,128)(2,1)S(1)}, u32[]{:S(2)}, u32[]{:S(2)}) collective-permute-start(bf16[64,512]{1,0:T(8,128)(2,1)} %get-tuple-element.35), channel_id=1, source_target_pairs={{0,511},{1,480},{2,481},{3,482},{4,483},{5,484},{6,485},{7,486},{8... | collective-permute-start | bytes 196616 | tf_op jit(solution)/shard_map/ppermute | solution.py:517
  11.2 24.0 %collective-permute-start = (bf16[160,512]{1,0:T(8,128)(2,1)}, bf16[160,512]{1,0:T(8,128)(2,1)S(1)}, u32[]{:S(2)}, u32[]{:S(2)}) collective-permute-start(bf16[160,512]{1,0:T(8,128)(2,1)} %get-tuple-element.33), channel_id=1, source_target_pairs={{0,480},{32,0},{64,32},{96,64},{128,96},{160,128},{192,160},{224,1... | collective-permute-start | bytes 491528 | tf_op jit(solution)/shard_map/ppermute | solution.py:511
  14.1 21.0 %collective-permute-start.1 = (bf16[224,512]{1,0:T(8,128)(2,1)}, bf16[224,512]{1,0:T(8,128)(2,1)S(1)}, u32[]{:S(2)}, u32[]{:S(2)}) collective-permute-start(bf16[224,512]{1,0:T(8,128)(2,1)} %get-tuple-element.34), channel_id=1, source_target_pairs={{0,31},{1,0},{2,1},{3,2},{4,3},{5,4},{6,5},{7,6},{8,7},{9,8},{10,9... | collective-permute-start | bytes 688136 | tf_op jit(solution)/shard_map/ppermute | solution.py:509
  27.3 7.8 %copy-start = (bf16[16,3072]{1,0:T(8,128)(2,1)S(1)}, bf16[16,3072]{1,0:T(8,128)(2,1)}, u32[]{:S(2)}) copy-start(bf16[16,3072]{1,0:T(8,128)(2,1)} %fusion.6.refs_3_.refs_4_.refs_2_) | copy-start | bytes 294916
  27.3 7.8 %copy-start.2 = (f32[512]{0:T(512)S(1)}, f32[512]{0:T(512)}, u32[]{:S(2)}) copy-start(f32[512]{0:T(512)} %param.11) | copy-start | bytes 6148
  35.2 0.9 copy-start.6
  36.1 16.1 %copy-start.1 = (bf16[512,512]{1,0:T(8,128)(2,1)S(1)}, bf16[512,512]{1,0:T(8,128)(2,1)}, u32[]{:S(2)}) copy-start(bf16[512,512]{1,0:T(8,128)(2,1)} %refs_3_.1) | copy-start | bytes 1572868
  48.5 11.0 %all-to-all-start = ((bf16[16,16,128]{2,1,0:T(8,128)(2,1)}), bf16[16,16,128]{2,1,0:T(8,128)(2,1)S(1)}, u32[]{:S(2)}, u32[]{:S(2)}) async-start(bf16[16,16,128]{2,1,0:T(8,128)(2,1)} %get-tuple-element.41), calls=%async_computation | async-start | bytes 131072 | tf_op jit(solution)/shard_map/all_to_all | solution.py:485
  52.2 1.2 %copy-start.3 = (bf16[320,1536]{1,0:T(8,128)(2,1)S(1)}, bf16[320,1536]{1,0:T(8,128)(2,1)}, u32[]{:S(2)}) copy-start(bf16[320,1536]{1,0:T(8,128)(2,1)} %get-tuple-element.38.refs_4_) | copy-start | bytes 2949124
  53.4 30.3 %copy-start.4 = (bf16[160,512]{1,0:T(8,128)(2,1)S(1)}, bf16[160,512]{1,0:T(8,128)(2,1)}, u32[]{:S(2)}) copy-start(bf16[160,512]{1,0:T(8,128)(2,1)} %get-tuple-element.31.refs_0_) | copy-start | bytes 491524
  53.4 30.3 %copy-start.5 = (bf16[160,512]{1,0:T(8,128)(2,1)S(1)}, bf16[160,512]{1,0:T(8,128)(2,1)}, u32[]{:S(2)}) copy-start(bf16[160,512]{1,0:T(8,128)(2,1)} %get-tuple-element.47.refs_5_) | copy-start | bytes 491524
  60.2 16.2 %all-to-all-start.1 = ((bf16[32,16,128]{2,1,0:T(8,128)(2,1)}), bf16[32,16,128]{2,1,0:T(8,128)(2,1)S(1)}, u32[]{:S(2)}, u32[]{:S(2)}) async-start(bf16[32,16,128]{2,1,0:T(8,128)(2,1)} %broadcast_in_dim.4), calls=%async_computation.1 | async-start | bytes 262144 | tf_op jit(solution)/shard_map/all_to_all | solution.py:485
  65.5 18.2 %collective-permute-start.5 = (bf16[192,512]{1,0:T(8,128)(2,1)S(1)}, bf16[192,512]{1,0:T(8,128)(2,1)S(1)}, u32[]{:S(2)}, u32[]{:S(2)}) collective-permute-start(bf16[192,512]{1,0:T(8,128)(2,1)S(1)} %get-tuple-element.46), channel_id=1, source_target_pairs={{0,1},{1,2},{2,3},{3,4},{4,5},{5,6},{6,7},{7,8},{8,9},{9,10},{10,1... | collective-permute-start | bytes 589832 | tf_op jit(solution)/shard_map/ppermute | solution.py:509
  69.9 13.8 %collective-permute-start.3 = (bf16[128,512]{1,0:T(8,128)(2,1)S(1)}, bf16[128,512]{1,0:T(8,128)(2,1)S(1)}, u32[]{:S(2)}, u32[]{:S(2)}) collective-permute-start(bf16[128,512]{1,0:T(8,128)(2,1)S(1)} %get-tuple-element.44), channel_id=1, source_target_pairs={{0,32},{32,64},{64,96},{96,128},{128,160},{160,192},{192,224},{224... | collective-permute-start | bytes 393224 | tf_op jit(solution)/shard_map/ppermute | solution.py:511
  72.5 11.1 %collective-permute-start.4 = (bf16[64,512]{1,0:T(8,128)(2,1)S(1)}, bf16[64,512]{1,0:T(8,128)(2,1)S(1)}, u32[]{:S(2)}, u32[]{:S(2)}) collective-permute-start(bf16[64,512]{1,0:T(8,128)(2,1)S(1)} %get-tuple-element.45), channel_id=1, source_target_pairs={{0,33},{1,34},{2,35},{3,36},{4,37},{5,38},{6,39},{7,40},{8,41},{9,... | collective-permute-start | bytes 196616 | tf_op jit(solution)/shard_map/ppermute | solution.py:517
  77.1 14.1 %all-to-all-start.2 = ((bf16[16,16,128]{2,1,0:T(8,128)(2,1)}), bf16[16,16,128]{2,1,0:T(8,128)(2,1)S(1)}, u32[]{:S(2)}, u32[]{:S(2)}) async-start(bf16[16,16,128]{2,1,0:T(8,128)(2,1)} %broadcast_in_dim.5), calls=%async_computation.2 | async-start | bytes 131072 | tf_op jit(solution)/shard_map/all_to_all | solution.py:485

commit v6 on v4

--- a/solution.py
+++ b/solution.py
@@ -226,14 +226,15 @@
 
 
 def send_body(given, made):
+    for at, name in enumerate(("x", "c")):
+        made["row"][ROW_IN * at : ROW_IN * (at + 1)] = given[name][:ROW_IN]
+    made.send("row")
     place = place_send()
     for at, name in enumerate(("x", "c")):
-        ref = given[name]
-        made["row"][ROW_IN * at : ROW_IN * (at + 1)] = ref[:ROW_IN]
-        picked = nn(place, ref[...]).astype(BF16)
+        picked = nn(place, given[name][...]).astype(BF16)
         made["col"][COL_IN * at : COL_IN * (at + 1)] = picked[:COL_IN]
         made["cor"][COR_IN * at : COR_IN * (at + 1)] = picked[COL_IN:]
-    made.send("col", "row", "cor")
+    made.send("col", "cor")
 
 
 def split_heads(block, marks):
@@ -531,7 +532,6 @@
             "cor": ((2 * COR_IN, D), BF16),
         },
         "send",
-        near=("row", "col", "cor"),
         flops=10**8,
     )
     col = moved(col, 0, -1)

time: 91.8 us -> 91.8 us (level)
  no operation moved by 1% of the time
where the time goes in v6:
time: 91.8 us; the launch traced here: 91 us
  starting transfers between devices  41.4 us (45%)
  Pallas kernels  28.1 us (31%)
  blocking collectives  10.4 us (11%)
  waiting for transfers between devices  6.41 us (7%)
  local copies, waits for them, and re-layouts  2.21 us (2%)
  other arithmetic  1.48 us (2%)
  between operations  0.99 us (1%)
    pallas_call x5, Pallas kernels, call(): pl.pallas_call(kernel, out_shape=shapes, in_specs=[pl.BlockSpec(memory_sp...  28.1 us
    ppermute x2, starting transfers between devices, moved(): return lax.ppermute(block, ('lat', 'lon'), route)  14.8 us
    ppermute x2, starting transfers between devices, moved(): lax.ppermute(block, 'lon', [(i, (i + lon_step) % lons) for i in range(lon...  13.2 us
    all_to_all x1, blocking collectives, exchange(): return lax.all_to_all(tiles, axis, 0, 0, tiled=True)  10.4 us
    all_to_all x2, starting transfers between devices, exchange(): return lax.all_to_all(tiles, axis, 0, 0, tiled=True)  8.81 us
    all_to_all x2, waiting for transfers between devices, exchange(): return lax.all_to_all(tiles, axis, 0, 0, tiled=True)  6.4 us
    ppermute x2, starting transfers between devices, moved(): lax.ppermute(block, 'lat', [(i, (i + lat_step) % lats) for i in range(lat...  4.55 us
  transfers between devices with their start and end apart: 8, of which 2 were waited for; matrix products, arithmetic and copies ran while one was open for 2% of the time, Pallas kernels for 11%

profile of v6, /device:TPU:1, one launch (start us, length us, event | category | flops | bytes accessed | tf_op | source)
XLA Modules:
  0.0 91.0 jit_solution(16663623986226645611)
XLA Ops:
  0.6 2.2 %send.1 = (bf16[160,512]{1,0:T(8,128)(2,1)}, bf16[224,512]{1,0:T(8,128)(2,1)}, bf16[64,512]{1,0:T(8,128)(2,1)}) custom-call(bf16[432,512]{1,0:T(8,128)(2,1)} %bitcast.12, bf16[432,512]{1,0:T(8,128)(2,1)} %bitcast.15), custom_call_target="tpu_custom_call" | custom-call | flops 100000000 | bytes 4194304 | tf_op jit(solution)/shard_map/send/pallas_call | solution.py:212
  2.8 8.8 %collective-permute-start.1 = (bf16[224,512]{1,0:T(8,128)(2,1)}, bf16[224,512]{1,0:T(8,128)(2,1)S(1)}, u32[]{:S(2)}, u32[]{:S(2)}) collective-permute-start(bf16[224,512]{1,0:T(8,128)(2,1)} %get-tuple-element.30), channel_id=1, source_target_pairs={{0,31},{1,0},{2,1},{3,2},{4,3},{5,4},{6,5},{7,6},{8,7},{9,8},{10,9... | collective-permute-start | bytes 688136 | tf_op jit(solution)/shard_map/ppermute | solution.py:492
  11.6 1.9 %collective-permute-start = (bf16[160,512]{1,0:T(8,128)(2,1)}, bf16[160,512]{1,0:T(8,128)(2,1)S(1)}, u32[]{:S(2)}, u32[]{:S(2)}) collective-permute-start(bf16[160,512]{1,0:T(8,128)(2,1)} %get-tuple-element.29), channel_id=1, source_target_pairs={{0,480},{32,0},{64,32},{96,64},{128,96},{160,128},{192,160},{224,1... | collective-permute-start | bytes 491528 | tf_op jit(solution)/shard_map/ppermute | solution.py:494
  13.6 12.5 %collective-permute-start.2 = (bf16[64,512]{1,0:T(8,128)(2,1)}, bf16[64,512]{1,0:T(8,128)(2,1)S(1)}, u32[]{:S(2)}, u32[]{:S(2)}) collective-permute-start(bf16[64,512]{1,0:T(8,128)(2,1)} %get-tuple-element.31), channel_id=1, source_target_pairs={{0,511},{1,480},{2,481},{3,482},{4,483},{5,484},{6,485},{7,486},{8... | collective-permute-start | bytes 196616 | tf_op jit(solution)/shard_map/ppermute | solution.py:500
  26.1 1.4 %fusion.6.refs_3_.refs_4_ = bf16[16,3072]{1,0:T(8,128)(2,1)} fusion(bf16[8,512]{1,0:T(8,128)(2,1)} %param.17, bf16[8,512]{1,0:T(8,128)(2,1)} %bitcast.18, bf16[8,1536]{1,0:T(8,128)(2,1)} %param.14, bf16[8,512]{1,0:T(8,128)(2,1)} %bitcast.19), kind=kLoop, calls=%fused_computation.7 | loop fusion | flops 638976 | bytes 147456 | tf_op jit(solution)/shard_map/concatenate | solution.py:517
  27.5 0.0 copy-start
  27.5 0.0 copy-start.1
  27.5 7.8 %early.1 = (bf16[160,512]{1,0:T(8,128)(2,1)}, bf16[160,512]{1,0:T(8,128)(2,1)}, f32[8,3072]{1,0:T(8,128)}) custom-call(bf16[432,512]{1,0:T(8,128)(2,1)} %bitcast.13, bf16[432,512]{1,0:T(8,128)(2,1)} %bitcast.16, f32[1,512]{1,0:T(1,128)} %bitcast.10, bf16[16,3072]{1,0:T(8,128)(2,1)} %fusion.6.refs_3_.refs_4_, bf16[512,1536]{1,0:T(8,128)(2,1)} %refs_5_.3, ...), custom_call_target="tpu_custom_call" | custom-call | flops 4000000000 | bytes 4194304 | tf_op jit(solution)/shard_map/early/pallas_call | solution.py:212
  35.3 0.0 collective-permute-done.2.refs_10_
  35.3 0.0 collective-permute-done.refs_8_
  35.3 0.0 collective-permute-done.1.refs_9_
  35.3 0.0 copy-done
  35.3 0.0 copy-done.1
  35.3 0.0 copy-start.4
  35.3 0.9 copy-done.4
  36.2 0.0 copy-start.2
  36.2 0.0 copy-start.3
  36.2 14.9 %late.1 = (bf16[320,512]{1,0:T(8,128)(2,1)S(1)}, bf16[320,512]{1,0:T(8,128)(2,1)S(1)}, bf16[16,16,128]{2,1,0:T(8,128)(2,1)S(1)}, bf16[128,512]{1,0:T(8,128)(2,1)...) custom-call(s32[1]{0:T(128)} %bitcast.5.refs_0_, bf16[432,512]{1,0:T(8,128)(2,1)} %bitcast.14, ...), custom_call_target="tpu_custom_call" | custom-call | flops 8000000000 | bytes 4194304 | tf_op jit(solution)/shard_map/late/pallas_call | solution.py:212
  51.2 10.4 %all_to_all.15 = bf16[16,16,128]{2,1,0:T(8,128)(2,1)S(1)} all-to-all(bf16[16,16,128]{2,1,0:T(8,128)(2,1)S(1)} %get-tuple-element.33), channel_id=1, replica_groups=mesh['lat'=16,'lon'=32] {'lat'}, dimensions={0} | all-to-all | bytes 131072 | tf_op jit(solution)/shard_map/all_to_all | solution.py:468
  61.6 0.7 broadcast_in_dim.4
  62.3 5.2 %all-to-all-start.1 = ((bf16[32,16,128]{2,1,0:T(8,128)(2,1)}), bf16[32,16,128]{2,1,0:T(8,128)(2,1)S(1)}, u32[]{:S(2)}, u32[]{:S(2)}) async-start(bf16[32,16,128]{2,1,0:T(8,128)(2,1)} %broadcast_in_dim.4), calls=%async_computation.1 | async-start | bytes 262144 | tf_op jit(solution)/shard_map/all_to_all | solution.py:468
  67.5 4.4 %collective-permute-start.5 = (bf16[192,512]{1,0:T(8,128)(2,1)S(1)}, bf16[192,512]{1,0:T(8,128)(2,1)S(1)}, u32[]{:S(2)}, u32[]{:S(2)}) collective-permute-start(bf16[192,512]{1,0:T(8,128)(2,1)S(1)} %get-tuple-element.38), channel_id=1, source_target_pairs={{0,1},{1,2},{2,3},{3,4},{4,5},{5,6},{6,7},{7,8},{8,9},{9,10},{10,1... | collective-permute-start | bytes 589832 | tf_op jit(solution)/shard_map/ppermute | solution.py:492
  71.9 2.6 %collective-permute-start.3 = (bf16[128,512]{1,0:T(8,128)(2,1)S(1)}, bf16[128,512]{1,0:T(8,128)(2,1)S(1)}, u32[]{:S(2)}, u32[]{:S(2)}) collective-permute-start(bf16[128,512]{1,0:T(8,128)(2,1)S(1)} %get-tuple-element.36), channel_id=1, source_target_pairs={{0,32},{32,64},{64,96},{96,128},{128,160},{160,192},{192,224},{224... | collective-permute-start | bytes 393224 | tf_op jit(solution)/shard_map/ppermute | solution.py:494
  74.6 2.3 %collective-permute-start.4 = (bf16[64,512]{1,0:T(8,128)(2,1)S(1)}, bf16[64,512]{1,0:T(8,128)(2,1)S(1)}, u32[]{:S(2)}, u32[]{:S(2)}) collective-permute-start(bf16[64,512]{1,0:T(8,128)(2,1)S(1)} %get-tuple-element.37), channel_id=1, source_target_pairs={{0,33},{1,34},{2,35},{3,36},{4,37},{5,38},{6,39},{7,40},{8,41},{9,... | collective-permute-start | bytes 196616 | tf_op jit(solution)/shard_map/ppermute | solution.py:500
  76.9 1.5 %all-to-all-done.1 = bf16[32,16,128]{2,1,0:T(8,128)(2,1)S(1)} async-done(((bf16[32,16,128]{2,1,0:T(8,128)(2,1)}), bf16[32,16,128]{2,1,0:T(8,128)(2,1)S(1)}, u32[]{:S(2)}, u32[]{:S(2)}) %all-to-all-start.1) | async-done | bytes 131104 | tf_op jit(solution)/shard_map/all_to_all | solution.py:468
  78.4 0.6 broadcast_in_dim.5
  79.1 3.7 %all-to-all-start.2 = ((bf16[16,16,128]{2,1,0:T(8,128)(2,1)}), bf16[16,16,128]{2,1,0:T(8,128)(2,1)S(1)}, u32[]{:S(2)}, u32[]{:S(2)}) async-start(bf16[16,16,128]{2,1,0:T(8,128)(2,1)} %broadcast_in_dim.5), calls=%async_computation.2 | async-start | bytes 131072 | tf_op jit(solution)/shard_map/all_to_all | solution.py:468
  82.7 0.0 collective-permute-done.4.refs_3_
  82.7 0.0 collective-permute-done.5.refs_4_
  82.8 0.0 collective-permute-done.3.refs_2_
  82.8 0.0 copy-done.2
  82.8 0.0 copy-done.3
  82.8 2.5 %place.1 = (bf16[432,512]{1,0:T(8,128)(2,1)}, bf16[432,512]{1,0:T(8,128)(2,1)}) custom-call(bf16[160,512]{1,0:T(8,128)(2,1)S(1)} %copy-done.2, bf16[320,512]{1,0:T(8,128)(2,1)S(1)} %get-tuple-element.32.refs_1_, bf16[128,512]{1,0:T(8,128)(2,1)S(1)} %collective-permute-done.3.refs_2_, bf16[64,512]{1,0:T(8,128)(2,1)S(1)} %collective-permute-done.4.refs_3_, ...), custom_call_target="tpu_custom_call" | custom-call | flops 1000000000 | bytes 4194304 | tf_op jit(solution)/shard_map/place/pallas_call | solution.py:212
  85.2 4.9 %all-to-all-done.2.refs_0_ = bf16[16,16,128]{2,1,0:T(8,128)(2,1)S(1)} async-done(((bf16[16,16,128]{2,1,0:T(8,128)(2,1)}), bf16[16,16,128]{2,1,0:T(8,128)(2,1)S(1)}, u32[]{:S(2)}, u32[]{:S(2)}) %all-to-all-start.2) | async-done | bytes 65568 | tf_op jit(solution)/shard_map/all_to_all | solution.py:468
  90.1 0.7 grads.1
  (2 shorter events, 0.1 us)
Async XLA Ops:
  2.8 32.5 %collective-permute-start.1 = (bf16[224,512]{1,0:T(8,128)(2,1)}, bf16[224,512]{1,0:T(8,128)(2,1)S(1)}, u32[]{:S(2)}, u32[]{:S(2)}) collective-permute-start(bf16[224,512]{1,0:T(8,128)(2,1)} %get-tuple-element.30), channel_id=1, source_target_pairs={{0,31},{1,0},{2,1},{3,2},{4,3},{5,4},{6,5},{7,6},{8,7},{9,8},{10,9... | collective-permute-start | bytes 688136 | tf_op jit(solution)/shard_map/ppermute | solution.py:492
  11.6 23.7 %collective-permute-start = (bf16[160,512]{1,0:T(8,128)(2,1)}, bf16[160,512]{1,0:T(8,128)(2,1)S(1)}, u32[]{:S(2)}, u32[]{:S(2)}) collective-permute-start(bf16[160,512]{1,0:T(8,128)(2,1)} %get-tuple-element.29), channel_id=1, source_target_pairs={{0,480},{32,0},{64,32},{96,64},{128,96},{160,128},{192,160},{224,1... | collective-permute-start | bytes 491528 | tf_op jit(solution)/shard_map/ppermute | solution.py:494
  13.6 21.7 %collective-permute-start.2 = (bf16[64,512]{1,0:T(8,128)(2,1)}, bf16[64,512]{1,0:T(8,128)(2,1)S(1)}, u32[]{:S(2)}, u32[]{:S(2)}) collective-permute-start(bf16[64,512]{1,0:T(8,128)(2,1)} %get-tuple-element.31), channel_id=1, source_target_pairs={{0,511},{1,480},{2,481},{3,482},{4,483},{5,484},{6,485},{7,486},{8... | collective-permute-start | bytes 196616 | tf_op jit(solution)/shard_map/ppermute | solution.py:500
  27.5 7.8 %copy-start = (bf16[16,3072]{1,0:T(8,128)(2,1)S(1)}, bf16[16,3072]{1,0:T(8,128)(2,1)}, u32[]{:S(2)}) copy-start(bf16[16,3072]{1,0:T(8,128)(2,1)} %fusion.6.refs_3_.refs_4_) | copy-start | bytes 294916
  27.5 7.8 %copy-start.1 = (f32[512]{0:T(512)S(1)}, f32[512]{0:T(512)}, u32[]{:S(2)}) copy-start(f32[512]{0:T(512)} %param.11) | copy-start | bytes 6148
  35.3 0.9 copy-start.4
  36.2 46.5 %copy-start.2 = (bf16[160,512]{1,0:T(8,128)(2,1)S(1)}, bf16[160,512]{1,0:T(8,128)(2,1)}, u32[]{:S(2)}) copy-start(bf16[160,512]{1,0:T(8,128)(2,1)} %get-tuple-element.27.refs_0_) | copy-start | bytes 491524
  36.2 46.5 %copy-start.3 = (bf16[160,512]{1,0:T(8,128)(2,1)S(1)}, bf16[160,512]{1,0:T(8,128)(2,1)}, u32[]{:S(2)}) copy-start(bf16[160,512]{1,0:T(8,128)(2,1)} %get-tuple-element.39.refs_5_) | copy-start | bytes 491524
  62.3 16.1 %all-to-all-start.1 = ((bf16[32,16,128]{2,1,0:T(8,128)(2,1)}), bf16[32,16,128]{2,1,0:T(8,128)(2,1)S(1)}, u32[]{:S(2)}, u32[]{:S(2)}) async-start(bf16[32,16,128]{2,1,0:T(8,128)(2,1)} %broadcast_in_dim.4), calls=%async_computation.1 | async-start | bytes 262144 | tf_op jit(solution)/shard_map/all_to_all | solution.py:468
  67.5 15.3 %collective-permute-start.5 = (bf16[192,512]{1,0:T(8,128)(2,1)S(1)}, bf16[192,512]{1,0:T(8,128)(2,1)S(1)}, u32[]{:S(2)}, u32[]{:S(2)}) collective-permute-start(bf16[192,512]{1,0:T(8,128)(2,1)S(1)} %get-tuple-element.38), channel_id=1, source_target_pairs={{0,1},{1,2},{2,3},{3,4},{4,5},{5,6},{6,7},{7,8},{8,9},{9,10},{10,1... | collective-permute-start | bytes 589832 | tf_op jit(solution)/shard_map/ppermute | solution.py:492
  71.9 10.8 %collective-permute-start.3 = (bf16[128,512]{1,0:T(8,128)(2,1)S(1)}, bf16[128,512]{1,0:T(8,128)(2,1)S(1)}, u32[]{:S(2)}, u32[]{:S(2)}) collective-permute-start(bf16[128,512]{1,0:T(8,128)(2,1)S(1)} %get-tuple-element.36), channel_id=1, source_target_pairs={{0,32},{32,64},{64,96},{96,128},{128,160},{160,192},{192,224},{224... | collective-permute-start | bytes 393224 | tf_op jit(solution)/shard_map/ppermute | solution.py:494
  74.6 8.2 %collective-permute-start.4 = (bf16[64,512]{1,0:T(8,128)(2,1)S(1)}, bf16[64,512]{1,0:T(8,128)(2,1)S(1)}, u32[]{:S(2)}, u32[]{:S(2)}) collective-permute-start(bf16[64,512]{1,0:T(8,128)(2,1)S(1)} %get-tuple-element.37), channel_id=1, source_target_pairs={{0,33},{1,34},{2,35},{3,36},{4,37},{5,38},{6,39},{7,40},{8,41},{9,... | collective-permute-start | bytes 196616 | tf_op jit(solution)/shard_map/ppermute | solution.py:500
  79.1 11.0 %all-to-all-start.2 = ((bf16[16,16,128]{2,1,0:T(8,128)(2,1)}), bf16[16,16,128]{2,1,0:T(8,128)(2,1)S(1)}, u32[]{:S(2)}, u32[]{:S(2)}) async-start(bf16[16,16,128]{2,1,0:T(8,128)(2,1)} %broadcast_in_dim.5), calls=%async_computation.2 | async-start | bytes 131072 | tf_op jit(solution)/shard_map/all_to_all | solution.py:468
